TPU v7x, 32 devices: a whole 2x2x4 slice. The times are simulated.
32 devices in a mesh: slab: 2 (over core), corpus: 16 (over z, y, x).
Axes of the slice: x: 2, y: 2, z: 4, core: 2. Of those that a mesh axis runs over, the one named last changes fastest.
Arguments:
- vectors: bfloat16 [65536, 128], P(('slab', 'corpus')), parts along dimension 0, may hold values from -1.796875 to 1.796875
- docs: int32 [65536], P(('slab', 'corpus')), parts along dimension 0, may hold values from 0 to 63
- prior: float32 [65536], P(('slab', 'corpus')), parts along dimension 0, may hold values from 0.5 to 3
Outputs:
- best: float32 [65536], P(('slab', 'corpus')), parts along dimension 0
There are 2 independent parts, one for each index of `slab`. A program takes and returns all parts, laid end to end along the dimension named above; each array names one. Nothing has to cross between parts.
All inputs are finite; a program needn't handle non-finite values.
Results may differ from a plain program's by a relative error of at most 0.0003.
Values may be sent and summed in bfloat16 or wider, within the bound.
No kernel may reach another device: no remote copies, remote signals or barrier semaphores. Data moves between devices by JAX's collectives and lax.ppermute only.
A program may use at most 128 MiB of HBM per device.

v0:
```python
import jax
import jax.numpy as jnp
from jax import lax
from jax.sharding import PartitionSpec as P

ROUNDS = 4


NEG = -1e30


def from_behind(value, axis, steps):
    count = lax.axis_size(axis)
    pairs = [(source, (source + steps) % count) for source in range(count)]
    return lax.ppermute(value, axis, pairs)


def one_tile(own, own_tags, other, other_tags):
    count = own.shape[0]
    rows_blk = min(512, count)
    pieces = count // rows_blk
    colmax = jnp.full((other.shape[0],), NEG, jnp.float32)
    row_parts = []
    for piece in range(pieces):
        rows_x = own[piece * rows_blk : (piece + 1) * rows_blk]
        rows_t = own_tags[piece * rows_blk : (piece + 1) * rows_blk]
        scores = lax.dot_general(
            rows_x, other, (((1,), (1,)), ((), ())), preferred_element_type=jnp.float32
        )
        scores = jnp.where(rows_t[:, None] == other_tags[None, :], NEG, scores)
        colmax = jnp.maximum(colmax, jnp.max(scores, axis=0))
        row_parts.append(jnp.max(scores, axis=1))
    return (jnp.concatenate(row_parts, axis=0), colmax)


def per_device(vectors, docs, prior):
    tags = docs.astype(jnp.bfloat16)
    best = prior
    for dist in range(1, ROUNDS + 1):
        behind, behind_tags = from_behind((vectors, tags), "corpus", dist)
        rowmax, colmax = one_tile(vectors, tags, behind, behind_tags)
        returned = from_behind(colmax, "corpus", -dist)
        best = jnp.maximum(best, jnp.maximum(rowmax, returned))
    return best


def solution(mesh):
    return jax.shard_map(
        per_device,
        mesh=mesh,
        in_specs=(P(("slab", "corpus"), None), P(("slab", "corpus")), P(("slab", "corpus"))),
        out_specs=P(("slab", "corpus")),
        check_vma=False,
    )
```

profile of v0, /device:TPU:0, one launch (start us, length us, event | category | flops | bytes accessed | tf_op | source)
XLA Modules:
  0.0 91.9 jit_solution(11164204383293478472)
XLA Ops:
  0.0 0.0 copy-start
  0.0 3.0 %collective-permute-start.10 = (bf16[2048,128]{1,0:T(8,128)(2,1)}, bf16[2048,128]{1,0:T(8,128)(2,1)S(1)}, u32[]{:S(2)}, u32[]{:S(2)}) collective-permute-start(bf16[2048,128]{1,0:T(8,128)(2,1)} %param.3), channel_id=1, source_target_pairs={{0,4},{1,5},{2,6},{3,7},{4,8},{5,9},{6,10},{7,11},{8,12},{9,13},{1... | collective-permute-start | bytes 1572872 | tf_op jit(solution)/shard_map/ppermute | solution.py:15
  3.0 0.7 convert_element_type.3
  3.7 1.5 %collective-permute-start.3 = (bf16[2048]{0:T(1024)(128)(2,1)S(1)}, bf16[2048]{0:T(1024)(128)(2,1)S(1)}, u32[]{:S(2)}, u32[]{:S(2)}) collective-permute-start(bf16[2048]{0:T(1024)(128)(2,1)S(1)} %convert_element_type.3), channel_id=1, source_target_pairs={{0,2},{1,3},{2,4},{3,5},{4,6},{5,7},{6,8},{7,9},{8,10},{9,11},{10,... | collective-permute-start | bytes 12296 | tf_op jit(solution)/shard_map/ppermute | solution.py:15
  5.2 2.4 %collective-permute-start.6 = (bf16[2048]{0:T(1024)(128)(2,1)S(1)}, bf16[2048]{0:T(1024)(128)(2,1)S(1)}, u32[]{:S(2)}, u32[]{:S(2)}) collective-permute-start(bf16[2048]{0:T(1024)(128)(2,1)S(1)} %convert_element_type.3), channel_id=1, source_target_pairs={{0,3},{1,4},{2,5},{3,6},{4,7},{5,8},{6,9},{7,10},{8,11},{9,12},{10... | collective-permute-start | bytes 12296 | tf_op jit(solution)/shard_map/ppermute | solution.py:15
  7.7 1.6 %collective-permute-start.9 = (bf16[2048]{0:T(1024)(128)(2,1)S(1)}, bf16[2048]{0:T(1024)(128)(2,1)S(1)}, u32[]{:S(2)}, u32[]{:S(2)}) collective-permute-start(bf16[2048]{0:T(1024)(128)(2,1)S(1)} %convert_element_type.3), channel_id=1, source_target_pairs={{0,4},{1,5},{2,6},{3,7},{4,8},{5,9},{6,10},{7,11},{8,12},{9,13},{1... | collective-permute-start | bytes 12296 | tf_op jit(solution)/shard_map/ppermute | solution.py:15
  9.3 0.0 collective-permute-start.7
  9.3 8.0 %collective-permute-done.10 = bf16[2048,128]{1,0:T(8,128)(2,1)S(1)} collective-permute-done((bf16[2048,128]{1,0:T(8,128)(2,1)}, bf16[2048,128]{1,0:T(8,128)(2,1)S(1)}, u32[]{:S(2)}, u32[]{:S(2)}) %collective-permute-start.10) | collective-permute-done | bytes 524320 | tf_op jit(solution)/shard_map/ppermute | solution.py:15
  17.3 2.5 %collective-permute-start.4 = (bf16[2048,128]{1,0:T(8,128)(2,1)}, bf16[2048,128]{1,0:T(8,128)(2,1)S(1)}, u32[]{:S(2)}, u32[]{:S(2)}) collective-permute-start(bf16[2048,128]{1,0:T(8,128)(2,1)} %param.3), channel_id=1, source_target_pairs={{0,2},{1,3},{2,4},{3,5},{4,6},{5,7},{6,8},{7,9},{8,10},{9,11},{10,... | collective-permute-start | bytes 1572872 | tf_op jit(solution)/shard_map/ppermute | solution.py:15
  19.8 3.6 %fusion.32 = f32[512,2048]{1,0:T(8,128)} fusion(bf16[2048,128]{1,0:T(8,128)(2,1)S(1)} %collective-permute-done.10, bf16[2048,128]{1,0:T(8,128)(2,1)} %param.3), kind=kOutput, calls=%fused_computation.48 | convolution fusion | flops 268435456 | bytes 4849664 | tf_op jit(solution)/shard_map/dot_general | solution.py:27
  23.4 0.0 copy-done
  23.4 2.7 %fusion.40 = f32[512,2048]{1,0:T(8,128)} fusion(bf16[2048,128]{1,0:T(8,128)(2,1)S(1)} %collective-permute-done.10, bf16[2048,128]{1,0:T(8,128)(2,1)S(1)} %copy-done), kind=kOutput, calls=%fused_computation.56 | convolution fusion | flops 268435456 | bytes 4849664 | tf_op jit(solution)/shard_map/dot_general | solution.py:27
  26.1 3.5 %collective-permute-done.7 = bf16[2048,128]{1,0:T(8,128)(2,1)S(1)} collective-permute-done((bf16[2048,128]{1,0:T(8,128)(2,1)}, bf16[2048,128]{1,0:T(8,128)(2,1)S(1)}, u32[]{:S(2)}, u32[]{:S(2)}) %collective-permute-start.7) | collective-permute-done | bytes 524320 | tf_op jit(solution)/shard_map/ppermute | solution.py:15
  29.6 2.6 %collective-permute-start = (bf16[2048]{0:T(1024)(128)(2,1)S(1)}, bf16[2048]{0:T(1024)(128)(2,1)S(1)}, u32[]{:S(2)}, u32[]{:S(2)}) collective-permute-start(bf16[2048]{0:T(1024)(128)(2,1)S(1)} %convert_element_type.3), channel_id=1, source_target_pairs={{0,1},{1,2},{2,3},{3,4},{4,5},{5,6},{6,7},{7,8},{8,9},{9,10},{10,1... | collective-permute-start | bytes 12296 | tf_op jit(solution)/shard_map/ppermute | solution.py:15
  32.2 2.7 %fusion.34 = f32[512,2048]{1,0:T(8,128)} fusion(bf16[2048,128]{1,0:T(8,128)(2,1)S(1)} %collective-permute-done.7, bf16[2048,128]{1,0:T(8,128)(2,1)S(1)} %copy-done), kind=kOutput, calls=%fused_computation.50 | convolution fusion | flops 268435456 | bytes 4849664 | tf_op jit(solution)/shard_map/dot_general | solution.py:27
  34.8 2.8 %fusion.42 = f32[512,2048]{1,0:T(8,128)} fusion(bf16[2048,128]{1,0:T(8,128)(2,1)S(1)} %collective-permute-done.7, bf16[2048,128]{1,0:T(8,128)(2,1)S(1)} %copy-done), kind=kOutput, calls=%fused_computation.58 | convolution fusion | flops 268435456 | bytes 4849664 | tf_op jit(solution)/shard_map/dot_general | solution.py:27
  37.6 3.4 %collective-permute-done.4 = bf16[2048,128]{1,0:T(8,128)(2,1)S(1)} collective-permute-done((bf16[2048,128]{1,0:T(8,128)(2,1)}, bf16[2048,128]{1,0:T(8,128)(2,1)S(1)}, u32[]{:S(2)}, u32[]{:S(2)}) %collective-permute-start.4) | collective-permute-done | bytes 524320 | tf_op jit(solution)/shard_map/ppermute | solution.py:15
  41.0 1.5 %collective-permute-start.1 = (bf16[2048,128]{1,0:T(8,128)(2,1)S(1)}, bf16[2048,128]{1,0:T(8,128)(2,1)S(1)}, u32[]{:S(2)}, u32[]{:S(2)}) collective-permute-start(bf16[2048,128]{1,0:T(8,128)(2,1)S(1)} %copy-done), channel_id=1, source_target_pairs={{0,1},{1,2},{2,3},{3,4},{4,5},{5,6},{6,7},{7,8},{8,9},{9,10},{10,1... | collective-permute-start | bytes 1572872 | tf_op jit(solution)/shard_map/ppermute | solution.py:15
  42.5 2.7 %fusion.36 = f32[512,2048]{1,0:T(8,128)} fusion(bf16[2048,128]{1,0:T(8,128)(2,1)S(1)} %collective-permute-done.4, bf16[2048,128]{1,0:T(8,128)(2,1)S(1)} %copy-done), kind=kOutput, calls=%fused_computation.52 | convolution fusion | flops 268435456 | bytes 4849664 | tf_op jit(solution)/shard_map/dot_general | solution.py:27
  45.2 2.7 %fusion.44 = f32[512,2048]{1,0:T(8,128)} fusion(bf16[2048,128]{1,0:T(8,128)(2,1)S(1)} %collective-permute-done.4, bf16[2048,128]{1,0:T(8,128)(2,1)S(1)} %copy-done), kind=kOutput, calls=%fused_computation.60 | convolution fusion | flops 268435456 | bytes 4849664 | tf_op jit(solution)/shard_map/dot_general | solution.py:27
  47.8 2.6 %fusion.48 = f32[512,2048]{1,0:T(8,128)} fusion(bf16[2048,128]{1,0:T(8,128)(2,1)S(1)} %collective-permute-done.10, bf16[2048,128]{1,0:T(8,128)(2,1)S(1)} %copy-done), kind=kOutput, calls=%fused_computation.64 | convolution fusion | flops 268435456 | bytes 4849664 | tf_op jit(solution)/shard_map/dot_general | solution.py:27
  50.5 2.7 %fusion.50 = f32[512,2048]{1,0:T(8,128)} fusion(bf16[2048,128]{1,0:T(8,128)(2,1)S(1)} %collective-permute-done.7, bf16[2048,128]{1,0:T(8,128)(2,1)S(1)} %copy-done), kind=kOutput, calls=%fused_computation.66 | convolution fusion | flops 268435456 | bytes 4849664 | tf_op jit(solution)/shard_map/dot_general | solution.py:27
  53.1 2.6 %fusion.52 = f32[512,2048]{1,0:T(8,128)} fusion(bf16[2048,128]{1,0:T(8,128)(2,1)S(1)} %collective-permute-done.4, bf16[2048,128]{1,0:T(8,128)(2,1)S(1)} %copy-done), kind=kOutput, calls=%fused_computation.68 | convolution fusion | flops 268435456 | bytes 4849664 | tf_op jit(solution)/shard_map/dot_general | solution.py:27
  55.8 2.7 %fusion.56 = f32[512,2048]{1,0:T(8,128)} fusion(bf16[2048,128]{1,0:T(8,128)(2,1)S(1)} %collective-permute-done.10, bf16[2048,128]{1,0:T(8,128)(2,1)S(1)} %copy-done), kind=kOutput, calls=%fused_computation.72 | convolution fusion | flops 268435456 | bytes 4849664 | tf_op jit(solution)/shard_map/dot_general | solution.py:27
  58.4 2.6 %fusion.58 = f32[512,2048]{1,0:T(8,128)} fusion(bf16[2048,128]{1,0:T(8,128)(2,1)S(1)} %collective-permute-done.7, bf16[2048,128]{1,0:T(8,128)(2,1)S(1)} %copy-done), kind=kOutput, calls=%fused_computation.74 | convolution fusion | flops 268435456 | bytes 4849664 | tf_op jit(solution)/shard_map/dot_general | solution.py:27
  61.1 0.0 collective-permute-done.3
  61.1 0.0 collective-permute-done.6
  61.1 0.0 collective-permute-done.9
  61.1 16.6 %fusion.9 = (f32[512]{0:T(512)S(1)}, f32[2048]{0:T(1024)S(1)}, f32[2048]{0:T(1024)S(1)}, f32[512]{0:T(512)S(1)}, f32[2048]{0:T(1024)S(1)}, /*index=5*/f32[512]{0...) fusion(bf16[2048]{0:T(1024)(128)(2,1)S(1)} %collective-permute-, ...), kind=kOutput, calls=%fused_computation.25 | convolution fusion | flops 318736384 | bytes 46931968 | tf_op jit(solution)/shard_map/dot_general | solution.py:27
  77.7 1.7 %collective-permute-start.11 = (f32[2048]{0:T(1024)S(1)}, f32[2048]{0:T(1024)S(1)}, u32[]{:S(2)}, u32[]{:S(2)}) collective-permute-start(f32[2048]{0:T(1024)S(1)} %maximum_maximum_fusion.4), channel_id=1, source_target_pairs={{0,12},{1,13},{2,14},{3,15},{4,0},{5,1},{6,2},{7,3},{8,4},{9,5},{1... | collective-permute-start | bytes 24584 | tf_op jit(solution)/shard_map/ppermute | solution.py:15
  79.4 0.0 collective-permute-start.8
  79.4 2.8 %collective-permute-start.5 = (f32[2048]{0:T(1024)S(1)}, f32[2048]{0:T(1024)S(1)}, u32[]{:S(2)}, u32[]{:S(2)}) collective-permute-start(f32[2048]{0:T(1024)S(1)} %maximum_maximum_fusion.6), channel_id=1, source_target_pairs={{0,14},{1,15},{2,0},{3,1},{4,2},{5,3},{6,4},{7,5},{8,6},{9,7},{10,... | collective-permute-start | bytes 24584 | tf_op jit(solution)/shard_map/ppermute | solution.py:15
  82.2 0.0 collective-permute-done.1
  82.2 0.7 fusion.38
  82.9 0.7 fusion.46
  83.6 0.7 fusion.54
  84.3 0.0 copy-start.1
  84.3 0.0 collective-permute-done
  84.4 3.2 %fusion.1 = (f32[512]{0:T(512)S(1)}, f32[2048]{0:T(1024)S(1)}, f32[2048]{0:T(1024)S(1)}, f32[512]{0:T(512)S(1)}, f32[2048]{0:T(1024)S(1)}, /*index=5*/f32[512]{0:T(512)S(1)}, f32[2048]{0:T(1024)S(1)}, f32[512]{0:T(512)S(1)}) fusion(bf16[2048]{0:T(1024)(128)(2,1)S(1)} %collective-permute-done, bf16[512]{0:T(512)(128)(2,1)S(1)} %get-tuple-element.88, ...), kind=kOutput, calls=%fused_computation.17 | convolution fusion | flops 285202432 | bytes 13287424 | tf_op jit(solution)/shard_map/dot_general | solution.py:27
  87.5 0.1 collective-permute-start.2
  87.6 0.0 collective-permute-done.11
  87.6 0.0 collective-permute-done.8
  87.6 0.0 collective-permute-done.5
  87.7 3.6 %collective-permute-done.2 = f32[2048]{0:T(1024)S(1)} collective-permute-done((f32[2048]{0:T(1024)S(1)}, f32[2048]{0:T(1024)S(1)}, u32[]{:S(2)}, u32[]{:S(2)}) %collective-permute-start.2) | collective-permute-done | bytes 8224 | tf_op jit(solution)/shard_map/ppermute | solution.py:15
  91.2 0.0 copy-done.1
  91.3 0.6 fusion.67
  (5 shorter events, 0.0 us)
Async XLA Ops:
  0.0 23.4 %copy-start = (bf16[2048,128]{1,0:T(8,128)(2,1)S(1)}, bf16[2048,128]{1,0:T(8,128)(2,1)}, u32[]{:S(2)}) copy-start(bf16[2048,128]{1,0:T(8,128)(2,1)} %param.3) | copy-start | bytes 1572868
  0.0 17.3 %collective-permute-start.10 = (bf16[2048,128]{1,0:T(8,128)(2,1)}, bf16[2048,128]{1,0:T(8,128)(2,1)S(1)}, u32[]{:S(2)}, u32[]{:S(2)}) collective-permute-start(bf16[2048,128]{1,0:T(8,128)(2,1)} %param.3), channel_id=1, source_target_pairs={{0,4},{1,5},{2,6},{3,7},{4,8},{5,9},{6,10},{7,11},{8,12},{9,13},{1... | collective-permute-start | bytes 1572872 | tf_op jit(solution)/shard_map/ppermute | solution.py:15
  3.7 57.3 %collective-permute-start.3 = (bf16[2048]{0:T(1024)(128)(2,1)S(1)}, bf16[2048]{0:T(1024)(128)(2,1)S(1)}, u32[]{:S(2)}, u32[]{:S(2)}) collective-permute-start(bf16[2048]{0:T(1024)(128)(2,1)S(1)} %convert_element_type.3), channel_id=1, source_target_pairs={{0,2},{1,3},{2,4},{3,5},{4,6},{5,7},{6,8},{7,9},{8,10},{9,11},{10,... | collective-permute-start | bytes 12296 | tf_op jit(solution)/shard_map/ppermute | solution.py:15
  5.2 55.8 %collective-permute-start.6 = (bf16[2048]{0:T(1024)(128)(2,1)S(1)}, bf16[2048]{0:T(1024)(128)(2,1)S(1)}, u32[]{:S(2)}, u32[]{:S(2)}) collective-permute-start(bf16[2048]{0:T(1024)(128)(2,1)S(1)} %convert_element_type.3), channel_id=1, source_target_pairs={{0,3},{1,4},{2,5},{3,6},{4,7},{5,8},{6,9},{7,10},{8,11},{9,12},{10... | collective-permute-start | bytes 12296 | tf_op jit(solution)/shard_map/ppermute | solution.py:15
  7.7 53.4 %collective-permute-start.9 = (bf16[2048]{0:T(1024)(128)(2,1)S(1)}, bf16[2048]{0:T(1024)(128)(2,1)S(1)}, u32[]{:S(2)}, u32[]{:S(2)}) collective-permute-start(bf16[2048]{0:T(1024)(128)(2,1)S(1)} %convert_element_type.3), channel_id=1, source_target_pairs={{0,4},{1,5},{2,6},{3,7},{4,8},{5,9},{6,10},{7,11},{8,12},{9,13},{1... | collective-permute-start | bytes 12296 | tf_op jit(solution)/shard_map/ppermute | solution.py:15
  9.3 20.3 %collective-permute-start.7 = (bf16[2048,128]{1,0:T(8,128)(2,1)}, bf16[2048,128]{1,0:T(8,128)(2,1)S(1)}, u32[]{:S(2)}, u32[]{:S(2)}) collective-permute-start(bf16[2048,128]{1,0:T(8,128)(2,1)} %param.3), channel_id=1, source_target_pairs={{0,3},{1,4},{2,5},{3,6},{4,7},{5,8},{6,9},{7,10},{8,11},{9,12},{10... | collective-permute-start | bytes 1572872 | tf_op jit(solution)/shard_map/ppermute | solution.py:15
  17.3 23.7 %collective-permute-start.4 = (bf16[2048,128]{1,0:T(8,128)(2,1)}, bf16[2048,128]{1,0:T(8,128)(2,1)S(1)}, u32[]{:S(2)}, u32[]{:S(2)}) collective-permute-start(bf16[2048,128]{1,0:T(8,128)(2,1)} %param.3), channel_id=1, source_target_pairs={{0,2},{1,3},{2,4},{3,5},{4,6},{5,7},{6,8},{7,9},{8,10},{9,11},{10,... | collective-permute-start | bytes 1572872 | tf_op jit(solution)/shard_map/ppermute | solution.py:15
  29.6 54.8 %collective-permute-start = (bf16[2048]{0:T(1024)(128)(2,1)S(1)}, bf16[2048]{0:T(1024)(128)(2,1)S(1)}, u32[]{:S(2)}, u32[]{:S(2)}) collective-permute-start(bf16[2048]{0:T(1024)(128)(2,1)S(1)} %convert_element_type.3), channel_id=1, source_target_pairs={{0,1},{1,2},{2,3},{3,4},{4,5},{5,6},{6,7},{7,8},{8,9},{9,10},{10,1... | collective-permute-start | bytes 12296 | tf_op jit(solution)/shard_map/ppermute | solution.py:15
  41.0 41.2 %collective-permute-start.1 = (bf16[2048,128]{1,0:T(8,128)(2,1)S(1)}, bf16[2048,128]{1,0:T(8,128)(2,1)S(1)}, u32[]{:S(2)}, u32[]{:S(2)}) collective-permute-start(bf16[2048,128]{1,0:T(8,128)(2,1)S(1)} %copy-done), channel_id=1, source_target_pairs={{0,1},{1,2},{2,3},{3,4},{4,5},{5,6},{6,7},{7,8},{8,9},{9,10},{10,1... | collective-permute-start | bytes 1572872 | tf_op jit(solution)/shard_map/ppermute | solution.py:15
  77.7 10.0 %collective-permute-start.11 = (f32[2048]{0:T(1024)S(1)}, f32[2048]{0:T(1024)S(1)}, u32[]{:S(2)}, u32[]{:S(2)}) collective-permute-start(f32[2048]{0:T(1024)S(1)} %maximum_maximum_fusion.4), channel_id=1, source_target_pairs={{0,12},{1,13},{2,14},{3,15},{4,0},{5,1},{6,2},{7,3},{8,4},{9,5},{1... | collective-permute-start | bytes 24584 | tf_op jit(solution)/shard_map/ppermute | solution.py:15
  79.4 8.2 %collective-permute-start.8 = (f32[2048]{0:T(1024)S(1)}, f32[2048]{0:T(1024)S(1)}, u32[]{:S(2)}, u32[]{:S(2)}) collective-permute-start(f32[2048]{0:T(1024)S(1)} %maximum_maximum_fusion.5), channel_id=1, source_target_pairs={{0,13},{1,14},{2,15},{3,0},{4,1},{5,2},{6,3},{7,4},{8,5},{9,6},{10... | collective-permute-start | bytes 24584 | tf_op jit(solution)/shard_map/ppermute | solution.py:15
  79.4 8.2 %collective-permute-start.5 = (f32[2048]{0:T(1024)S(1)}, f32[2048]{0:T(1024)S(1)}, u32[]{:S(2)}, u32[]{:S(2)}) collective-permute-start(f32[2048]{0:T(1024)S(1)} %maximum_maximum_fusion.6), channel_id=1, source_target_pairs={{0,14},{1,15},{2,0},{3,1},{4,2},{5,3},{6,4},{7,5},{8,6},{9,7},{10,... | collective-permute-start | bytes 24584 | tf_op jit(solution)/shard_map/ppermute | solution.py:15
  84.3 6.9 %copy-start.1 = (f32[2048]{0:T(1024)S(1)}, f32[2048]{0:T(1024)}, u32[]{:S(2)}) copy-start(f32[2048]{0:T(1024)} %param.5) | copy-start | bytes 24580
  87.5 3.7 %collective-permute-start.2 = (f32[2048]{0:T(1024)S(1)}, f32[2048]{0:T(1024)S(1)}, u32[]{:S(2)}, u32[]{:S(2)}) collective-permute-start(f32[2048]{0:T(1024)S(1)} %maximum_maximum_fusion.7), channel_id=1, source_target_pairs={{0,15},{1,0},{2,1},{3,2},{4,3},{5,4},{6,5},{7,6},{8,7},{9,8},{10,9... | collective-permute-start | bytes 24584 | tf_op jit(solution)/shard_map/ppermute | solution.py:15
where the time goes:
time: 92.1 us; the launch traced here: 91.9 us
  matrix products  52.1 us (57%)
  starting transfers between devices  19.8 us (21%)
  waiting for transfers between devices  18.5 us (20%)
  other arithmetic  1.34 us (1%)
    dot_general x16, matrix products, one_tile(): lax.dot_general(rows_x, other, (((1,), (1,)), ((), ())), preferred_elemen...  52.1 us
    ppermute x12, starting transfers between devices, from_behind(): return lax.ppermute(value, axis, pairs)  19.8 us
    ppermute x12, waiting for transfers between devices, from_behind(): return lax.ppermute(value, axis, pairs)  18.5 us
  transfers between devices with their start and end apart: 12, of which 4 were waited for; matrix products, arithmetic and copies ran while one was open for 58% of the time, Pallas kernels for 0%

commit v1 on v0

v1 whole, which is shorter than its diff:
```python
import functools

import jax
import jax.numpy as jnp
from jax import lax
from jax.experimental import pallas as pl
from jax.experimental.pallas import tpu as pltpu
from jax.sharding import PartitionSpec as P

ROUNDS = 4
NEG = -1e30
MARK = 2.0**50
LANES = 128
ROWS = 256
VMEM = 48 * 2**20


def routes(slabs, count):
    layer, ring, pair = [], [], []
    for slab in range(slabs):
        for block in range(count):
            place = block % ROUNDS

            def device(position):
                position = position % count
                return slab * count + (count - 1 - position if slab % 2 else position)

            layer.append((device(block), device(block - ROUNDS if place == 0 else block + ROUNDS)))
            ring.append((device(block), device(block - place + (place + 1) % ROUNDS)))
            if place < 2:
                pair.append((device(block), device(block + 2)))
    return layer, ring, pair


def backwards(pairs):
    return [(target, source) for source, target in pairs]


def pack_kernel(vec_ref, tag_ref, *outs):
    rows = vec_ref.shape[0] // len(outs)
    for index, out in enumerate(outs):
        out[:rows] = vec_ref[index * rows : (index + 1) * rows]
        out[rows:] = tag_ref[...]


def pack(vectors, tags, parts):
    count, dim = vectors.shape
    shape = jax.ShapeDtypeStruct((count // parts + tags.shape[0], dim), vectors.dtype)
    return pl.pallas_call(
        pack_kernel,
        out_shape=[shape] * parts,
        compiler_params=pltpu.CompilerParams(vmem_limit_bytes=VMEM),
        name="pack",
    )(vectors, tags)


def mark(tags, out, value):
    lane = lax.broadcasted_iota(jnp.int32, (LANES, LANES), 0).astype(jnp.float32)
    for row in range(tags.shape[0]):
        hit = jnp.where(tags[row : row + 1].astype(jnp.float32) == lane, jnp.float32(value), jnp.float32(0.0))
        out[row * LANES : (row + 1) * LANES] = hit.T.astype(jnp.bfloat16)


def tile(left, left_marks, right, right_marks, rowacc, col, fresh_row, fresh_col):
    wide = jnp.concatenate([right, right_marks], axis=1)
    columns = wide.shape[0]
    colmax = None
    for start in range(0, left.shape[0], ROWS):
        here = slice(start, start + ROWS)
        tall = jnp.concatenate([left[here], left_marks[here]], axis=1)
        scores = lax.dot_general(tall, wide, (((1,), (1,)), ((), ())), preferred_element_type=jnp.float32)
        best = scores[:, :LANES]
        for lane in range(LANES, columns, LANES):
            best = jnp.maximum(best, scores[:, lane : lane + LANES])
        rowacc[here] = best if fresh_row else jnp.maximum(rowacc[here], best)
        over = jnp.max(scores.reshape(ROWS // 8, 8, columns), axis=0)
        colmax = over if colmax is None else jnp.maximum(colmax, over)
    colmax = jnp.max(colmax, axis=0, keepdims=True)
    col[...] = colmax if fresh_col else jnp.maximum(col[...], colmax)


def fold(rowacc):
    return jnp.max(rowacc[...].reshape(rowacc.shape[0] // LANES, LANES, LANES), axis=2)


def first_kernel(has_pair, own, own_tags, z1, p1, q1, own_row, own_col, z_row, p_col, q_col,
                 own_m, z_m, p_m, q_m, own_acc, z_acc):
    half = own.shape[0] // 2
    mark(own_tags[...], own_m, -MARK)
    mark(z1[half:], z_m, MARK)
    mark(p1[half:], p_m, MARK)
    tile(own[...], own_m[...], p1[:half], p_m[:half], own_acc, p_col, True, True)
    tile(z1[:half], -z_m[:half], p1[:half], p_m[:half], z_acc, p_col, True, False)
    tile(z1[:half], z_m[:half], own[...], own_m[...], z_acc, own_col, False, True)
    q_col[...] = jnp.full(q_col.shape, NEG, jnp.float32)

    @pl.when(has_pair[0] > 0)
    def _():
        mark(q1[half:], q_m, MARK)
        tile(own[...], own_m[...], q1[:half], q_m[:half], own_acc, q_col, False, False)
        tile(z1[:half], -z_m[:half], q1[:half], q_m[:half], z_acc, q_col, False, False)

    own_row[...] = fold(own_acc)
    z_row[...] = fold(z_acc)


def second_kernel(has_pair, own, own_tags, z1, p1, q1, z2, p2, q2, own_row1, own_col1, z_row1, p_col1, q_col1,
                  own_out, z_out, p_out, q_out, own_m, z_m, p_m, q_m, own_acc, z_acc, own_col, p_col, q_col):
    half = own.shape[0] // 2
    mark(own_tags[...], own_m, -MARK)
    mark(z1[half:], z_m, MARK)
    mark(p1[half:], p_m, MARK)
    p_a, p_b = p_col.at[:, :half], p_col.at[:, half:]
    q_a, q_b = q_col.at[:, :half], q_col.at[:, half:]
    z_a, z_b = z_acc.at[:half], z_acc.at[half:]
    p_a[...] = p_col1[...]
    q_a[...] = q_col1[...]
    q_b[...] = jnp.full(q_b.shape, NEG, jnp.float32)
    own_col[...] = own_col1[...]
    tile(own[...], own_m[...], p2[:half], p_m[half:], own_acc, p_b, True, True)
    tile(z1[:half], -z_m[:half], p2[:half], p_m[half:], z_a, p_b, True, False)
    tile(z2[:half], -z_m[half:], p2[:half], p_m[half:], z_b, p_b, True, False)
    tile(z2[:half], -z_m[half:], p1[:half], p_m[:half], z_b, p_a, False, False)
    tile(z2[:half], z_m[half:], own[...], own_m[...], z_b, own_col, False, False)

    @pl.when(has_pair[0] > 0)
    def _():
        mark(q1[half:], q_m, MARK)
        tile(own[...], own_m[...], q2[:half], q_m[half:], own_acc, q_b, False, False)
        tile(z1[:half], -z_m[:half], q2[:half], q_m[half:], z_a, q_b, False, False)
        tile(z2[:half], -z_m[half:], q2[:half], q_m[half:], z_b, q_b, False, False)
        tile(z2[:half], -z_m[half:], q1[:half], q_m[:half], z_b, q_a, False, False)

    own_out[...] = jnp.maximum(jnp.maximum(own_row1[...], fold(own_acc)), own_col[...].reshape(own_out.shape))
    z_row = fold(z_acc)
    rows = z_row.shape[0] // 2
    z_out[:rows] = jnp.maximum(z_row1[...], z_row[:rows])
    z_out[rows:] = z_row[rows:]
    p_out[...] = p_col[...].reshape(p_out.shape)
    q_out[...] = q_col[...].reshape(q_out.shape)


def per_device(slabs, count, vectors, docs, prior):
    axes = ("slab", "corpus")
    tokens = vectors.shape[0]
    half = tokens // 2
    f32 = jnp.float32
    layer, ring, pair = routes(slabs, count)
    block = lax.axis_index("corpus")
    block = jnp.where(lax.axis_index("slab") % 2 == 1, count - 1 - block, block)
    has_pair = (block % ROUNDS >= 2).astype(jnp.int32).reshape(1)
    tags = docs.reshape(tokens // LANES, LANES).astype(jnp.bfloat16)
    halves = pack(vectors, tags, 2)
    (z1, p1, q1), (z2, p2, q2) = [
        [lax.ppermute(part, axes, pairs) for pairs in (layer, ring, pair)] for part in halves
    ]
    smem = pl.BlockSpec(memory_space=pltpu.SMEM)
    vmem = pl.BlockSpec(memory_space=pltpu.VMEM)
    rows = (tokens // LANES, LANES)
    marks = [pltpu.VMEM((tokens, LANES), jnp.bfloat16)] * 4
    params = pltpu.CompilerParams(vmem_limit_bytes=VMEM)
    struct = lambda *shape: jax.ShapeDtypeStruct(shape, f32)
    own_row, own_col, z_row, p_col, q_col = pl.pallas_call(
        first_kernel,
        out_shape=[struct(*rows), struct(1, tokens), struct(rows[0] // 2, LANES), struct(1, half), struct(1, half)],
        in_specs=[smem] + [vmem] * 5,
        scratch_shapes=marks + [pltpu.VMEM((tokens, LANES), f32), pltpu.VMEM((half, LANES), f32)],
        compiler_params=params,
        name="first",
    )(has_pair, vectors, tags, z1, p1, q1)
    own, z_max, p_max, q_max = pl.pallas_call(
        second_kernel,
        out_shape=[struct(*rows)] * 4,
        in_specs=[smem] + [vmem] * 13,
        scratch_shapes=marks
        + [pltpu.VMEM((tokens, LANES), f32)] * 2
        + [pltpu.VMEM((1, tokens), f32)] * 3,
        compiler_params=params,
        name="second",
    )(has_pair, vectors, tags, z1, p1, q1, z2, p2, q2, own_row, own_col, z_row, p_col, q_col)
    z_back = lax.ppermute(z_max, axes, backwards(layer))
    p_back = lax.ppermute(p_max, axes, backwards(ring))
    q_back = lax.ppermute(q_max, axes, backwards(pair))
    q_back = jnp.where(block % ROUNDS < 2, q_back, NEG)
    best = jnp.maximum(jnp.maximum(own, z_back), jnp.maximum(p_back, q_back))
    return jnp.maximum(prior, best.reshape(tokens))


def solution(mesh):
    spec = P(("slab", "corpus"))
    return jax.shard_map(
        functools.partial(per_device, mesh.shape["slab"], mesh.shape["corpus"]),
        mesh=mesh,
        in_specs=(spec, spec, spec),
        out_specs=spec,
        check_vma=False,
    )
```

time: 92.1 us -> 42.7 us (0.46)
  matrix products: 52.1 us -> 0 us
  waiting for transfers between devices: 18.5 us -> 7.6 us
  Pallas kernels: 0 us -> 8.82 us
  starting transfers between devices: 19.8 us -> 23.5 us
  local copies, waits for them, and re-layouts: 0.02 us -> 1.05 us
    dot_general x16 -> x0, matrix products: 52.1 us -> none  [one_tile(): lax.dot_general(rows_x, other, (((1,), (1,)), ((), ())), preferred_elemen...]
    ppermute x12 -> x9, waiting for transfers between devices: 18.5 us -> 7.6 us  [the longest x1 4.16 us: per_device(): q_back = lax.ppermute(q_max, axes, backwards(pair))]
    pallas_call x0 -> x3, Pallas kernels: none -> 8.82 us  [the longest x1 5.03 us: per_device(): pl.pallas_call(second_kernel, out_shape=[struct(*rows)] * 4, in_specs=[sm...]
    ppermute x12 -> x9, starting transfers between devices: 19.8 us -> 23.5 us  [the longest x6 13.9 us: per_device(): lax.ppermute(part, axes, pairs)]
    unnamed x4 -> x6, local copies, waits for them, and re-layouts: 0.01 us -> 1.05 us
  transfers between devices with their start and end apart: 12 -> 9, of which waited for: 4 -> 5; matrix products, arithmetic and copies ran while one was open for 58% -> 0% of each run, Pallas kernels for 0% -> 9%
where the time goes in v1:
time: 42.7 us; the launch traced here: 42.4 us
  starting transfers between devices  23.5 us (55%)
  Pallas kernels  8.82 us (21%)
  waiting for transfers between devices  7.6 us (18%)
  other arithmetic  1.3 us (3%)
  local copies, waits for them, and re-layouts  1.05 us (2%)
    ppermute x6, starting transfers between devices, per_device(): lax.ppermute(part, axes, pairs)  13.9 us
    ppermute x1, starting transfers between devices, per_device(): p_back = lax.ppermute(p_max, axes, backwards(ring))  8.26 us
    pallas_call x1, Pallas kernels, per_device(): pl.pallas_call(second_kernel, out_shape=[struct(*rows)] * 4, in_specs=[sm...  5.03 us
    ppermute x1, waiting for transfers between devices, per_device(): q_back = lax.ppermute(q_max, axes, backwards(pair))  4.16 us
    pallas_call x1, Pallas kernels, per_device(): pl.pallas_call(first_kernel, out_shape=[struct(*rows), struct(1, tokens),...  3.76 us
    ppermute x6, waiting for transfers between devices, per_device(): lax.ppermute(part, axes, pairs)  2.17 us
    ppermute x1, starting transfers between devices, per_device(): q_back = lax.ppermute(q_max, axes, backwards(pair))  1.28 us
    ppermute x1, waiting for transfers between devices, per_device(): z_back = lax.ppermute(z_max, axes, backwards(layer))  1.26 us
  transfers between devices with their start and end apart: 9, of which 5 were waited for; matrix products, arithmetic and copies ran while one was open for 0% of the time, Pallas kernels for 9%

profile of v1, /device:TPU:0, one launch (start us, length us, event | category | flops | bytes accessed | tf_op | source)
XLA Modules:
  0.0 42.4 jit_solution(17104141720044780908)
XLA Ops:
  0.0 0.7 %convert_bitcast_fusion.tag_ref.own_tags = bf16[16,128]{1,0:T(8,128)(2,1)S(1)} fusion(s32[2048]{0:T(1024)} %param.4), kind=kLoop, calls=%fused_computation.1 | loop fusion | flops 2048 | bytes 12288 | tf_op jit(solution)/shard_map/convert_element_type | solution.py:152
  0.7 0.0 copy-start
  0.7 1.0 %copy-done = bf16[2048,128]{1,0:T(8,128)(2,1)S(1)} copy-done((bf16[2048,128]{1,0:T(8,128)(2,1)S(1)}, bf16[2048,128]{1,0:T(8,128)(2,1)}, u32[]{:S(2)}) %copy-start) | copy-done | bytes 524312
  1.7 0.0 copy-start.1
  1.8 5.1 %collective-permute-start = (bf16[1040,128]{1,0:T(8,128)(2,1)S(1)}, bf16[1040,128]{1,0:T(8,128)(2,1)S(1)}, u32[]{:S(2)}, u32[]{:S(2)}) collective-permute-start(bf16[1040,128]{1,0:T(8,128)(2,1)S(1)} %get-tuple-element.16), channel_id=1, source_target_pairs={{0,12},{1,5},{2,6},{3,7},{4,0},{5,9},{6,10},{7,11},{8,4},{9,13},{1... | collective-permute-start | bytes 798728 | tf_op jit(solution)/shard_map/ppermute | solution.py:155
  6.9 0.0 collective-permute-start.1
  6.9 2.9 %collective-permute-start.2 = (bf16[1040,128]{1,0:T(8,128)(2,1)S(1)}, bf16[1040,128]{1,0:T(8,128)(2,1)S(1)}, u32[]{:S(2)}, u32[]{:S(2)}) collective-permute-start(bf16[1040,128]{1,0:T(8,128)(2,1)S(1)} %get-tuple-element.16), channel_id=1, source_target_pairs={{0,2},{1,3},{4,6},{5,7},{8,10},{9,11},{12,14},{13,15},{31,29},{30,... | collective-permute-start | bytes 798728 | tf_op jit(solution)/shard_map/ppermute | solution.py:155
  9.8 2.3 %collective-permute-start.3 = (bf16[1040,128]{1,0:T(8,128)(2,1)S(1)}, bf16[1040,128]{1,0:T(8,128)(2,1)S(1)}, u32[]{:S(2)}, u32[]{:S(2)}) collective-permute-start(bf16[1040,128]{1,0:T(8,128)(2,1)S(1)} %get-tuple-element.17), channel_id=1, source_target_pairs={{0,12},{1,5},{2,6},{3,7},{4,0},{5,9},{6,10},{7,11},{8,4},{9,13},{1... | collective-permute-start | bytes 798728 | tf_op jit(solution)/shard_map/ppermute | solution.py:155
  12.1 0.3 collective-permute-start.4
  12.4 1.3 %collective-permute-done.z1 = bf16[1040,128]{1,0:T(8,128)(2,1)S(1)} collective-permute-done((bf16[1040,128]{1,0:T(8,128)(2,1)S(1)}, bf16[1040,128]{1,0:T(8,128)(2,1)S(1)}, u32[]{:S(2)}, u32[]{:S(2)}) %collective-permute-start) | collective-permute-done | bytes 266272 | tf_op jit(solution)/shard_map/ppermute | solution.py:155
  13.7 3.3 %collective-permute-start.5 = (bf16[1040,128]{1,0:T(8,128)(2,1)S(1)}, bf16[1040,128]{1,0:T(8,128)(2,1)S(1)}, u32[]{:S(2)}, u32[]{:S(2)}) collective-permute-start(bf16[1040,128]{1,0:T(8,128)(2,1)S(1)} %get-tuple-element.17), channel_id=1, source_target_pairs={{0,2},{1,3},{4,6},{5,7},{8,10},{9,11},{12,14},{13,15},{31,29},{30,... | collective-permute-start | bytes 798728 | tf_op jit(solution)/shard_map/ppermute | solution.py:155
  17.0 0.0 collective-permute-done.1.p1
  17.0 0.0 collective-permute-done.2.q1
  17.0 0.0 copy-done.1
  17.0 3.8 %first.1 = (f32[16,128]{1,0:T(8,128)S(1)}, f32[1,2048]{1,0:T(1,128)S(1)}, f32[8,128]{1,0:T(8,128)S(1)}, f32[1,1024]{1,0:T(1,128)S(1)}, f32[1,1024]{1,0:T(1,128)S(1)}) custom-call(s32[1]{0:T(128)} %bitcast.has_pair, bf16[2048,128]{1,0:T(8,128)(2,1)S(1)} %copy-done.1, bf16[16,128]{1,0:T(8,128)(2,1)S(1)} %convert_bitcast_fusion.tag_ref.own_tags, ...), custom_call_target="tpu_custom_call" | custom-call | tf_op jit(solution)/shard_map/first/pallas_call | solution.py:163
  20.8 0.0 collective-permute-done.3.z2
  20.8 0.6 %collective-permute-done.4.p2 = bf16[1040,128]{1,0:T(8,128)(2,1)S(1)} collective-permute-done((bf16[1040,128]{1,0:T(8,128)(2,1)S(1)}, bf16[1040,128]{1,0:T(8,128)(2,1)S(1)}, u32[]{:S(2)}, u32[]{:S(2)}) %collective-permute-start.4) | collective-permute-done | bytes 266272 | tf_op jit(solution)/shard_map/ppermute | solution.py:155
  21.5 0.3 collective-permute-done.5.q2
  21.7 5.0 %second.1 = (f32[16,128]{1,0:T(8,128)S(1)}, f32[16,128]{1,0:T(8,128)S(1)}, f32[16,128]{1,0:T(8,128)S(1)}, f32[16,128]{1,0:T(8,128)S(1)}) custom-call(s32[1]{0:T(128)} %bitcast.has_pair, bf16[2048,128]{1,0:T(8,128)(2,1)S(1)} %copy-done.1, bf16[16,128]{1,0:T(8,128)(2,1)S(1)} %convert_bitcast_fusion.tag_ref.own_tags, ...), custom_call_target="tpu_custom_call" | custom-call | tf_op jit(solution)/shard_map/second/pallas_call | solution.py:171
  26.7 0.0 copy-start.2
  26.8 8.3 %collective-permute-start.7 = (f32[16,128]{1,0:T(8,128)S(1)}, f32[16,128]{1,0:T(8,128)S(1)}, u32[]{:S(2)}, u32[]{:S(2)}) collective-permute-start(f32[16,128]{1,0:T(8,128)S(1)} %get-tuple-element.25), channel_id=1, source_target_pairs={{1,0},{2,1},{3,2},{0,3},{5,4},{6,5},{7,6},{4,7},{9,8},{10,9},{11,1... | collective-permute-start | bytes 24584 | tf_op jit(solution)/shard_map/ppermute | solution.py:182
  35.0 1.3 %collective-permute-start.8 = (f32[16,128]{1,0:T(8,128)S(1)}, f32[16,128]{1,0:T(8,128)S(1)}, u32[]{:S(2)}, u32[]{:S(2)}) collective-permute-start(f32[16,128]{1,0:T(8,128)S(1)} %get-tuple-element.26), channel_id=1, source_target_pairs={{2,0},{3,1},{6,4},{7,5},{10,8},{11,9},{14,12},{15,13},{29,31},{28,... | collective-permute-start | bytes 24584 | tf_op jit(solution)/shard_map/ppermute | solution.py:183
  36.3 0.1 collective-permute-start.6
  36.4 0.0 collective-permute-done.7
  36.4 4.2 %collective-permute-done.8 = f32[16,128]{1,0:T(8,128)S(1)} collective-permute-done((f32[16,128]{1,0:T(8,128)S(1)}, f32[16,128]{1,0:T(8,128)S(1)}, u32[]{:S(2)}, u32[]{:S(2)}) %collective-permute-start.8) | collective-permute-done | bytes 8224 | tf_op jit(solution)/shard_map/ppermute | solution.py:183
  40.6 1.3 %collective-permute-done.6 = f32[16,128]{1,0:T(8,128)S(1)} collective-permute-done((f32[16,128]{1,0:T(8,128)S(1)}, f32[16,128]{1,0:T(8,128)S(1)}, u32[]{:S(2)}, u32[]{:S(2)}) %collective-permute-start.6) | collective-permute-done | bytes 8224 | tf_op jit(solution)/shard_map/ppermute | solution.py:181
  41.8 0.0 copy-done.2
  41.8 0.6 %bitcast_maximum_fusion = f32[2048]{0:T(1024)} fusion(f32[2048]{0:T(1024)S(1)} %copy-done.2, f32[16,128]{1,0:T(8,128)S(1)} %collective-permute-done.7, f32[16,128]{1,0:T(8,128)S(1)} %collective-permute-done.8, f32[16,128]{1,0:T(8,128)S(1)} %get-tuple-element.23, f32[16,128]{1,0:T(8,128)S(1)} %collective-permute-done.6, pred[]{:T(512)S(6)} %lt.17), kind=kLoop, calls=%fused_computation | loop fusion | flops 10240 | bytes 49153 | tf_op jit(solution)/shard_map/max | solution.py:186
  (1 shorter events, 0.0 us)
Async XLA Ops:
  0.7 1.0 %copy-start = (bf16[2048,128]{1,0:T(8,128)(2,1)S(1)}, bf16[2048,128]{1,0:T(8,128)(2,1)}, u32[]{:S(2)}) copy-start(bf16[2048,128]{1,0:T(8,128)(2,1)} %own.3) | copy-start | bytes 1572868
  1.7 15.3 %copy-start.1 = (bf16[2048,128]{1,0:T(8,128)(2,1)S(1)}, bf16[2048,128]{1,0:T(8,128)(2,1)}, u32[]{:S(2)}) copy-start(bf16[2048,128]{1,0:T(8,128)(2,1)} %own.3) | copy-start | bytes 1572868
  1.8 11.9 %collective-permute-start = (bf16[1040,128]{1,0:T(8,128)(2,1)S(1)}, bf16[1040,128]{1,0:T(8,128)(2,1)S(1)}, u32[]{:S(2)}, u32[]{:S(2)}) collective-permute-start(bf16[1040,128]{1,0:T(8,128)(2,1)S(1)} %get-tuple-element.16), channel_id=1, source_target_pairs={{0,12},{1,5},{2,6},{3,7},{4,0},{5,9},{6,10},{7,11},{8,4},{9,13},{1... | collective-permute-start | bytes 798728 | tf_op jit(solution)/shard_map/ppermute | solution.py:155
  6.9 10.1 %collective-permute-start.1 = (bf16[1040,128]{1,0:T(8,128)(2,1)S(1)}, bf16[1040,128]{1,0:T(8,128)(2,1)S(1)}, u32[]{:S(2)}, u32[]{:S(2)}) collective-permute-start(bf16[1040,128]{1,0:T(8,128)(2,1)S(1)} %get-tuple-element.16), channel_id=1, source_target_pairs={{0,1},{1,2},{2,3},{3,0},{4,5},{5,6},{6,7},{7,4},{8,9},{9,10},{10,1... | collective-permute-start | bytes 798728 | tf_op jit(solution)/shard_map/ppermute | solution.py:155
  6.9 10.1 %collective-permute-start.2 = (bf16[1040,128]{1,0:T(8,128)(2,1)S(1)}, bf16[1040,128]{1,0:T(8,128)(2,1)S(1)}, u32[]{:S(2)}, u32[]{:S(2)}) collective-permute-start(bf16[1040,128]{1,0:T(8,128)(2,1)S(1)} %get-tuple-element.16), channel_id=1, source_target_pairs={{0,2},{1,3},{4,6},{5,7},{8,10},{9,11},{12,14},{13,15},{31,29},{30,... | collective-permute-start | bytes 798728 | tf_op jit(solution)/shard_map/ppermute | solution.py:155
  9.8 11.0 %collective-permute-start.3 = (bf16[1040,128]{1,0:T(8,128)(2,1)S(1)}, bf16[1040,128]{1,0:T(8,128)(2,1)S(1)}, u32[]{:S(2)}, u32[]{:S(2)}) collective-permute-start(bf16[1040,128]{1,0:T(8,128)(2,1)S(1)} %get-tuple-element.17), channel_id=1, source_target_pairs={{0,12},{1,5},{2,6},{3,7},{4,0},{5,9},{6,10},{7,11},{8,4},{9,13},{1... | collective-permute-start | bytes 798728 | tf_op jit(solution)/shard_map/ppermute | solution.py:155
  12.1 9.4 %collective-permute-start.4 = (bf16[1040,128]{1,0:T(8,128)(2,1)S(1)}, bf16[1040,128]{1,0:T(8,128)(2,1)S(1)}, u32[]{:S(2)}, u32[]{:S(2)}) collective-permute-start(bf16[1040,128]{1,0:T(8,128)(2,1)S(1)} %get-tuple-element.17), channel_id=1, source_target_pairs={{0,1},{1,2},{2,3},{3,0},{4,5},{5,6},{6,7},{7,4},{8,9},{9,10},{10,1... | collective-permute-start | bytes 798728 | tf_op jit(solution)/shard_map/ppermute | solution.py:155
  13.7 8.0 %collective-permute-start.5 = (bf16[1040,128]{1,0:T(8,128)(2,1)S(1)}, bf16[1040,128]{1,0:T(8,128)(2,1)S(1)}, u32[]{:S(2)}, u32[]{:S(2)}) collective-permute-start(bf16[1040,128]{1,0:T(8,128)(2,1)S(1)} %get-tuple-element.17), channel_id=1, source_target_pairs={{0,2},{1,3},{4,6},{5,7},{8,10},{9,11},{12,14},{13,15},{31,29},{30,... | collective-permute-start | bytes 798728 | tf_op jit(solution)/shard_map/ppermute | solution.py:155
  26.7 15.1 %copy-start.2 = (f32[2048]{0:T(1024)S(1)}, f32[2048]{0:T(1024)}, u32[]{:S(2)}) copy-start(f32[2048]{0:T(1024)} %param.5) | copy-start | bytes 24580
  26.8 9.6 %collective-permute-start.7 = (f32[16,128]{1,0:T(8,128)S(1)}, f32[16,128]{1,0:T(8,128)S(1)}, u32[]{:S(2)}, u32[]{:S(2)}) collective-permute-start(f32[16,128]{1,0:T(8,128)S(1)} %get-tuple-element.25), channel_id=1, source_target_pairs={{1,0},{2,1},{3,2},{0,3},{5,4},{6,5},{7,6},{4,7},{9,8},{10,9},{11,1... | collective-permute-start | bytes 24584 | tf_op jit(solution)/shard_map/ppermute | solution.py:182
  35.0 5.5 %collective-permute-start.8 = (f32[16,128]{1,0:T(8,128)S(1)}, f32[16,128]{1,0:T(8,128)S(1)}, u32[]{:S(2)}, u32[]{:S(2)}) collective-permute-start(f32[16,128]{1,0:T(8,128)S(1)} %get-tuple-element.26), channel_id=1, source_target_pairs={{2,0},{3,1},{6,4},{7,5},{10,8},{11,9},{14,12},{15,13},{29,31},{28,... | collective-permute-start | bytes 24584 | tf_op jit(solution)/shard_map/ppermute | solution.py:183
  36.3 5.5 %collective-permute-start.6 = (f32[16,128]{1,0:T(8,128)S(1)}, f32[16,128]{1,0:T(8,128)S(1)}, u32[]{:S(2)}, u32[]{:S(2)}) collective-permute-start(f32[16,128]{1,0:T(8,128)S(1)} %get-tuple-element.24), channel_id=1, source_target_pairs={{12,0},{5,1},{6,2},{7,3},{0,4},{9,5},{10,6},{11,7},{4,8},{13,9},{1... | collective-permute-start | bytes 24584 | tf_op jit(solution)/shard_map/ppermute | solution.py:181

commit v2 on v0

v2 whole, which is shorter than its diff:
```python
import functools

import jax
import jax.numpy as jnp
from jax import lax
from jax.experimental import pallas as pl
from jax.experimental.pallas import tpu as pltpu
from jax.sharding import PartitionSpec as P

ROUNDS = 4
NEG = -1e30
MARK = 2.0**50
LANES = 128
ROWS = 256
VMEM = 24 * 2**20
F32 = jnp.float32
BF16 = jnp.bfloat16


def routes(slabs, count):
    layer, ring, pair, beside = [], [], [], []
    for slab in range(slabs):
        for block in range(count):
            place = block % ROUNDS

            def device(position, slab=slab):
                position = position % count
                return slab * count + (count - 1 - position if slab % 2 else position)

            here, other = device(block), device(count - 1 - block, slab ^ 1)
            layer.append((here, device(block - ROUNDS if place == 0 else block + ROUNDS)))
            ring.append((here, device(block - place + (place + 1) % ROUNDS)))
            pair.append((here, device(block + 2) if place < 2 else other))
            beside.append((here, other))
    return layer, ring, pair, beside


def backwards(pairs):
    return [(target, source) for source, target in pairs]


def struct(*shape, dtype=F32):
    return jax.ShapeDtypeStruct(shape, dtype)


def call(name, kernel, operands, outs, specs=None, scratch=()):
    moved = sum(x.size * x.dtype.itemsize for x in list(operands) + list(outs))
    return pl.pallas_call(
        kernel,
        out_shape=outs,
        in_specs=specs or [pl.BlockSpec(memory_space=pltpu.VMEM)] * len(operands),
        out_specs=[pl.BlockSpec(memory_space=pltpu.VMEM)] * len(outs),
        scratch_shapes=scratch,
        compiler_params=pltpu.CompilerParams(vmem_limit_bytes=VMEM),
        cost_estimate=pl.CostEstimate(flops=0, bytes_accessed=moved, transcendentals=0),
        name=name,
    )(*operands)


def mark(tags, out, value):
    lane = lax.broadcasted_iota(jnp.int32, (LANES, LANES), 0).astype(F32)
    for row in range(tags.shape[0]):
        hit = jnp.where(tags[row : row + 1].astype(F32) == lane, F32(value), F32(0.0))
        out[row * LANES : (row + 1) * LANES] = hit.T.astype(BF16)


def tile(left, left_marks, right, right_marks):
    wide = jnp.concatenate([right, right_marks], axis=1)
    columns = wide.shape[0]
    colmax, rowmax = None, []
    for start in range(0, left.shape[0], ROWS):
        here = slice(start, start + ROWS)
        tall = jnp.concatenate([left[here], left_marks[here]], axis=1)
        scores = lax.dot_general(tall, wide, (((1,), (1,)), ((), ())), preferred_element_type=F32)
        best = scores[:, :LANES]
        for lane in range(LANES, columns, LANES):
            best = jnp.maximum(best, scores[:, lane : lane + LANES])
        rowmax.append(jnp.max(best.reshape(ROWS // LANES, LANES, LANES), axis=2))
        over = jnp.max(scores.reshape(ROWS // 8, 8, columns), axis=0)
        colmax = over if colmax is None else jnp.maximum(colmax, over)
    return jnp.concatenate(rowmax, axis=0), jnp.max(colmax, axis=0, keepdims=True)


def pack(vec, docs, own1, own2, own):
    tokens = vec.shape[0]
    half = tokens // 2
    tags = docs[...].astype(F32).astype(BF16)
    own1[:half] = vec[:half]
    own2[:half] = vec[half:]
    own[:tokens] = vec[...]
    own1[half:] = tags
    own2[half:] = tags
    own[tokens:] = tags


def per_device(slabs, count, vectors, docs, prior):
    axes = ("slab", "corpus")
    tokens, dim = vectors.shape
    half = tokens // 2
    lines = tokens // LANES
    part = lines // 2
    layer, ring, pair, beside = routes(slabs, count)
    block = lax.axis_index("corpus")
    block = jnp.where(lax.axis_index("slab") % 2 == 1, count - 1 - block, block)
    has_pair = (block % ROUNDS >= 2).astype(jnp.int32).reshape(1)
    marks = struct(tokens, LANES, dtype=BF16)
    smem = pl.BlockSpec(memory_space=pltpu.SMEM)
    vmem = pl.BlockSpec(memory_space=pltpu.VMEM)
    whole, piece = struct(lines, LANES), struct(part, LANES)

    own1, own2, own = call(
        "pack",
        pack,
        [vectors, docs.reshape(lines, LANES)],
        [struct(half + lines, dim, dtype=BF16)] * 2 + [struct(tokens + lines, dim, dtype=BF16)],
    )
    p1 = lax.ppermute(own1, axes, ring)
    z1 = lax.ppermute(own1, axes, layer)
    q = lax.ppermute(own, axes, pair)
    p2 = lax.ppermute(own2, axes, ring)
    z2 = lax.ppermute(own2, axes, layer)
    def own_marks(own, out):
        mark(own[tokens:], out, -MARK)

    (own_m,) = call("own_marks", own_marks, [own], [marks])

    def ring1(own, own_m, p1, p_m, own_out, p_out):
        mark(p1[half:], p_m, MARK)
        row, col = tile(own[:tokens], own_m[...], p1[:half], p_m[:half])
        own_out[...] = row
        p_out[...] = col.reshape(part, LANES)

    p_m, own_max, p1_max = call("ring1", ring1, [own, own_m, p1], [marks, whole, piece])

    def layer1(own, own_m, p1, p_m, z1, own_max, p_max, z_m, own_out, p_out, z_out):
        mark(z1[half:], z_m, MARK)
        row1, col1 = tile(z1[:half], -z_m[:half], p1[:half], p_m[:half])
        row2, col2 = tile(z1[:half], z_m[:half], own[:tokens], own_m[...])
        own_out[...] = jnp.maximum(own_max[...], col2.reshape(lines, LANES))
        p_out[...] = jnp.maximum(p_max[...], col1.reshape(part, LANES))
        z_out[...] = jnp.maximum(row1, row2)

    z_m, own_max, p1_max, z1_max = call(
        "layer1", layer1, [own, own_m, p1, p_m, z1, own_max, p1_max], [marks, whole, piece, piece]
    )

    def second(p1, p2, p_m, z1, z2, z_m, z1_max, p1_max, z_out, p_out):
        row1, col1 = tile(z2[:half], -z_m[half:], p1[:half], p_m[:half])
        row2, col2 = tile(z2[:half], -z_m[half:], p2[:half], p_m[half:])
        row3, col3 = tile(z1[:half], -z_m[:half], p2[:half], p_m[half:])
        z_out[:part] = jnp.maximum(z1_max[...], row3)
        z_out[part:] = jnp.maximum(row1, row2)
        p_out[:part] = jnp.maximum(p1_max[...], col1.reshape(part, LANES))
        p_out[part:] = jnp.maximum(col2, col3).reshape(part, LANES)

    z_max, p_max = call("second", second, [p1, p2, p_m, z1, z2, z_m, z1_max, p1_max], [whole, whole])
    swap, z_max = lax.optimization_barrier((q, z_max))
    r = lax.ppermute(swap, axes, beside)

    def ring2(own, own_m, p2, p_m, own_max, p_max, own_out, p_out):
        row, col = tile(own[:tokens], own_m[...], p2[:half], p_m[half:])
        own_out[...] = jnp.maximum(own_max[...], row)
        p_out[:part] = p_max[:part]
        p_out[part:] = jnp.maximum(p_max[part:], col.reshape(part, LANES))

    own_max, p_max = call("ring2", ring2, [own, own_m, p2, p_m, own_max, p_max], [whole, whole])
    p_back = lax.ppermute(p_max, axes, backwards(ring))

    cut = tokens * 3 // 4

    def pairs1(has, z1, z2, z_m, q, r, z_max, after, z_out, row_out, col_out, q_m, r_m):
        mark(q[tokens:], q_m, MARK)

        @pl.when(has[0] > 0)
        def _():
            row1, col1 = tile(z1[:half], -z_m[:half], q[:cut], q_m[:cut])
            row2, col2 = tile(z2[:half], -z_m[half:], q[:cut], q_m[:cut])
            z_out[:part] = jnp.maximum(z_max[:part], row1)
            z_out[part:] = jnp.maximum(z_max[part:], row2)
            row_out[...] = jnp.full((lines, LANES), NEG, F32)
            col_out[...] = jnp.maximum(col1, col2).reshape(cut // LANES, LANES)

        @pl.when(has[0] == 0)
        def _():
            mark(r[tokens:], r_m, -MARK)
            row, col = tile(q[:tokens], q_m[...], r[:cut], r_m[:cut])
            z_out[...] = z_max[...]
            row_out[...] = row
            col_out[...] = col.reshape(cut // LANES, LANES)

    z_max, row_max, col_max, q_m, r_m = call(
        "pairs1",
        pairs1,
        [has_pair, z1, z2, z_m, q, r, z_max, p_max],
        [whole, whole, struct(cut // LANES, LANES), marks, marks],
        specs=[smem] + [vmem] * 7,
    )

    def pairs2(has, z1, z2, z_m, q, q_m, r, r_m, z_max, row_max, col_max, own_max, p_back, z_out, own_out, out):
        own_out[...] = jnp.maximum(own_max[...], p_back[...])
        out[lines : lines + cut // LANES] = col_max[...]

        @pl.when(has[0] > 0)
        def _():
            row1, col1 = tile(z1[:half], -z_m[:half], q[cut:tokens], q_m[cut:])
            row2, col2 = tile(z2[:half], -z_m[half:], q[cut:tokens], q_m[cut:])
            z_out[:part] = jnp.maximum(z_max[:part], row1)
            z_out[part:] = jnp.maximum(z_max[part:], row2)
            out[:lines] = row_max[...]
            out[lines + cut // LANES :] = jnp.maximum(col1, col2).reshape(lines - cut // LANES, LANES)

        @pl.when(has[0] == 0)
        def _():
            row, col = tile(q[:tokens], q_m[...], r[cut:tokens], r_m[cut:])
            z_out[...] = z_max[...]
            out[:lines] = jnp.maximum(row_max[...], row)
            out[lines + cut // LANES :] = col.reshape(lines - cut // LANES, LANES)

    z_max, own_max, mine = call(
        "pairs2",
        pairs2,
        [has_pair, z1, z2, z_m, q, q_m, r, r_m, z_max, row_max, col_max, own_max, p_back],
        [whole, whole, struct(2 * lines, LANES)],
        specs=[smem] + [vmem] * 12,
    )
    theirs = lax.ppermute(mine, axes, beside)

    def layer2(own, own_m, z2, z_m, own_max, z_max, own_out, z_out):
        row, col = tile(z2[:half], z_m[half:], own[:tokens], own_m[...])
        own_out[...] = jnp.maximum(own_max[...], col.reshape(lines, LANES))
        z_out[:part] = z_max[:part]
        z_out[part:] = jnp.maximum(z_max[part:], row)

    own_max, z_max = call(
        "layer2", layer2, [own, own_m, z2, z_m, own_max, z_max], [whole, whole]
    )
    z_back = lax.ppermute(z_max, axes, backwards(layer))

    def merge(has, mine, theirs, own_max, own_out, q_out):
        got = jnp.where(has[0] > 0, theirs[...], F32(NEG))
        own_out[...] = jnp.maximum(own_max[...], got[:lines])
        q_out[...] = jnp.maximum(mine[lines:], got[lines:])

    own_max, q_max = call(
        "merge", merge, [has_pair, mine, theirs, own_max], [whole, whole], specs=[smem] + [vmem] * 3
    )
    q_back = lax.ppermute(q_max, axes, backwards(pair))
    q_back = jnp.where(has_pair > 0, NEG, q_back)
    best = jnp.maximum(jnp.maximum(own_max, z_back), q_back)
    return jnp.maximum(prior, best.reshape(tokens))


def solution(mesh):
    spec = P(("slab", "corpus"))
    return jax.shard_map(
        functools.partial(per_device, mesh.shape["slab"], mesh.shape["corpus"]),
        mesh=mesh,
        in_specs=(spec, spec, spec),
        out_specs=spec,
        check_vma=False,
    )
```

time: 92.1 us -> 37.2 us (0.40)
  matrix products: 52.1 us -> 0 us
  Pallas kernels: 0 us -> 12 us
  starting transfers between devices: 19.8 us -> 10.8 us
  waiting for transfers between devices: 18.5 us -> 11.7 us
  local copies, waits for them, and re-layouts: 0.02 us -> 1.74 us
    dot_general x16 -> x0, matrix products: 52.1 us -> none  [one_tile(): lax.dot_general(rows_x, other, (((1,), (1,)), ((), ())), preferred_elemen...]
    pallas_call x0 -> x10, Pallas kernels: none -> 12 us  [call(): pl.pallas_call(kernel, out_shape=outs, in_specs=specs or [pl.BlockSpec(me...]
    ppermute x12 -> x10, starting transfers between devices: 19.8 us -> 10.8 us  [the longest x1 3.6 us: per_device(): z1 = lax.ppermute(own1, axes, layer)]
    ppermute x12 -> x10, waiting for transfers between devices: 18.5 us -> 11.7 us  [the longest x1 5.14 us: per_device(): z_back = lax.ppermute(z_max, axes, backwards(layer))]
    unnamed x4 -> x6, local copies, waits for them, and re-layouts: 0.01 us -> 1.74 us
  transfers between devices with their start and end apart: 12 -> 10, of which waited for: 4 -> 5; matrix products, arithmetic and copies ran while one was open for 58% -> 0% of each run, Pallas kernels for 0% -> 30%
where the time goes in v2:
time: 37.2 us; the launch traced here: 37 us
  Pallas kernels  12 us (32%)
  waiting for transfers between devices  11.7 us (31%)
  starting transfers between devices  10.8 us (29%)
  local copies, waits for them, and re-layouts  1.74 us (5%)
  other arithmetic  0.6 us (2%)
    pallas_call x10, Pallas kernels, call(): pl.pallas_call(kernel, out_shape=outs, in_specs=specs or [pl.BlockSpec(me...  12 us
    ppermute x1, waiting for transfers between devices, per_device(): z_back = lax.ppermute(z_max, axes, backwards(layer))  5.14 us
    ppermute x1, starting transfers between devices, per_device(): z1 = lax.ppermute(own1, axes, layer)  3.6 us
    ppermute x1, starting transfers between devices, per_device(): q = lax.ppermute(own, axes, pair)  2.98 us
    ppermute x1, waiting for transfers between devices, per_device(): p1 = lax.ppermute(own1, axes, ring)  2.59 us
    ppermute x1, waiting for transfers between devices, per_device(): z1 = lax.ppermute(own1, axes, layer)  2.1 us
    ppermute x1, waiting for transfers between devices, per_device(): z2 = lax.ppermute(own2, axes, layer)  1.85 us
    unnamed x6, local copies, waits for them, and re-layouts  1.74 us
  transfers between devices with their start and end apart: 10, of which 5 were waited for; matrix products, arithmetic and copies ran while one was open for 0% of the time, Pallas kernels for 30%

profile of v2, /device:TPU:0, one launch (start us, length us, event | category | flops | bytes accessed | tf_op | source)
XLA Modules:
  0.0 37.0 jit_solution(10381283572041079634)
XLA Ops:
  0.0 0.0 copy-start
  0.0 1.0 %copy-done = bf16[2048,128]{1,0:T(8,128)(2,1)S(1)} copy-done((bf16[2048,128]{1,0:T(8,128)(2,1)S(1)}, bf16[2048,128]{1,0:T(8,128)(2,1)}, u32[]{:S(2)}) %copy-start) | copy-done | bytes 524312
  1.0 0.0 copy-start.1
  1.0 0.7 %copy-done.1 = s32[2048]{0:T(1024)S(1)} copy-done((s32[2048]{0:T(1024)S(1)}, s32[2048]{0:T(1024)}, u32[]{:S(2)}) %copy-start.1) | copy-done | bytes 8216
  1.7 0.1 pack.1
  1.8 3.0 %collective-permute-start.3 = (bf16[2064,128]{1,0:T(8,128)(2,1)S(1)}, bf16[2064,128]{1,0:T(8,128)(2,1)S(1)}, u32[]{:S(2)}, u32[]{:S(2)}) collective-permute-start(bf16[2064,128]{1,0:T(8,128)(2,1)S(1)} %get-tuple-element.35.own), channel_id=1, source_target_pairs={{0,2},{1,3},{2,18},{3,19},{4,6},{5,7},{6,22},{7,23},{8,10},{9,11},... | collective-permute-start | bytes 1585160 | tf_op jit(solution)/shard_map/ppermute | solution.py:119
  4.8 1.5 %collective-permute-start.2 = (bf16[1040,128]{1,0:T(8,128)(2,1)S(1)}, bf16[1040,128]{1,0:T(8,128)(2,1)S(1)}, u32[]{:S(2)}, u32[]{:S(2)}) collective-permute-start(bf16[1040,128]{1,0:T(8,128)(2,1)S(1)} %get-tuple-element.33), channel_id=1, source_target_pairs={{0,1},{1,2},{2,3},{3,0},{4,5},{5,6},{6,7},{7,4},{8,9},{9,10},{10,1... | collective-permute-start | bytes 798728 | tf_op jit(solution)/shard_map/ppermute | solution.py:117
  6.3 3.6 %collective-permute-start = (bf16[1040,128]{1,0:T(8,128)(2,1)S(1)}, bf16[1040,128]{1,0:T(8,128)(2,1)S(1)}, u32[]{:S(2)}, u32[]{:S(2)}) collective-permute-start(bf16[1040,128]{1,0:T(8,128)(2,1)S(1)} %get-tuple-element.33), channel_id=1, source_target_pairs={{0,12},{1,5},{2,6},{3,7},{4,0},{5,9},{6,10},{7,11},{8,4},{9,13},{1... | collective-permute-start | bytes 798728 | tf_op jit(solution)/shard_map/ppermute | solution.py:118
  9.9 0.4 %collective-permute-start.1 = (bf16[1040,128]{1,0:T(8,128)(2,1)S(1)}, bf16[1040,128]{1,0:T(8,128)(2,1)S(1)}, u32[]{:S(2)}, u32[]{:S(2)}) collective-permute-start(bf16[1040,128]{1,0:T(8,128)(2,1)S(1)} %get-tuple-element.34), channel_id=1, source_target_pairs={{0,12},{1,5},{2,6},{3,7},{4,0},{5,9},{6,10},{7,11},{8,4},{9,13},{1... | collective-permute-start | bytes 798728 | tf_op jit(solution)/shard_map/ppermute | solution.py:121
  10.3 0.0 collective-permute-start.4
  10.3 0.2 own_marks.1.own_m
  10.6 2.6 %collective-permute-done.2.p1 = bf16[1040,128]{1,0:T(8,128)(2,1)S(1)} collective-permute-done((bf16[1040,128]{1,0:T(8,128)(2,1)S(1)}, bf16[1040,128]{1,0:T(8,128)(2,1)S(1)}, u32[]{:S(2)}, u32[]{:S(2)}) %collective-permute-start.2) | collective-permute-done | bytes 266272 | tf_op jit(solution)/shard_map/ppermute | solution.py:117
  13.1 1.5 %ring1.1 = (bf16[2048,128]{1,0:T(8,128)(2,1)S(1)}, f32[16,128]{1,0:T(8,128)S(1)}, f32[8,128]{1,0:T(8,128)S(1)}) custom-call(bf16[2064,128]{1,0:T(8,128)(2,1)S(1)} %get-tuple-element.35.own, bf16[2048,128]{1,0:T(8,128)(2,1)S(1)} %own_marks.1.own_m, bf16[1040,128]{1,0:T(8,128)(2,1)S(1)} %collective-permute-done.2.p1), custom_call_target="tpu_custom_call" | custom-call | bytes 1855488 | tf_op jit(solution)/shard_map/ring1/pallas_call | solution.py:48
  14.6 2.1 %collective-permute-done.z1 = bf16[1040,128]{1,0:T(8,128)(2,1)S(1)} collective-permute-done((bf16[1040,128]{1,0:T(8,128)(2,1)S(1)}, bf16[1040,128]{1,0:T(8,128)(2,1)S(1)}, u32[]{:S(2)}, u32[]{:S(2)}) %collective-permute-start) | collective-permute-done | bytes 266272 | tf_op jit(solution)/shard_map/ppermute | solution.py:118
  16.7 2.0 %layer1.1 = (bf16[2048,128]{1,0:T(8,128)(2,1)S(1)}, f32[16,128]{1,0:T(8,128)S(1)}, f32[8,128]{1,0:T(8,128)S(1)}, f32[8,128]{1,0:T(8,128)S(1)}) custom-call(bf16[2064,128]{1,0:T(8,128)(2,1)S(1)} %get-tuple-element.35.own, bf16[2048,128]{1,0:T(8,128)(2,1)S(1)} %own_marks.1.own_m, bf16[1040,128]{1,0:T(8,128)(2,1)S(1)} %collective-permute-done.2.p1, ...), custom_call_target="tpu_custom_call" | custom-call | bytes 2662400 | tf_op jit(solution)/shard_map/layer1/pallas_call | solution.py:48
  18.8 1.8 %collective-permute-done.1.z2 = bf16[1040,128]{1,0:T(8,128)(2,1)S(1)} collective-permute-done((bf16[1040,128]{1,0:T(8,128)(2,1)S(1)}, bf16[1040,128]{1,0:T(8,128)(2,1)S(1)}, u32[]{:S(2)}, u32[]{:S(2)}) %collective-permute-start.1) | collective-permute-done | bytes 266272 | tf_op jit(solution)/shard_map/ppermute | solution.py:121
  20.6 0.0 collective-permute-done.4.p2
  20.6 2.0 %second.1 = (f32[16,128]{1,0:T(8,128)S(1)}, f32[16,128]{1,0:T(8,128)S(1)}) custom-call(bf16[1040,128]{1,0:T(8,128)(2,1)S(1)} %collective-permute-done.2.p1, bf16[1040,128]{1,0:T(8,128)(2,1)S(1)} %collective-permute-done.4.p2, bf16[2048,128]{1,0:T(8,128)(2,1)S(1)} %get-tuple-element.36.p_m, bf16[1040,128]{1,0:T(8,128)(2,1)S(1)} %collective-permute-done.z1, ...), custom_call_target="tpu_custom_call" | custom-call | bytes 2138112 | tf_op jit(solution)/shard_map/second/pallas_call | solution.py:48
  22.6 0.0 collective-permute-done.3.q
  22.6 0.1 collective-permute-start.5
  22.7 1.4 %ring2.1 = (f32[16,128]{1,0:T(8,128)S(1)}, f32[16,128]{1,0:T(8,128)S(1)}) custom-call(bf16[2064,128]{1,0:T(8,128)(2,1)S(1)} %get-tuple-element.35.own, bf16[2048,128]{1,0:T(8,128)(2,1)S(1)} %own_marks.1.own_m, bf16[1040,128]{1,0:T(8,128)(2,1)S(1)} %collective-permute-done.4.p2, bf16[2048,128]{1,0:T(8,128)(2,1)S(1)} %get-tuple-element.36.p_m, ...), custom_call_target="tpu_custom_call" | custom-call | bytes 1875968 | tf_op jit(solution)/shard_map/ring2/pallas_call | solution.py:48
  24.1 1.3 %collective-permute-start.6 = (f32[16,128]{1,0:T(8,128)S(1)}, f32[16,128]{1,0:T(8,128)S(1)}, u32[]{:S(2)}, u32[]{:S(2)}) collective-permute-start(f32[16,128]{1,0:T(8,128)S(1)} %get-tuple-element.47.after), channel_id=1, source_target_pairs={{1,0},{2,1},{3,2},{0,3},{5,4},{6,5},{7,6},{4,7},{9,8},{10,9},{11,1... | collective-permute-start | bytes 24584 | tf_op jit(solution)/shard_map/ppermute | solution.py:167
  25.5 0.0 collective-permute-done.5.r
  25.5 2.4 %pairs1.1 = (f32[16,128]{1,0:T(8,128)S(1)}, f32[16,128]{1,0:T(8,128)S(1)}, f32[12,128]{1,0:T(8,128)S(1)}, bf16[2048,128]{1,0:T(8,128)(2,1)S(1)}, bf16[2048,128]{1,0:T(8,128)(2,1)S(1)}) custom-call(s32[1]{0:T(128)} %bitcast.has, bf16[1040,128]{1,0:T(8,128)(2,1)S(1)} %collective-permute-done.z1, bf16[1040,128]{1,0:T(8,128)(2,1)S(1)} %collective-permute-done.1.z2, ...), custom_call_target="tpu_custom_call" | custom-call | bytes 3201028 | tf_op jit(solution)/shard_map/pairs1/pallas_call | solution.py:48
  27.9 0.0 collective-permute-done.6.p_back
  27.9 1.0 %pairs2.1 = (f32[16,128]{1,0:T(8,128)S(1)}, f32[16,128]{1,0:T(8,128)S(1)}, f32[32,128]{1,0:T(8,128)S(1)}) custom-call(s32[1]{0:T(128)} %bitcast.has, bf16[1040,128]{1,0:T(8,128)(2,1)S(1)} %collective-permute-done.z1, bf16[1040,128]{1,0:T(8,128)(2,1)S(1)} %collective-permute-done.1.z2, bf16[2048,128]{1,0:T(8,128)(2,1)S(1)} %get-tuple-element.39.z_m, ...), custom_call_target="tpu_custom_call" | custom-call | bytes 3233796 | tf_op jit(solution)/shard_map/pairs2/pallas_call | solution.py:48
  28.9 0.1 collective-permute-start.7
  29.0 1.4 %layer2.1 = (f32[16,128]{1,0:T(8,128)S(1)}, f32[16,128]{1,0:T(8,128)S(1)}) custom-call(bf16[2064,128]{1,0:T(8,128)(2,1)S(1)} %get-tuple-element.35.own, bf16[2048,128]{1,0:T(8,128)(2,1)S(1)} %own_marks.1.own_m, bf16[1040,128]{1,0:T(8,128)(2,1)S(1)} %collective-permute-done.1.z2, bf16[2048,128]{1,0:T(8,128)(2,1)S(1)} %get-tuple-element.39.z_m, ...), custom_call_target="tpu_custom_call" | custom-call | bytes 1875968 | tf_op jit(solution)/shard_map/layer2/pallas_call | solution.py:48
  30.4 0.8 %collective-permute-start.8 = (f32[16,128]{1,0:T(8,128)S(1)}, f32[16,128]{1,0:T(8,128)S(1)}, u32[]{:S(2)}, u32[]{:S(2)}) collective-permute-start(f32[16,128]{1,0:T(8,128)S(1)} %get-tuple-element.59), channel_id=1, source_target_pairs={{12,0},{5,1},{6,2},{7,3},{0,4},{9,5},{10,6},{11,7},{4,8},{13,9},{1... | collective-permute-start | bytes 24584 | tf_op jit(solution)/shard_map/ppermute | solution.py:237
  31.2 0.0 collective-permute-done.7.theirs
  31.2 0.0 copy-start.2
  31.2 0.0 collective-permute-start.9
  31.2 5.1 %collective-permute-done.8 = f32[16,128]{1,0:T(8,128)S(1)} collective-permute-done((f32[16,128]{1,0:T(8,128)S(1)}, f32[16,128]{1,0:T(8,128)S(1)}, u32[]{:S(2)}, u32[]{:S(2)}) %collective-permute-start.8) | collective-permute-done | bytes 8224 | tf_op jit(solution)/shard_map/ppermute | solution.py:237
  36.4 0.1 collective-permute-done.9
  36.4 0.0 copy-done.2
  36.4 0.6 %bitcast_maximum_fusion = f32[2048]{0:T(1024)} fusion(f32[2048]{0:T(1024)S(1)} %copy-done.2, f32[16,128]{1,0:T(8,128)S(1)} %collective-permute-done.9, f32[16,128]{1,0:T(8,128)S(1)} %get-tuple-element.58, f32[16,128]{1,0:T(8,128)S(1)} %collective-permute-done.8, pred[]{:T(512)} %bitcast.2), kind=kLoop, calls=%fused_computation | loop fusion | flops 8192 | bytes 40961 | tf_op jit(solution)/shard_map/max | solution.py:250
  (1 shorter events, 0.0 us)
Async XLA Ops:
  0.0 1.0 %copy-start = (bf16[2048,128]{1,0:T(8,128)(2,1)S(1)}, bf16[2048,128]{1,0:T(8,128)(2,1)}, u32[]{:S(2)}) copy-start(bf16[2048,128]{1,0:T(8,128)(2,1)} %vec.1) | copy-start | bytes 1572868
  1.0 0.7 %copy-start.1 = (s32[2048]{0:T(1024)S(1)}, s32[2048]{0:T(1024)}, u32[]{:S(2)}) copy-start(s32[2048]{0:T(1024)} %param.4) | copy-start | bytes 24580
  1.8 20.8 %collective-permute-start.3 = (bf16[2064,128]{1,0:T(8,128)(2,1)S(1)}, bf16[2064,128]{1,0:T(8,128)(2,1)S(1)}, u32[]{:S(2)}, u32[]{:S(2)}) collective-permute-start(bf16[2064,128]{1,0:T(8,128)(2,1)S(1)} %get-tuple-element.35.own), channel_id=1, source_target_pairs={{0,2},{1,3},{2,18},{3,19},{4,6},{5,7},{6,22},{7,23},{8,10},{9,11},... | collective-permute-start | bytes 1585160 | tf_op jit(solution)/shard_map/ppermute | solution.py:119
  4.8 8.3 %collective-permute-start.2 = (bf16[1040,128]{1,0:T(8,128)(2,1)S(1)}, bf16[1040,128]{1,0:T(8,128)(2,1)S(1)}, u32[]{:S(2)}, u32[]{:S(2)}) collective-permute-start(bf16[1040,128]{1,0:T(8,128)(2,1)S(1)} %get-tuple-element.33), channel_id=1, source_target_pairs={{0,1},{1,2},{2,3},{3,0},{4,5},{5,6},{6,7},{7,4},{8,9},{9,10},{10,1... | collective-permute-start | bytes 798728 | tf_op jit(solution)/shard_map/ppermute | solution.py:117
  6.3 10.5 %collective-permute-start = (bf16[1040,128]{1,0:T(8,128)(2,1)S(1)}, bf16[1040,128]{1,0:T(8,128)(2,1)S(1)}, u32[]{:S(2)}, u32[]{:S(2)}) collective-permute-start(bf16[1040,128]{1,0:T(8,128)(2,1)S(1)} %get-tuple-element.33), channel_id=1, source_target_pairs={{0,12},{1,5},{2,6},{3,7},{4,0},{5,9},{6,10},{7,11},{8,4},{9,13},{1... | collective-permute-start | bytes 798728 | tf_op jit(solution)/shard_map/ppermute | solution.py:118
  9.9 10.7 %collective-permute-start.1 = (bf16[1040,128]{1,0:T(8,128)(2,1)S(1)}, bf16[1040,128]{1,0:T(8,128)(2,1)S(1)}, u32[]{:S(2)}, u32[]{:S(2)}) collective-permute-start(bf16[1040,128]{1,0:T(8,128)(2,1)S(1)} %get-tuple-element.34), channel_id=1, source_target_pairs={{0,12},{1,5},{2,6},{3,7},{4,0},{5,9},{6,10},{7,11},{8,4},{9,13},{1... | collective-permute-start | bytes 798728 | tf_op jit(solution)/shard_map/ppermute | solution.py:121
  10.3 10.3 %collective-permute-start.4 = (bf16[1040,128]{1,0:T(8,128)(2,1)S(1)}, bf16[1040,128]{1,0:T(8,128)(2,1)S(1)}, u32[]{:S(2)}, u32[]{:S(2)}) collective-permute-start(bf16[1040,128]{1,0:T(8,128)(2,1)S(1)} %get-tuple-element.34), channel_id=1, source_target_pairs={{0,1},{1,2},{2,3},{3,0},{4,5},{5,6},{6,7},{7,4},{8,9},{9,10},{10,1... | collective-permute-start | bytes 798728 | tf_op jit(solution)/shard_map/ppermute | solution.py:120
  22.6 2.8 %collective-permute-start.5 = (bf16[2064,128]{1,0:T(8,128)(2,1)S(1)}, bf16[2064,128]{1,0:T(8,128)(2,1)S(1)}, u32[]{:S(2)}, u32[]{:S(2)}) collective-permute-start(bf16[2064,128]{1,0:T(8,128)(2,1)S(1)} %collective-permute-done.3.q), channel_id=1, source_target_pairs={{0,16},{1,17},{2,18},{3,19},{4,20},{5,21},{6,22},{7,23},{8,24},{9,... | collective-permute-start | bytes 1585160 | tf_op jit(solution)/shard_map/ppermute | solution.py:158
  24.1 3.7 %collective-permute-start.6 = (f32[16,128]{1,0:T(8,128)S(1)}, f32[16,128]{1,0:T(8,128)S(1)}, u32[]{:S(2)}, u32[]{:S(2)}) collective-permute-start(f32[16,128]{1,0:T(8,128)S(1)} %get-tuple-element.47.after), channel_id=1, source_target_pairs={{1,0},{2,1},{3,2},{0,3},{5,4},{6,5},{7,6},{4,7},{9,8},{10,9},{11,1... | collective-permute-start | bytes 24584 | tf_op jit(solution)/shard_map/ppermute | solution.py:167
  28.9 2.2 %collective-permute-start.7 = (f32[32,128]{1,0:T(8,128)S(1)}, f32[32,128]{1,0:T(8,128)S(1)}, u32[]{:S(2)}, u32[]{:S(2)}) collective-permute-start(f32[32,128]{1,0:T(8,128)S(1)} %get-tuple-element.54.mine), channel_id=1, source_target_pairs={{0,16},{1,17},{2,18},{3,19},{4,20},{5,21},{6,22},{7,23},{8,24},{9,... | collective-permute-start | bytes 49160 | tf_op jit(solution)/shard_map/ppermute | solution.py:226
  30.4 6.0 %collective-permute-start.8 = (f32[16,128]{1,0:T(8,128)S(1)}, f32[16,128]{1,0:T(8,128)S(1)}, u32[]{:S(2)}, u32[]{:S(2)}) collective-permute-start(f32[16,128]{1,0:T(8,128)S(1)} %get-tuple-element.59), channel_id=1, source_target_pairs={{12,0},{5,1},{6,2},{7,3},{0,4},{9,5},{10,6},{11,7},{4,8},{13,9},{1... | collective-permute-start | bytes 24584 | tf_op jit(solution)/shard_map/ppermute | solution.py:237
  31.2 5.2 %copy-start.2 = (f32[2048]{0:T(1024)S(1)}, f32[2048]{0:T(1024)}, u32[]{:S(2)}) copy-start(f32[2048]{0:T(1024)} %param.5) | copy-start | bytes 24580
  31.2 5.2 %collective-permute-start.9 = (f32[16,128]{1,0:T(8,128)S(1)}, f32[16,128]{1,0:T(8,128)S(1)}, u32[]{:S(2)}, u32[]{:S(2)}) collective-permute-start(f32[16,128]{1,0:T(8,128)S(1)} %get-tuple-element.60), channel_id=1, source_target_pairs={{2,0},{3,1},{18,2},{19,3},{6,4},{7,5},{22,6},{23,7},{10,8},{11,9},... | collective-permute-start | bytes 24584 | tf_op jit(solution)/shard_map/ppermute | solution.py:247

commit v3 on v2

v3 whole, which is shorter than its diff:
```python
import functools

import jax
import jax.numpy as jnp
from jax import lax
from jax.experimental import pallas as pl
from jax.experimental.pallas import tpu as pltpu
from jax.sharding import PartitionSpec as P

ROUNDS = 4
NEG = -1e30
MARK = 2.0**50
LANES = 128
ROWS = 256
VMEM = 24 * 2**20
F32 = jnp.float32
BF16 = jnp.bfloat16
HEAD = 10


def routes(slabs, count):
    layer, ring, pair, beside = [], [], [], []
    for slab in range(slabs):
        for block in range(count):
            place = block % ROUNDS

            def device(position, slab=slab):
                position = position % count
                return slab * count + (count - 1 - position if slab % 2 else position)

            here, other = device(block), device(count - 1 - block, slab ^ 1)
            layer.append((here, device(block - ROUNDS if place == 0 else block + ROUNDS)))
            ring.append((here, device(block - place + (place + 1) % ROUNDS)))
            pair.append((here, device(block + 2) if place < 2 else other))
            beside.append((here, other))
    return layer, ring, pair, beside


def backwards(pairs):
    return [(target, source) for source, target in pairs]


def struct(*shape, dtype=F32):
    return jax.ShapeDtypeStruct(shape, dtype)


def call(name, kernel, operands, outs, specs=None, scratch=()):
    moved = sum(x.size * x.dtype.itemsize for x in list(operands) + list(outs))
    return pl.pallas_call(
        kernel,
        out_shape=outs,
        in_specs=specs or [pl.BlockSpec(memory_space=pltpu.VMEM)] * len(operands),
        out_specs=[pl.BlockSpec(memory_space=pltpu.VMEM)] * len(outs),
        scratch_shapes=scratch,
        compiler_params=pltpu.CompilerParams(vmem_limit_bytes=VMEM),
        cost_estimate=pl.CostEstimate(flops=0, bytes_accessed=moved, transcendentals=0),
        name=name,
    )(*operands)


def mark(tags, out, value):
    lane = lax.broadcasted_iota(jnp.int32, (LANES, LANES), 0).astype(F32)
    for row in range(tags.shape[0]):
        hit = jnp.where(tags[row : row + 1].astype(F32) == lane, F32(value), F32(0.0))
        out[row * LANES : (row + 1) * LANES] = hit.T.astype(BF16)


def tile(lefts, rights):
    wide = jnp.concatenate([jnp.concatenate(pair, axis=1) for pair in rights], axis=0)
    columns = wide.shape[0]
    colmax, rowmax = None, []
    for left, left_marks in lefts:
        for start in range(0, left.shape[0], ROWS):
            here = slice(start, start + ROWS)
            tall = jnp.concatenate([left[here], left_marks[here]], axis=1)
            scores = lax.dot_general(tall, wide, (((1,), (1,)), ((), ())), preferred_element_type=F32)
            best = scores[:, :LANES]
            for lane in range(LANES, columns, LANES):
                best = jnp.maximum(best, scores[:, lane : lane + LANES])
            rowmax.append(jnp.max(best.reshape(ROWS // LANES, LANES, LANES), axis=2))
            over = jnp.max(scores.reshape(ROWS // 8, 8, columns), axis=0)
            colmax = over if colmax is None else jnp.maximum(colmax, over)
    return jnp.concatenate(rowmax, axis=0), jnp.max(colmax, axis=0).reshape(columns // LANES, LANES)


def pack(vec, docs, own1, own2, own):
    tokens = vec.shape[0]
    head = own1.shape[0] - docs.shape[0]
    tags = docs[...].astype(F32).astype(BF16)
    own1[:head] = vec[:head]
    own1[head:] = tags
    own2[...] = vec[head:]
    own[:tokens] = vec[...]
    own[tokens:] = tags


def after(value, *others):
    return lax.optimization_barrier((value, *others))[0]


def per_device(slabs, count, vectors, docs, prior):
    axes = ("slab", "corpus")
    tokens, dim = vectors.shape
    lines = tokens // LANES
    head = tokens * HEAD // 16
    part = head // LANES
    rest = lines - part
    layer, ring, pair, beside = routes(slabs, count)
    block = lax.axis_index("corpus")
    block = jnp.where(lax.axis_index("slab") % 2 == 1, count - 1 - block, block)
    has_pair = (block % ROUNDS >= 2).astype(jnp.int32).reshape(1)
    marks = struct(tokens, LANES, dtype=BF16)
    smem = pl.BlockSpec(memory_space=pltpu.SMEM)
    vmem = pl.BlockSpec(memory_space=pltpu.VMEM)
    whole, piece1, piece2 = struct(lines, LANES), struct(part, LANES), struct(rest, LANES)

    own1, own2, own = call(
        "pack",
        pack,
        [vectors, docs.reshape(lines, LANES)],
        [struct(rows, dim, dtype=BF16) for rows in (head + lines, tokens - head, tokens + lines)],
    )
    p1 = lax.ppermute(own1, axes, ring)
    z1 = lax.ppermute(own1, axes, layer)
    q = lax.ppermute(own, axes, pair)
    p2 = lax.ppermute(own2, axes, ring)
    z2 = lax.ppermute(own2, axes, layer)

    def own_marks(own, out):
        mark(own[tokens:], out, -MARK)

    (own_m,) = call("own_marks", own_marks, [own], [marks])

    def ring1(own, own_m, p1, p_m, own_out, p_out):
        mark(p1[head:], p_m, MARK)
        p_out[...], own_out[...] = tile([(p1[:head], p_m[:head])], [(own[:tokens], own_m[...])])

    p_m, own_max, p1_max = call("ring1", ring1, [own, own_m, p1], [marks, whole, piece1])

    def layer1(own, own_m, p1, p_m, z1, own_max, p_max, z_m, own_out, p_out, z_out):
        mark(z1[head:], z_m, MARK)
        row, col = tile([(z1[:head], z_m[:head])], [(own[:tokens], own_m[...]), (p1[:head], -p_m[:head])])
        own_out[...] = jnp.maximum(own_max[...], col[:lines])
        p_out[...] = jnp.maximum(p_max[...], col[lines:])
        z_out[...] = row

    z_m, own_max, p1_max, z1_max = call(
        "layer1", layer1, [own, own_m, p1, p_m, z1, own_max, p1_max], [marks, whole, piece1, piece1]
    )

    def second(p1, p2, p_m, z1, z2, z_m, z1_max, p1_max, z_out, p_out):
        row1, col1 = tile([(z2[...], -z_m[head:])], [(p1[:head], p_m[:head]), (p2[...], p_m[head:])])
        row2, col2 = tile([(p2[...], -p_m[head:])], [(z1[:head], z_m[:head])])
        z_out[:part] = jnp.maximum(z1_max[...], col2)
        z_out[part:] = row1
        p_out[:part] = jnp.maximum(p1_max[...], col1[:part])
        p_out[part:] = jnp.maximum(col1[part:], row2)

    z_max, p_max = call("second", second, [p1, p2, p_m, z1, z2, z_m, z1_max, p1_max], [whole, whole])
    r = lax.ppermute(after(q, z_max), axes, beside)

    def ring2(own, own_m, p2, p_m, own_max, p_max, own_out, p_out):
        row, col = tile([(p2[...], p_m[head:])], [(own[:tokens], own_m[...])])
        own_out[...] = jnp.maximum(own_max[...], col)
        p_out[:part] = p_max[:part]
        p_out[part:lines] = jnp.maximum(p_max[part:], row)
        p_out[lines:] = jnp.full((3 * lines, LANES), NEG, F32)

    own_max, p_max = call(
        "ring2", ring2, [own, own_m, p2, p_m, own_max, p_max], [whole, struct(4 * lines, LANES)]
    )
    p_back = lax.ppermute(p_max, axes, backwards(ring))

    def pairs(has, z1, z2, z_m, q, r, z_max, after, z_out, out, q_m, r_m):
        mark(q[tokens:], q_m, MARK)

        @pl.when(has[0] > 0)
        def _():
            row, col = tile([(z1[:head], -z_m[:head]), (z2[...], -z_m[head:])], [(q[:tokens], q_m[...])])
            z_out[...] = jnp.maximum(z_max[...], row)
            out[:lines] = jnp.full((lines, LANES), NEG, F32)
            out[lines:] = col

        @pl.when(has[0] == 0)
        def _():
            mark(r[tokens:], r_m, -MARK)
            z_out[...] = z_max[...]
            out[:lines], out[lines:] = tile([(q[:tokens], q_m[...])], [(r[:tokens], r_m[...])])

    z_max, mine = call(
        "pairs",
        pairs,
        [has_pair, z1, z2, z_m, q, r, z_max, p_max],
        [whole, struct(2 * lines, LANES)],
        specs=[smem] + [vmem] * 7,
        scratch=[pltpu.VMEM((tokens, LANES), BF16)] * 2,
    )
    theirs = lax.ppermute(mine, axes, beside)

    def layer2(own, own_m, z2, z_m, own_max, z_max, own_out, z_out):
        row, col = tile([(z2[...], z_m[head:])], [(own[:tokens], own_m[...])])
        own_out[...] = jnp.maximum(own_max[...], col)
        z_out[:part] = z_max[:part]
        z_out[part:] = jnp.maximum(z_max[part:], row)

    own_max, z_max = call("layer2", layer2, [own, own_m, z2, z_m, own_max, z_max], [whole, whole])
    z_back = lax.ppermute(z_max, axes, backwards(layer))

    def merge(has, mine, theirs, own_max, p_back, own_out, q_out):
        got = jnp.where(has[0] > 0, theirs[...], F32(NEG))
        own_out[...] = jnp.maximum(jnp.maximum(own_max[...], p_back[:lines]), got[:lines])
        q_out[...] = jnp.maximum(mine[lines:], got[lines:])

    own_max, q_max = call(
        "merge", merge, [has_pair, mine, theirs, own_max, p_back], [whole, whole], specs=[smem] + [vmem] * 4
    )
    q_back = lax.ppermute(q_max, axes, backwards(pair))
    q_back = jnp.where(has_pair > 0, NEG, q_back)
    best = jnp.maximum(jnp.maximum(own_max, z_back), q_back)
    return jnp.maximum(prior, best.reshape(tokens))


def solution(mesh):
    spec = P(("slab", "corpus"))
    return jax.shard_map(
        functools.partial(per_device, mesh.shape["slab"], mesh.shape["corpus"]),
        mesh=mesh,
        in_specs=(spec, spec, spec),
        out_specs=spec,
        check_vma=False,
    )
```

time: 37.2 us -> 36.3 us (0.976)
  waiting for transfers between devices: 11.7 us -> 10.8 us
  starting transfers between devices: 10.8 us -> 11.2 us
    ppermute x1, waiting for transfers between devices: 2.59 us -> 5.06 us  [per_device(): p1 = lax.ppermute(own1, axes, ring)]
    ppermute x1, waiting for transfers between devices: 1.85 us -> 0.01 us  [per_device(): z2 = lax.ppermute(own2, axes, layer)]
    ppermute x1, waiting for transfers between devices: 2.1 us -> 0.77 us  [per_device(): z1 = lax.ppermute(own1, axes, layer)]
    ppermute x1, waiting for transfers between devices: 5.14 us -> 4.57 us  [per_device(): z_back = lax.ppermute(z_max, axes, backwards(layer))]
    pallas_call x10 -> x9, Pallas kernels: 12 us -> 11.7 us  [call(): pl.pallas_call(kernel, out_shape=outs, in_specs=specs or [pl.BlockSpec(me...]
  transfers between devices with their start and end apart: 10 -> 10, of which waited for: 5 -> 4; matrix products, arithmetic and copies ran while one was open for 0% -> 0% of each run, Pallas kernels for 30% -> 32%
where the time goes in v3:
time: 36.3 us; the launch traced here: 36.1 us
  Pallas kernels  11.7 us (32%)
  starting transfers between devices  11.2 us (31%)
  waiting for transfers between devices  10.8 us (30%)
  local copies, waits for them, and re-layouts  1.74 us (5%)
  other arithmetic  0.6 us (2%)
    pallas_call x9, Pallas kernels, call(): pl.pallas_call(kernel, out_shape=outs, in_specs=specs or [pl.BlockSpec(me...  11.7 us
    ppermute x1, waiting for transfers between devices, per_device(): p1 = lax.ppermute(own1, axes, ring)  5.06 us
    ppermute x1, waiting for transfers between devices, per_device(): z_back = lax.ppermute(z_max, axes, backwards(layer))  4.57 us
    ppermute x1, starting transfers between devices, per_device(): z1 = lax.ppermute(own1, axes, layer)  3.6 us
    ppermute x1, starting transfers between devices, per_device(): q = lax.ppermute(own, axes, pair)  2.98 us
    unnamed x6, local copies, waits for them, and re-layouts  1.74 us
    ppermute x1, starting transfers between devices, per_device(): p_back = lax.ppermute(p_max, axes, backwards(ring))  1.62 us
    ppermute x1, starting transfers between devices, per_device(): p1 = lax.ppermute(own1, axes, ring)  1.49 us
  transfers between devices with their start and end apart: 10, of which 4 were waited for; matrix products, arithmetic and copies ran while one was open for 0% of the time, Pallas kernels for 32%

profile of v3, /device:TPU:0, one launch (start us, length us, event | category | flops | bytes accessed | tf_op | source)
XLA Modules:
  0.0 36.1 jit_solution(3576940463098581546)
XLA Ops:
  0.0 0.0 copy-start
  0.0 1.0 %copy-done = bf16[2048,128]{1,0:T(8,128)(2,1)S(1)} copy-done((bf16[2048,128]{1,0:T(8,128)(2,1)S(1)}, bf16[2048,128]{1,0:T(8,128)(2,1)}, u32[]{:S(2)}) %copy-start) | copy-done | bytes 524312
  1.0 0.0 copy-start.1
  1.0 0.7 %copy-done.1 = s32[2048]{0:T(1024)S(1)} copy-done((s32[2048]{0:T(1024)S(1)}, s32[2048]{0:T(1024)}, u32[]{:S(2)}) %copy-start.1) | copy-done | bytes 8216
  1.7 0.1 pack.1
  1.8 3.0 %collective-permute-start.3 = (bf16[2064,128]{1,0:T(8,128)(2,1)S(1)}, bf16[2064,128]{1,0:T(8,128)(2,1)S(1)}, u32[]{:S(2)}, u32[]{:S(2)}) collective-permute-start(bf16[2064,128]{1,0:T(8,128)(2,1)S(1)} %get-tuple-element.28.own), channel_id=1, source_target_pairs={{0,2},{1,3},{2,18},{3,19},{4,6},{5,7},{6,22},{7,23},{8,10},{9,11},... | collective-permute-start | bytes 1585160 | tf_op jit(solution)/shard_map/ppermute | solution.py:125
  4.8 1.5 %collective-permute-start.2 = (bf16[1296,128]{1,0:T(8,128)(2,1)S(1)}, bf16[1296,128]{1,0:T(8,128)(2,1)S(1)}, u32[]{:S(2)}, u32[]{:S(2)}) collective-permute-start(bf16[1296,128]{1,0:T(8,128)(2,1)S(1)} %get-tuple-element.26), channel_id=1, source_target_pairs={{0,1},{1,2},{2,3},{3,0},{4,5},{5,6},{6,7},{7,4},{8,9},{9,10},{10,1... | collective-permute-start | bytes 995336 | tf_op jit(solution)/shard_map/ppermute | solution.py:123
  6.3 3.6 %collective-permute-start = (bf16[1296,128]{1,0:T(8,128)(2,1)S(1)}, bf16[1296,128]{1,0:T(8,128)(2,1)S(1)}, u32[]{:S(2)}, u32[]{:S(2)}) collective-permute-start(bf16[1296,128]{1,0:T(8,128)(2,1)S(1)} %get-tuple-element.26), channel_id=1, source_target_pairs={{0,12},{1,5},{2,6},{3,7},{4,0},{5,9},{6,10},{7,11},{8,4},{9,13},{1... | collective-permute-start | bytes 995336 | tf_op jit(solution)/shard_map/ppermute | solution.py:124
  9.9 0.4 %collective-permute-start.1 = (bf16[768,128]{1,0:T(8,128)(2,1)S(1)}, bf16[768,128]{1,0:T(8,128)(2,1)S(1)}, u32[]{:S(2)}, u32[]{:S(2)}) collective-permute-start(bf16[768,128]{1,0:T(8,128)(2,1)S(1)} %get-tuple-element.27), channel_id=1, source_target_pairs={{0,12},{1,5},{2,6},{3,7},{4,0},{5,9},{6,10},{7,11},{8,4},{9,13},{1... | collective-permute-start | bytes 589832 | tf_op jit(solution)/shard_map/ppermute | solution.py:127
  10.3 0.0 collective-permute-start.4
  10.3 0.2 own_marks.1.own_m
  10.6 5.1 %collective-permute-done.2.p1 = bf16[1296,128]{1,0:T(8,128)(2,1)S(1)} collective-permute-done((bf16[1296,128]{1,0:T(8,128)(2,1)S(1)}, bf16[1296,128]{1,0:T(8,128)(2,1)S(1)}, u32[]{:S(2)}, u32[]{:S(2)}) %collective-permute-start.2) | collective-permute-done | bytes 331808 | tf_op jit(solution)/shard_map/ppermute | solution.py:123
  15.6 1.8 %ring1.1 = (bf16[2048,128]{1,0:T(8,128)(2,1)S(1)}, f32[16,128]{1,0:T(8,128)S(1)}, f32[10,128]{1,0:T(8,128)S(1)}) custom-call(bf16[2064,128]{1,0:T(8,128)(2,1)S(1)} %get-tuple-element.28.own, bf16[2048,128]{1,0:T(8,128)(2,1)S(1)} %own_marks.1.own_m, bf16[1296,128]{1,0:T(8,128)(2,1)S(1)} %collective-permute-done.2.p1), custom_call_target="tpu_custom_call" | custom-call | bytes 1922048 | tf_op jit(solution)/shard_map/ring1/pallas_call | solution.py:49
  17.4 0.8 %collective-permute-done.z1 = bf16[1296,128]{1,0:T(8,128)(2,1)S(1)} collective-permute-done((bf16[1296,128]{1,0:T(8,128)(2,1)S(1)}, bf16[1296,128]{1,0:T(8,128)(2,1)S(1)}, u32[]{:S(2)}, u32[]{:S(2)}) %collective-permute-start) | collective-permute-done | bytes 331808 | tf_op jit(solution)/shard_map/ppermute | solution.py:124
  18.1 2.7 %layer1.1 = (bf16[2048,128]{1,0:T(8,128)(2,1)S(1)}, f32[16,128]{1,0:T(8,128)S(1)}, f32[10,128]{1,0:T(8,128)S(1)}, f32[10,128]{1,0:T(8,128)S(1)}) custom-call(bf16[2064,128]{1,0:T(8,128)(2,1)S(1)} %get-tuple-element.28.own, bf16[2048,128]{1,0:T(8,128)(2,1)S(1)} %own_marks.1.own_m, bf16[1296,128]{1,0:T(8,128)(2,1)S(1)} %collective-permute-done.2.p1, ...), custom_call_target="tpu_custom_call" | custom-call | bytes 2796544 | tf_op jit(solution)/shard_map/layer1/pallas_call | solution.py:49
  20.8 0.0 collective-permute-done.1.z2
  20.8 0.0 collective-permute-done.4.p2
  20.8 1.7 %second.1 = (f32[16,128]{1,0:T(8,128)S(1)}, f32[16,128]{1,0:T(8,128)S(1)}) custom-call(bf16[1296,128]{1,0:T(8,128)(2,1)S(1)} %collective-permute-done.2.p1, bf16[768,128]{1,0:T(8,128)(2,1)S(1)} %collective-permute-done.4.p2, bf16[2048,128]{1,0:T(8,128)(2,1)S(1)} %get-tuple-element.29.p_m, bf16[1296,128]{1,0:T(8,128)(2,1)S(1)} %collective-permute-done.z1, ...), custom_call_target="tpu_custom_call" | custom-call | bytes 2131968 | tf_op jit(solution)/shard_map/second/pallas_call | solution.py:49
  22.5 0.0 collective-permute-done.3.q
  22.5 0.1 collective-permute-start.5
  22.6 1.1 %ring2.1 = (f32[16,128]{1,0:T(8,128)S(1)}, f32[64,128]{1,0:T(8,128)S(1)}) custom-call(bf16[2064,128]{1,0:T(8,128)(2,1)S(1)} %get-tuple-element.28.own, bf16[2048,128]{1,0:T(8,128)(2,1)S(1)} %own_marks.1.own_m, bf16[768,128]{1,0:T(8,128)(2,1)S(1)} %collective-permute-done.4.p2, bf16[2048,128]{1,0:T(8,128)(2,1)S(1)} %get-tuple-element.29.p_m, ...), custom_call_target="tpu_custom_call" | custom-call | bytes 1830912 | tf_op jit(solution)/shard_map/ring2/pallas_call | solution.py:49
  23.8 1.6 %collective-permute-start.7 = (f32[64,128]{1,0:T(8,128)S(1)}, f32[64,128]{1,0:T(8,128)S(1)}, u32[]{:S(2)}, u32[]{:S(2)}) collective-permute-start(f32[64,128]{1,0:T(8,128)S(1)} %get-tuple-element.39.after), channel_id=1, source_target_pairs={{1,0},{2,1},{3,2},{0,3},{5,4},{6,5},{7,6},{4,7},{9,8},{10,9},{11,1... | collective-permute-start | bytes 98312 | tf_op jit(solution)/shard_map/ppermute | solution.py:172
  25.4 0.0 collective-permute-done.5.r
  25.4 3.0 %pairs.1 = (f32[16,128]{1,0:T(8,128)S(1)}, f32[32,128]{1,0:T(8,128)S(1)}) custom-call(s32[1]{0:T(128)} %bitcast.has, bf16[1296,128]{1,0:T(8,128)(2,1)S(1)} %collective-permute-done.z1, bf16[768,128]{1,0:T(8,128)(2,1)S(1)} %collective-permute-done.1.z2, bf16[2048,128]{1,0:T(8,128)(2,1)S(1)} %get-tuple-element.32.z_m, ...), custom_call_target="tpu_custom_call" | custom-call | bytes 2174980 | tf_op jit(solution)/shard_map/pairs/pallas_call | solution.py:49
  28.4 0.1 collective-permute-start.6
  28.5 1.1 %layer2.1 = (f32[16,128]{1,0:T(8,128)S(1)}, f32[16,128]{1,0:T(8,128)S(1)}) custom-call(bf16[2064,128]{1,0:T(8,128)(2,1)S(1)} %get-tuple-element.28.own, bf16[2048,128]{1,0:T(8,128)(2,1)S(1)} %own_marks.1.own_m, bf16[768,128]{1,0:T(8,128)(2,1)S(1)} %collective-permute-done.1.z2, bf16[2048,128]{1,0:T(8,128)(2,1)S(1)} %get-tuple-element.32.z_m, ...), custom_call_target="tpu_custom_call" | custom-call | bytes 1806336 | tf_op jit(solution)/shard_map/layer2/pallas_call | solution.py:49
  29.6 0.9 %collective-permute-start.8 = (f32[16,128]{1,0:T(8,128)S(1)}, f32[16,128]{1,0:T(8,128)S(1)}, u32[]{:S(2)}, u32[]{:S(2)}) collective-permute-start(f32[16,128]{1,0:T(8,128)S(1)} %get-tuple-element.45), channel_id=1, source_target_pairs={{12,0},{5,1},{6,2},{7,3},{0,4},{9,5},{10,6},{11,7},{4,8},{13,9},{1... | collective-permute-start | bytes 24584 | tf_op jit(solution)/shard_map/ppermute | solution.py:207
  30.5 0.0 collective-permute-done.7.p_back
  30.5 0.0 collective-permute-done.6.theirs
  30.5 0.0 copy-start.2
  30.5 0.0 collective-permute-start.9
  30.5 4.6 %collective-permute-done.8 = f32[16,128]{1,0:T(8,128)S(1)} collective-permute-done((f32[16,128]{1,0:T(8,128)S(1)}, f32[16,128]{1,0:T(8,128)S(1)}, u32[]{:S(2)}, u32[]{:S(2)}) %collective-permute-start.8) | collective-permute-done | bytes 8224 | tf_op jit(solution)/shard_map/ppermute | solution.py:207
  35.1 0.4 collective-permute-done.9
  35.5 0.0 copy-done.2
  35.5 0.6 %bitcast_maximum_fusion = f32[2048]{0:T(1024)} fusion(f32[2048]{0:T(1024)S(1)} %copy-done.2, f32[16,128]{1,0:T(8,128)S(1)} %collective-permute-done.9, f32[16,128]{1,0:T(8,128)S(1)} %get-tuple-element.44, f32[16,128]{1,0:T(8,128)S(1)} %collective-permute-done.8, pred[]{:T(512)} %bitcast.2), kind=kLoop, calls=%fused_computation | loop fusion | flops 8192 | bytes 40961 | tf_op jit(solution)/shard_map/max | solution.py:220
  (1 shorter events, 0.0 us)
Async XLA Ops:
  0.0 1.0 %copy-start = (bf16[2048,128]{1,0:T(8,128)(2,1)S(1)}, bf16[2048,128]{1,0:T(8,128)(2,1)}, u32[]{:S(2)}) copy-start(bf16[2048,128]{1,0:T(8,128)(2,1)} %vec.1) | copy-start | bytes 1572868
  1.0 0.7 %copy-start.1 = (s32[2048]{0:T(1024)S(1)}, s32[2048]{0:T(1024)}, u32[]{:S(2)}) copy-start(s32[2048]{0:T(1024)} %param.4) | copy-start | bytes 24580
  1.8 20.7 %collective-permute-start.3 = (bf16[2064,128]{1,0:T(8,128)(2,1)S(1)}, bf16[2064,128]{1,0:T(8,128)(2,1)S(1)}, u32[]{:S(2)}, u32[]{:S(2)}) collective-permute-start(bf16[2064,128]{1,0:T(8,128)(2,1)S(1)} %get-tuple-element.28.own), channel_id=1, source_target_pairs={{0,2},{1,3},{2,18},{3,19},{4,6},{5,7},{6,22},{7,23},{8,10},{9,11},... | collective-permute-start | bytes 1585160 | tf_op jit(solution)/shard_map/ppermute | solution.py:125
  4.8 10.8 %collective-permute-start.2 = (bf16[1296,128]{1,0:T(8,128)(2,1)S(1)}, bf16[1296,128]{1,0:T(8,128)(2,1)S(1)}, u32[]{:S(2)}, u32[]{:S(2)}) collective-permute-start(bf16[1296,128]{1,0:T(8,128)(2,1)S(1)} %get-tuple-element.26), channel_id=1, source_target_pairs={{0,1},{1,2},{2,3},{3,0},{4,5},{5,6},{6,7},{7,4},{8,9},{9,10},{10,1... | collective-permute-start | bytes 995336 | tf_op jit(solution)/shard_map/ppermute | solution.py:123
  6.3 11.9 %collective-permute-start = (bf16[1296,128]{1,0:T(8,128)(2,1)S(1)}, bf16[1296,128]{1,0:T(8,128)(2,1)S(1)}, u32[]{:S(2)}, u32[]{:S(2)}) collective-permute-start(bf16[1296,128]{1,0:T(8,128)(2,1)S(1)} %get-tuple-element.26), channel_id=1, source_target_pairs={{0,12},{1,5},{2,6},{3,7},{4,0},{5,9},{6,10},{7,11},{8,4},{9,13},{1... | collective-permute-start | bytes 995336 | tf_op jit(solution)/shard_map/ppermute | solution.py:124
  9.9 10.9 %collective-permute-start.1 = (bf16[768,128]{1,0:T(8,128)(2,1)S(1)}, bf16[768,128]{1,0:T(8,128)(2,1)S(1)}, u32[]{:S(2)}, u32[]{:S(2)}) collective-permute-start(bf16[768,128]{1,0:T(8,128)(2,1)S(1)} %get-tuple-element.27), channel_id=1, source_target_pairs={{0,12},{1,5},{2,6},{3,7},{4,0},{5,9},{6,10},{7,11},{8,4},{9,13},{1... | collective-permute-start | bytes 589832 | tf_op jit(solution)/shard_map/ppermute | solution.py:127
  10.3 10.5 %collective-permute-start.4 = (bf16[768,128]{1,0:T(8,128)(2,1)S(1)}, bf16[768,128]{1,0:T(8,128)(2,1)S(1)}, u32[]{:S(2)}, u32[]{:S(2)}) collective-permute-start(bf16[768,128]{1,0:T(8,128)(2,1)S(1)} %get-tuple-element.27), channel_id=1, source_target_pairs={{0,1},{1,2},{2,3},{3,0},{4,5},{5,6},{6,7},{7,4},{8,9},{9,10},{10,1... | collective-permute-start | bytes 589832 | tf_op jit(solution)/shard_map/ppermute | solution.py:126
  22.5 2.8 %collective-permute-start.5 = (bf16[2064,128]{1,0:T(8,128)(2,1)S(1)}, bf16[2064,128]{1,0:T(8,128)(2,1)S(1)}, u32[]{:S(2)}, u32[]{:S(2)}) collective-permute-start(bf16[2064,128]{1,0:T(8,128)(2,1)S(1)} %collective-permute-done.3.q), channel_id=1, source_target_pairs={{0,16},{1,17},{2,18},{3,19},{4,20},{5,21},{6,22},{7,23},{8,24},{9,... | collective-permute-start | bytes 1585160 | tf_op jit(solution)/shard_map/ppermute | solution.py:160
  23.8 6.7 %collective-permute-start.7 = (f32[64,128]{1,0:T(8,128)S(1)}, f32[64,128]{1,0:T(8,128)S(1)}, u32[]{:S(2)}, u32[]{:S(2)}) collective-permute-start(f32[64,128]{1,0:T(8,128)S(1)} %get-tuple-element.39.after), channel_id=1, source_target_pairs={{1,0},{2,1},{3,2},{0,3},{5,4},{6,5},{7,6},{4,7},{9,8},{10,9},{11,1... | collective-permute-start | bytes 98312 | tf_op jit(solution)/shard_map/ppermute | solution.py:172
  28.4 2.1 %collective-permute-start.6 = (f32[32,128]{1,0:T(8,128)S(1)}, f32[32,128]{1,0:T(8,128)S(1)}, u32[]{:S(2)}, u32[]{:S(2)}) collective-permute-start(f32[32,128]{1,0:T(8,128)S(1)} %get-tuple-element.40.mine), channel_id=1, source_target_pairs={{0,16},{1,17},{2,18},{3,19},{4,20},{5,21},{6,22},{7,23},{8,24},{9,... | collective-permute-start | bytes 49160 | tf_op jit(solution)/shard_map/ppermute | solution.py:198
  29.6 5.5 %collective-permute-start.8 = (f32[16,128]{1,0:T(8,128)S(1)}, f32[16,128]{1,0:T(8,128)S(1)}, u32[]{:S(2)}, u32[]{:S(2)}) collective-permute-start(f32[16,128]{1,0:T(8,128)S(1)} %get-tuple-element.45), channel_id=1, source_target_pairs={{12,0},{5,1},{6,2},{7,3},{0,4},{9,5},{10,6},{11,7},{4,8},{13,9},{1... | collective-permute-start | bytes 24584 | tf_op jit(solution)/shard_map/ppermute | solution.py:207
  30.5 5.0 %copy-start.2 = (f32[2048]{0:T(1024)S(1)}, f32[2048]{0:T(1024)}, u32[]{:S(2)}) copy-start(f32[2048]{0:T(1024)} %param.5) | copy-start | bytes 24580
  30.5 5.0 %collective-permute-start.9 = (f32[16,128]{1,0:T(8,128)S(1)}, f32[16,128]{1,0:T(8,128)S(1)}, u32[]{:S(2)}, u32[]{:S(2)}) collective-permute-start(f32[16,128]{1,0:T(8,128)S(1)} %get-tuple-element.46), channel_id=1, source_target_pairs={{2,0},{3,1},{18,2},{19,3},{6,4},{7,5},{22,6},{23,7},{10,8},{11,9},... | collective-permute-start | bytes 24584 | tf_op jit(solution)/shard_map/ppermute | solution.py:217

commit v4 on v3

--- a/solution.py
+++ b/solution.py
@@ -11,7 +11,7 @@
 NEG = -1e30
 MARK = 2.0**50
 LANES = 128
-ROWS = 256
+ROWS = 512
 VMEM = 24 * 2**20
 F32 = jnp.float32
 BF16 = jnp.bfloat16
@@ -70,15 +70,18 @@
     columns = wide.shape[0]
     colmax, rowmax = None, []
     for left, left_marks in lefts:
-        for start in range(0, left.shape[0], ROWS):
-            here = slice(start, start + ROWS)
+        count = left.shape[0] // LANES
+        pieces = -(-count * LANES // ROWS)
+        for piece in range(pieces):
+            here = slice(piece * count // pieces * LANES, (piece + 1) * count // pieces * LANES)
+            size = here.stop - here.start
             tall = jnp.concatenate([left[here], left_marks[here]], axis=1)
             scores = lax.dot_general(tall, wide, (((1,), (1,)), ((), ())), preferred_element_type=F32)
             best = scores[:, :LANES]
             for lane in range(LANES, columns, LANES):
                 best = jnp.maximum(best, scores[:, lane : lane + LANES])
-            rowmax.append(jnp.max(best.reshape(ROWS // LANES, LANES, LANES), axis=2))
-            over = jnp.max(scores.reshape(ROWS // 8, 8, columns), axis=0)
+            rowmax.append(jnp.max(best.reshape(size // LANES, LANES, LANES), axis=2))
+            over = jnp.max(scores.reshape(size // 8, 8, columns), axis=0)
             colmax = over if colmax is None else jnp.maximum(colmax, over)
     return jnp.concatenate(rowmax, axis=0), jnp.max(colmax, axis=0).reshape(columns // LANES, LANES)
 
@@ -109,7 +112,9 @@
     block = lax.axis_index("corpus")
     block = jnp.where(lax.axis_index("slab") % 2 == 1, count - 1 - block, block)
     has_pair = (block % ROUNDS >= 2).astype(jnp.int32).reshape(1)
+    far = jnp.where(block % ROUNDS == 0, block == count - ROUNDS, block < ROUNDS).astype(jnp.int32).reshape(1)
     marks = struct(tokens, LANES, dtype=BF16)
+    marks1, marks2 = struct(head, LANES, dtype=BF16), struct(tokens - head, LANES, dtype=BF16)
     smem = pl.BlockSpec(memory_space=pltpu.SMEM)
     vmem = pl.BlockSpec(memory_space=pltpu.VMEM)
     whole, piece1, piece2 = struct(lines, LANES), struct(part, LANES), struct(rest, LANES)
@@ -131,92 +136,114 @@
 
     (own_m,) = call("own_marks", own_marks, [own], [marks])
 
-    def ring1(own, own_m, p1, p_m, own_out, p_out):
-        mark(p1[head:], p_m, MARK)
-        p_out[...], own_out[...] = tile([(p1[:head], p_m[:head])], [(own[:tokens], own_m[...])])
-
-    p_m, own_max, p1_max = call("ring1", ring1, [own, own_m, p1], [marks, whole, piece1])
-
-    def layer1(own, own_m, p1, p_m, z1, own_max, p_max, z_m, own_out, p_out, z_out):
-        mark(z1[head:], z_m, MARK)
-        row, col = tile([(z1[:head], z_m[:head])], [(own[:tokens], own_m[...]), (p1[:head], -p_m[:head])])
+    def ring1(own, own_m, p1, p_m1, p_m2, own_out, p_out):
+        mark(p1[head : head + part], p_m1, MARK)
+        mark(p1[head + part :], p_m2, MARK)
+        p_out[...], own_out[...] = tile([(p1[:head], p_m1[...])], [(own[:tokens], own_m[...])])
+
+    p_m1, p_m2, own_max, p1_max = call("ring1", ring1, [own, own_m, p1], [marks1, marks2, whole, piece1])
+
+    def layer1(own, own_m, p1, p_m1, z1, own_max, p_max, z_m1, z_m2, own_out, p_out, z_out):
+        mark(z1[head : head + part], z_m1, MARK)
+        mark(z1[head + part :], z_m2, MARK)
+        row, col = tile([(z1[:head], z_m1[...])], [(own[:tokens], own_m[...]), (p1[:head], -p_m1[...])])
         own_out[...] = jnp.maximum(own_max[...], col[:lines])
         p_out[...] = jnp.maximum(p_max[...], col[lines:])
         z_out[...] = row
 
-    z_m, own_max, p1_max, z1_max = call(
-        "layer1", layer1, [own, own_m, p1, p_m, z1, own_max, p1_max], [marks, whole, piece1, piece1]
-    )
-
-    def second(p1, p2, p_m, z1, z2, z_m, z1_max, p1_max, z_out, p_out):
-        row1, col1 = tile([(z2[...], -z_m[head:])], [(p1[:head], p_m[:head]), (p2[...], p_m[head:])])
-        row2, col2 = tile([(p2[...], -p_m[head:])], [(z1[:head], z_m[:head])])
+    z_m1, z_m2, own_max, p1_max, z1_max = call(
+        "layer1",
+        layer1,
+        [own, own_m, p1, p_m1, z1, own_max, p1_max],
+        [marks1, marks2, whole, piece1, piece1],
+    )
+
+    def second(p1, p_m1, p2, p_m2, z1, z_m1, z2, z_m2, z1_max, p1_max, z_out, p_out):
+        row1, col1 = tile([(z2[...], -z_m2[...])], [(p1[:head], p_m1[...]), (p2[...], p_m2[...])])
+        row2, col2 = tile([(p2[...], -p_m2[...])], [(z1[:head], z_m1[...])])
         z_out[:part] = jnp.maximum(z1_max[...], col2)
         z_out[part:] = row1
         p_out[:part] = jnp.maximum(p1_max[...], col1[:part])
         p_out[part:] = jnp.maximum(col1[part:], row2)
 
-    z_max, p_max = call("second", second, [p1, p2, p_m, z1, z2, z_m, z1_max, p1_max], [whole, whole])
+    z_max, p_max = call(
+        "second", second, [p1, p_m1, p2, p_m2, z1, z_m1, z2, z_m2, z1_max, p1_max], [whole, whole]
+    )
     r = lax.ppermute(after(q, z_max), axes, beside)
 
-    def ring2(own, own_m, p2, p_m, own_max, p_max, own_out, p_out):
-        row, col = tile([(p2[...], p_m[head:])], [(own[:tokens], own_m[...])])
+    def layer2(own, own_m, z2, z_m2, own_max, z_max, own_out, z_out):
+        row, col = tile([(z2[...], z_m2[...])], [(own[:tokens], own_m[...])])
         own_out[...] = jnp.maximum(own_max[...], col)
-        p_out[:part] = p_max[:part]
-        p_out[part:lines] = jnp.maximum(p_max[part:], row)
-        p_out[lines:] = jnp.full((3 * lines, LANES), NEG, F32)
-
-    own_max, p_max = call(
-        "ring2", ring2, [own, own_m, p2, p_m, own_max, p_max], [whole, struct(4 * lines, LANES)]
-    )
-    p_back = lax.ppermute(p_max, axes, backwards(ring))
-
-    def pairs(has, z1, z2, z_m, q, r, z_max, after, z_out, out, q_m, r_m):
+        z_out[:part] = z_max[:part]
+        z_out[part:] = jnp.maximum(z_max[part:], row)
+
+    own_max, z_max = call("layer2", layer2, [own, own_m, z2, z_m2, own_max, z_max], [whole, whole])
+
+    def pairs(has, z1, z2, q, r, z_max, z_out, out, q_m, other_m):
         mark(q[tokens:], q_m, MARK)
+        z_out[lines:] = jnp.full((3 * lines, LANES), NEG, F32)
 
         @pl.when(has[0] > 0)
         def _():
-            row, col = tile([(z1[:head], -z_m[:head]), (z2[...], -z_m[head:])], [(q[:tokens], q_m[...])])
-            z_out[...] = jnp.maximum(z_max[...], row)
+            mark(z1[head:], other_m, -MARK)
+            row, col = tile([(z1[:head], other_m[:head]), (z2[...], other_m[head:])], [(q[:tokens], q_m[...])])
+            z_out[:lines] = jnp.maximum(z_max[...], row)
             out[:lines] = jnp.full((lines, LANES), NEG, F32)
             out[lines:] = col
 
         @pl.when(has[0] == 0)
         def _():
-            mark(r[tokens:], r_m, -MARK)
-            z_out[...] = z_max[...]
-            out[:lines], out[lines:] = tile([(q[:tokens], q_m[...])], [(r[:tokens], r_m[...])])
+            mark(r[tokens:], other_m, -MARK)
+            z_out[:lines] = z_max[...]
+            out[:lines], out[lines:] = tile([(q[:tokens], q_m[...])], [(r[:tokens], other_m[...])])
 
     z_max, mine = call(
         "pairs",
         pairs,
-        [has_pair, z1, z2, z_m, q, r, z_max, p_max],
-        [whole, struct(2 * lines, LANES)],
-        specs=[smem] + [vmem] * 7,
+        [has_pair, z1, z2, q, r, z_max],
+        [struct(4 * lines, LANES), struct(2 * lines, LANES)],
+        specs=[smem] + [vmem] * 5,
         scratch=[pltpu.VMEM((tokens, LANES), BF16)] * 2,
     )
     theirs = lax.ppermute(mine, axes, beside)
 
-    def layer2(own, own_m, z2, z_m, own_max, z_max, own_out, z_out):
-        row, col = tile([(z2[...], z_m[head:])], [(own[:tokens], own_m[...])])
-        own_out[...] = jnp.maximum(own_max[...], col)
-        z_out[:part] = z_max[:part]
-        z_out[part:] = jnp.maximum(z_max[part:], row)
-
-    own_max, z_max = call("layer2", layer2, [own, own_m, z2, z_m, own_max, z_max], [whole, whole])
-    z_back = lax.ppermute(z_max, axes, backwards(layer))
-
-    def merge(has, mine, theirs, own_max, p_back, own_out, q_out):
+    def ring2(wanted, far, own, own_m, p2, p_m2, own_max, p_max, own_out, p_out):
+        @pl.when(far[0] == wanted)
+        def _():
+            row, col = tile([(p2[...], p_m2[...])], [(own[:tokens], own_m[...])])
+            own_out[...] = jnp.maximum(own_max[...], col)
+            p_out[:part] = p_max[:part]
+            p_out[part:] = jnp.maximum(p_max[part:], row)
+
+        @pl.when(far[0] != wanted)
+        def _():
+            own_out[...] = own_max[...]
+            p_out[...] = p_max[...]
+
+    p_max = after(p_max, mine)
+    for wanted in (1, 0):
+        own_max, p_max = call(
+            "ring2",
+            functools.partial(ring2, wanted),
+            [far, own, own_m, p2, p_m2, own_max, p_max],
+            [whole, whole],
+            specs=[smem] + [vmem] * 6,
+        )
+        if wanted:
+            z_back = lax.ppermute(after(z_max, p_max), axes, backwards(layer))
+    p_back = lax.ppermute(p_max, axes, backwards(ring))
+
+    def merge(has, mine, theirs, own_max, own_out, q_out):
         got = jnp.where(has[0] > 0, theirs[...], F32(NEG))
-        own_out[...] = jnp.maximum(jnp.maximum(own_max[...], p_back[:lines]), got[:lines])
+        own_out[...] = jnp.maximum(own_max[...], got[:lines])
         q_out[...] = jnp.maximum(mine[lines:], got[lines:])
 
     own_max, q_max = call(
-        "merge", merge, [has_pair, mine, theirs, own_max, p_back], [whole, whole], specs=[smem] + [vmem] * 4
+        "merge", merge, [has_pair, mine, theirs, own_max], [whole, whole], specs=[smem] + [vmem] * 3
     )
     q_back = lax.ppermute(q_max, axes, backwards(pair))
     q_back = jnp.where(has_pair > 0, NEG, q_back)
-    best = jnp.maximum(jnp.maximum(own_max, z_back), q_back)
+    best = jnp.maximum(jnp.maximum(own_max, z_back[:lines]), jnp.maximum(p_back, q_back))
     return jnp.maximum(prior, best.reshape(tokens))
 
 

time: 36.3 us -> 35.7 us (0.983)
  waiting for transfers between devices: 10.8 us -> 8.31 us
  starting transfers between devices: 11.2 us -> 13.2 us
    ppermute x1, waiting for transfers between devices: 4.57 us -> 0.01 us  [per_device(): z_back = lax.ppermute(after(z_max, p_max), axes, backwards(layer))]
    ppermute x1, starting transfers between devices: 0.02 us -> 2.05 us  [per_device(): q_back = lax.ppermute(q_max, axes, backwards(pair))]
    ppermute x1, waiting for transfers between devices: 0.36 us -> 1.42 us  [per_device(): q_back = lax.ppermute(q_max, axes, backwards(pair))]
    ppermute x1, waiting for transfers between devices: 0.01 us -> 0.75 us  [per_device(): r = lax.ppermute(after(q, z_max), axes, beside)]
    pallas_call x9 -> x10, Pallas kernels: 11.7 us -> 11.5 us  [call(): pl.pallas_call(kernel, out_shape=outs, in_specs=specs or [pl.BlockSpec(me...]
  transfers between devices with their start and end apart: 10 -> 10, of which waited for: 4 -> 5; matrix products, arithmetic and copies ran while one was open for 0% -> 0% of each run, Pallas kernels for 32% -> 24%
where the time goes in v4:
time: 35.7 us; the launch traced here: 35.5 us
  starting transfers between devices  13.2 us (37%)
  Pallas kernels  11.5 us (32%)
  waiting for transfers between devices  8.31 us (23%)
  local copies, waits for them, and re-layouts  1.74 us (5%)
  other arithmetic  0.61 us (2%)
    pallas_call x10, Pallas kernels, call(): pl.pallas_call(kernel, out_shape=outs, in_specs=specs or [pl.BlockSpec(me...  11.5 us
    ppermute x1, waiting for transfers between devices, per_device(): p1 = lax.ppermute(own1, axes, ring)  5.06 us
    ppermute x1, starting transfers between devices, per_device(): z1 = lax.ppermute(own1, axes, layer)  3.6 us
    ppermute x1, starting transfers between devices, per_device(): q = lax.ppermute(own, axes, pair)  2.98 us
    ppermute x1, starting transfers between devices, per_device(): q_back = lax.ppermute(q_max, axes, backwards(pair))  2.05 us
    unnamed x6, local copies, waits for them, and re-layouts  1.74 us
    ppermute x1, starting transfers between devices, per_device(): p1 = lax.ppermute(own1, axes, ring)  1.49 us
    ppermute x1, waiting for transfers between devices, per_device(): q_back = lax.ppermute(q_max, axes, backwards(pair))  1.42 us
  transfers between devices with their start and end apart: 10, of which 5 were waited for; matrix products, arithmetic and copies ran while one was open for 0% of the time, Pallas kernels for 24%

profile of v4, /device:TPU:0, one launch (start us, length us, event | category | flops | bytes accessed | tf_op | source)
XLA Modules:
  0.0 35.5 jit_solution(4422068262882805340)
XLA Ops:
  0.0 0.0 copy-start
  0.0 1.0 %copy-done = bf16[2048,128]{1,0:T(8,128)(2,1)S(1)} copy-done((bf16[2048,128]{1,0:T(8,128)(2,1)S(1)}, bf16[2048,128]{1,0:T(8,128)(2,1)}, u32[]{:S(2)}) %copy-start) | copy-done | bytes 524312
  1.0 0.0 copy-start.1
  1.0 0.7 %copy-done.1 = s32[2048]{0:T(1024)S(1)} copy-done((s32[2048]{0:T(1024)S(1)}, s32[2048]{0:T(1024)}, u32[]{:S(2)}) %copy-start.1) | copy-done | bytes 8216
  1.7 0.1 pack.1
  1.8 3.0 %collective-permute-start.2 = (bf16[2064,128]{1,0:T(8,128)(2,1)S(1)}, bf16[2064,128]{1,0:T(8,128)(2,1)S(1)}, u32[]{:S(2)}, u32[]{:S(2)}) collective-permute-start(bf16[2064,128]{1,0:T(8,128)(2,1)S(1)} %get-tuple-element.34.own), channel_id=1, source_target_pairs={{0,2},{1,3},{2,18},{3,19},{4,6},{5,7},{6,22},{7,23},{8,10},{9,11},... | collective-permute-start | bytes 1585160 | tf_op jit(solution)/shard_map/ppermute | solution.py:130
  4.8 1.5 %collective-permute-start.3 = (bf16[1296,128]{1,0:T(8,128)(2,1)S(1)}, bf16[1296,128]{1,0:T(8,128)(2,1)S(1)}, u32[]{:S(2)}, u32[]{:S(2)}) collective-permute-start(bf16[1296,128]{1,0:T(8,128)(2,1)S(1)} %get-tuple-element.32), channel_id=1, source_target_pairs={{0,1},{1,2},{2,3},{3,0},{4,5},{5,6},{6,7},{7,4},{8,9},{9,10},{10,1... | collective-permute-start | bytes 995336 | tf_op jit(solution)/shard_map/ppermute | solution.py:128
  6.3 3.6 %collective-permute-start = (bf16[1296,128]{1,0:T(8,128)(2,1)S(1)}, bf16[1296,128]{1,0:T(8,128)(2,1)S(1)}, u32[]{:S(2)}, u32[]{:S(2)}) collective-permute-start(bf16[1296,128]{1,0:T(8,128)(2,1)S(1)} %get-tuple-element.32), channel_id=1, source_target_pairs={{0,12},{1,5},{2,6},{3,7},{4,0},{5,9},{6,10},{7,11},{8,4},{9,13},{1... | collective-permute-start | bytes 995336 | tf_op jit(solution)/shard_map/ppermute | solution.py:129
  9.9 0.4 %collective-permute-start.1 = (bf16[768,128]{1,0:T(8,128)(2,1)S(1)}, bf16[768,128]{1,0:T(8,128)(2,1)S(1)}, u32[]{:S(2)}, u32[]{:S(2)}) collective-permute-start(bf16[768,128]{1,0:T(8,128)(2,1)S(1)} %get-tuple-element.33), channel_id=1, source_target_pairs={{0,12},{1,5},{2,6},{3,7},{4,0},{5,9},{6,10},{7,11},{8,4},{9,13},{1... | collective-permute-start | bytes 589832 | tf_op jit(solution)/shard_map/ppermute | solution.py:132
  10.3 0.0 collective-permute-start.4
  10.3 0.2 own_marks.1.own_m
  10.6 5.1 %collective-permute-done.3.p1 = bf16[1296,128]{1,0:T(8,128)(2,1)S(1)} collective-permute-done((bf16[1296,128]{1,0:T(8,128)(2,1)S(1)}, bf16[1296,128]{1,0:T(8,128)(2,1)S(1)}, u32[]{:S(2)}, u32[]{:S(2)}) %collective-permute-start.3) | collective-permute-done | bytes 331808 | tf_op jit(solution)/shard_map/ppermute | solution.py:128
  15.6 1.7 %ring1.1 = (bf16[1280,128]{1,0:T(8,128)(2,1)S(1)}, bf16[768,128]{1,0:T(8,128)(2,1)S(1)}, f32[16,128]{1,0:T(8,128)S(1)}, f32[10,128]{1,0:T(8,128)S(1)}) custom-call(bf16[2064,128]{1,0:T(8,128)(2,1)S(1)} %get-tuple-element.34.own, bf16[2048,128]{1,0:T(8,128)(2,1)S(1)} %own_marks.1.own_m, bf16[1296,128]{1,0:T(8,128)(2,1)S(1)} %collective-permute-done.3.p1), custom_call_target="tpu_custom_call" | custom-call | bytes 1922048 | tf_op jit(solution)/shard_map/ring1/pallas_call | solution.py:49
  17.4 0.8 %collective-permute-done.z1 = bf16[1296,128]{1,0:T(8,128)(2,1)S(1)} collective-permute-done((bf16[1296,128]{1,0:T(8,128)(2,1)S(1)}, bf16[1296,128]{1,0:T(8,128)(2,1)S(1)}, u32[]{:S(2)}, u32[]{:S(2)}) %collective-permute-start) | collective-permute-done | bytes 331808 | tf_op jit(solution)/shard_map/ppermute | solution.py:129
  18.1 2.6 %layer1.1 = (bf16[1280,128]{1,0:T(8,128)(2,1)S(1)}, bf16[768,128]{1,0:T(8,128)(2,1)S(1)}, f32[16,128]{1,0:T(8,128)S(1)}, f32[10,128]{1,0:T(8,128)S(1)}, f32[10,128]{1,0:T(8,128)S(1)}) custom-call(bf16[2064,128]{1,0:T(8,128)(2,1)S(1)} %get-tuple-element.34.own, bf16[2048,128]{1,0:T(8,128)(2,1)S(1)} %own_marks.1.own_m, ...), custom_call_target="tpu_custom_call" | custom-call | bytes 2599936 | tf_op jit(solution)/shard_map/layer1/pallas_call | solution.py:49
  20.7 0.0 collective-permute-done.1.z2
  20.8 0.0 collective-permute-done.4.p2
  20.8 1.7 %second.1 = (f32[16,128]{1,0:T(8,128)S(1)}, f32[16,128]{1,0:T(8,128)S(1)}) custom-call(bf16[1296,128]{1,0:T(8,128)(2,1)S(1)} %collective-permute-done.3.p1, bf16[1280,128]{1,0:T(8,128)(2,1)S(1)} %get-tuple-element.35.p_m1, bf16[768,128]{1,0:T(8,128)(2,1)S(1)} %collective-permute-done.4.p2, bf16[768,128]{1,0:T(8,128)(2,1)S(1)} %get-tuple-element.36.p_m2, ...), custom_call_target="tpu_custom_call" | custom-call | bytes 2131968 | tf_op jit(solution)/shard_map/second/pallas_call | solution.py:49
  22.4 0.0 collective-permute-done.2.q
  22.5 0.1 collective-permute-start.5
  22.6 1.1 %layer2.1 = (f32[16,128]{1,0:T(8,128)S(1)}, f32[16,128]{1,0:T(8,128)S(1)}) custom-call(bf16[2064,128]{1,0:T(8,128)(2,1)S(1)} %get-tuple-element.34.own, bf16[2048,128]{1,0:T(8,128)(2,1)S(1)} %own_marks.1.own_m, bf16[768,128]{1,0:T(8,128)(2,1)S(1)} %collective-permute-done.1.z2, bf16[768,128]{1,0:T(8,128)(2,1)S(1)} %get-tuple-element.40.z_m2, ...), custom_call_target="tpu_custom_call" | custom-call | bytes 1478656 | tf_op jit(solution)/shard_map/layer2/pallas_call | solution.py:49
  23.7 0.8 %collective-permute-done.5.r = bf16[2064,128]{1,0:T(8,128)(2,1)S(1)} collective-permute-done((bf16[2064,128]{1,0:T(8,128)(2,1)S(1)}, bf16[2064,128]{1,0:T(8,128)(2,1)S(1)}, u32[]{:S(2)}, u32[]{:S(2)}) %collective-permute-start.5) | collective-permute-done | bytes 528416 | tf_op jit(solution)/shard_map/ppermute | solution.py:172
  24.4 3.0 %pairs.1 = (f32[64,128]{1,0:T(8,128)S(1)}, f32[32,128]{1,0:T(8,128)S(1)}) custom-call(s32[1]{0:T(128)} %bitcast.has, bf16[1296,128]{1,0:T(8,128)(2,1)S(1)} %collective-permute-done.z1, bf16[768,128]{1,0:T(8,128)(2,1)S(1)} %collective-permute-done.1.z2, bf16[2064,128]{1,0:T(8,128)(2,1)S(1)} %collective-permute-done.2.q, ...), custom_call_target="tpu_custom_call" | custom-call | bytes 1642500 | tf_op jit(solution)/shard_map/pairs/pallas_call | solution.py:49
  27.5 1.2 %collective-permute-start.7 = (f32[64,128]{1,0:T(8,128)S(1)}, f32[64,128]{1,0:T(8,128)S(1)}, u32[]{:S(2)}, u32[]{:S(2)}) collective-permute-start(f32[64,128]{1,0:T(8,128)S(1)} %get-tuple-element.56), channel_id=1, source_target_pairs={{12,0},{5,1},{6,2},{7,3},{0,4},{9,5},{10,6},{11,7},{4,8},{13,9},{1... | collective-permute-start | bytes 98312 | tf_op jit(solution)/shard_map/ppermute | solution.py:233
  28.6 0.0 collective-permute-start.6
  28.6 1.1 %ring2.3 = (f32[16,128]{1,0:T(8,128)S(1)}, f32[16,128]{1,0:T(8,128)S(1)}) custom-call(s32[1]{0:T(128)} %bitcast.2.far, bf16[2064,128]{1,0:T(8,128)(2,1)S(1)} %get-tuple-element.34.own, bf16[2048,128]{1,0:T(8,128)(2,1)S(1)} %own_marks.1.own_m, bf16[768,128]{1,0:T(8,128)(2,1)S(1)} %collective-permute-done.4.p2, bf16[768,128]{1,0:T(8,128)(2,1)S(1)} %get-tuple-element.36.p_m2, ...), custom_call_target="tpu_custom_call" | custom-call | bytes 1478660 | tf_op jit(solution)/shard_map/ring2/pallas_call | solution.py:49
  29.8 1.4 %collective-permute-start.8 = (f32[16,128]{1,0:T(8,128)S(1)}, f32[16,128]{1,0:T(8,128)S(1)}, u32[]{:S(2)}, u32[]{:S(2)}) collective-permute-start(f32[16,128]{1,0:T(8,128)S(1)} %get-tuple-element.57), channel_id=1, source_target_pairs={{1,0},{2,1},{3,2},{0,3},{5,4},{6,5},{7,6},{4,7},{9,8},{10,9},{11,1... | collective-permute-start | bytes 24584 | tf_op jit(solution)/shard_map/ppermute | solution.py:234
  31.1 0.0 collective-permute-done.6.theirs
  31.1 0.0 copy-start.2
  31.1 2.1 %collective-permute-start.9 = (f32[16,128]{1,0:T(8,128)S(1)}, f32[16,128]{1,0:T(8,128)S(1)}, u32[]{:S(2)}, u32[]{:S(2)}) collective-permute-start(f32[16,128]{1,0:T(8,128)S(1)} %get-tuple-element.58), channel_id=1, source_target_pairs={{2,0},{3,1},{18,2},{19,3},{6,4},{7,5},{22,6},{23,7},{10,8},{11,9},... | collective-permute-start | bytes 24584 | tf_op jit(solution)/shard_map/ppermute | solution.py:244
  33.2 0.3 collective-permute-done.8
  33.5 1.4 %collective-permute-done.9 = f32[16,128]{1,0:T(8,128)S(1)} collective-permute-done((f32[16,128]{1,0:T(8,128)S(1)}, f32[16,128]{1,0:T(8,128)S(1)}, u32[]{:S(2)}, u32[]{:S(2)}) %collective-permute-start.9) | collective-permute-done | bytes 8224 | tf_op jit(solution)/shard_map/ppermute | solution.py:244
  34.9 0.0 collective-permute-done.7
  34.9 0.0 copy-done.2
  34.9 0.6 %fusion.2 = f32[2048]{0:T(1024)} fusion(f32[2048]{0:T(1024)S(1)} %copy-done.2, f32[16,128]{1,0:T(8,128)S(1)} %get-tuple-element.54, f32[64,128]{1,0:T(8,128)S(1)} %collective-permute-done.7, f32[16,128]{1,0:T(8,128)S(1)} %collective-permute-done.8, f32[16,128]{1,0:T(8,128)S(1)} %collective-permute-done.9, pred[]{:T(512)} %bitcast.3), kind=kLoop, calls=%fused_computation.3 | loop fusion | flops 10240 | bytes 49153 | tf_op jit(solution)/shard_map/max | solution.py:247
  (2 shorter events, 0.0 us)
Async XLA Ops:
  0.0 1.0 %copy-start = (bf16[2048,128]{1,0:T(8,128)(2,1)S(1)}, bf16[2048,128]{1,0:T(8,128)(2,1)}, u32[]{:S(2)}) copy-start(bf16[2048,128]{1,0:T(8,128)(2,1)} %vec.1) | copy-start | bytes 1572868
  1.0 0.7 %copy-start.1 = (s32[2048]{0:T(1024)S(1)}, s32[2048]{0:T(1024)}, u32[]{:S(2)}) copy-start(s32[2048]{0:T(1024)} %param.4) | copy-start | bytes 24580
  1.8 20.6 %collective-permute-start.2 = (bf16[2064,128]{1,0:T(8,128)(2,1)S(1)}, bf16[2064,128]{1,0:T(8,128)(2,1)S(1)}, u32[]{:S(2)}, u32[]{:S(2)}) collective-permute-start(bf16[2064,128]{1,0:T(8,128)(2,1)S(1)} %get-tuple-element.34.own), channel_id=1, source_target_pairs={{0,2},{1,3},{2,18},{3,19},{4,6},{5,7},{6,22},{7,23},{8,10},{9,11},... | collective-permute-start | bytes 1585160 | tf_op jit(solution)/shard_map/ppermute | solution.py:130
  4.8 10.8 %collective-permute-start.3 = (bf16[1296,128]{1,0:T(8,128)(2,1)S(1)}, bf16[1296,128]{1,0:T(8,128)(2,1)S(1)}, u32[]{:S(2)}, u32[]{:S(2)}) collective-permute-start(bf16[1296,128]{1,0:T(8,128)(2,1)S(1)} %get-tuple-element.32), channel_id=1, source_target_pairs={{0,1},{1,2},{2,3},{3,0},{4,5},{5,6},{6,7},{7,4},{8,9},{9,10},{10,1... | collective-permute-start | bytes 995336 | tf_op jit(solution)/shard_map/ppermute | solution.py:128
  6.3 11.9 %collective-permute-start = (bf16[1296,128]{1,0:T(8,128)(2,1)S(1)}, bf16[1296,128]{1,0:T(8,128)(2,1)S(1)}, u32[]{:S(2)}, u32[]{:S(2)}) collective-permute-start(bf16[1296,128]{1,0:T(8,128)(2,1)S(1)} %get-tuple-element.32), channel_id=1, source_target_pairs={{0,12},{1,5},{2,6},{3,7},{4,0},{5,9},{6,10},{7,11},{8,4},{9,13},{1... | collective-permute-start | bytes 995336 | tf_op jit(solution)/shard_map/ppermute | solution.py:129
  9.9 10.9 %collective-permute-start.1 = (bf16[768,128]{1,0:T(8,128)(2,1)S(1)}, bf16[768,128]{1,0:T(8,128)(2,1)S(1)}, u32[]{:S(2)}, u32[]{:S(2)}) collective-permute-start(bf16[768,128]{1,0:T(8,128)(2,1)S(1)} %get-tuple-element.33), channel_id=1, source_target_pairs={{0,12},{1,5},{2,6},{3,7},{4,0},{5,9},{6,10},{7,11},{8,4},{9,13},{1... | collective-permute-start | bytes 589832 | tf_op jit(solution)/shard_map/ppermute | solution.py:132
  10.3 10.4 %collective-permute-start.4 = (bf16[768,128]{1,0:T(8,128)(2,1)S(1)}, bf16[768,128]{1,0:T(8,128)(2,1)S(1)}, u32[]{:S(2)}, u32[]{:S(2)}) collective-permute-start(bf16[768,128]{1,0:T(8,128)(2,1)S(1)} %get-tuple-element.33), channel_id=1, source_target_pairs={{0,1},{1,2},{2,3},{3,0},{4,5},{5,6},{6,7},{7,4},{8,9},{9,10},{10,1... | collective-permute-start | bytes 589832 | tf_op jit(solution)/shard_map/ppermute | solution.py:131
  22.5 2.0 %collective-permute-start.5 = (bf16[2064,128]{1,0:T(8,128)(2,1)S(1)}, bf16[2064,128]{1,0:T(8,128)(2,1)S(1)}, u32[]{:S(2)}, u32[]{:S(2)}) collective-permute-start(bf16[2064,128]{1,0:T(8,128)(2,1)S(1)} %collective-permute-done.2.q), channel_id=1, source_target_pairs={{0,16},{1,17},{2,18},{3,19},{4,20},{5,21},{6,22},{7,23},{8,24},{9,... | collective-permute-start | bytes 1585160 | tf_op jit(solution)/shard_map/ppermute | solution.py:172
  27.5 7.4 %collective-permute-start.7 = (f32[64,128]{1,0:T(8,128)S(1)}, f32[64,128]{1,0:T(8,128)S(1)}, u32[]{:S(2)}, u32[]{:S(2)}) collective-permute-start(f32[64,128]{1,0:T(8,128)S(1)} %get-tuple-element.56), channel_id=1, source_target_pairs={{12,0},{5,1},{6,2},{7,3},{0,4},{9,5},{10,6},{11,7},{4,8},{13,9},{1... | collective-permute-start | bytes 98312 | tf_op jit(solution)/shard_map/ppermute | solution.py:233
  28.6 2.5 %collective-permute-start.6 = (f32[32,128]{1,0:T(8,128)S(1)}, f32[32,128]{1,0:T(8,128)S(1)}, u32[]{:S(2)}, u32[]{:S(2)}) collective-permute-start(f32[32,128]{1,0:T(8,128)S(1)} %get-tuple-element.47.mine), channel_id=1, source_target_pairs={{0,16},{1,17},{2,18},{3,19},{4,20},{5,21},{6,22},{7,23},{8,24},{9,... | collective-permute-start | bytes 49160 | tf_op jit(solution)/shard_map/ppermute | solution.py:208
  29.8 3.7 %collective-permute-start.8 = (f32[16,128]{1,0:T(8,128)S(1)}, f32[16,128]{1,0:T(8,128)S(1)}, u32[]{:S(2)}, u32[]{:S(2)}) collective-permute-start(f32[16,128]{1,0:T(8,128)S(1)} %get-tuple-element.57), channel_id=1, source_target_pairs={{1,0},{2,1},{3,2},{0,3},{5,4},{6,5},{7,6},{4,7},{9,8},{10,9},{11,1... | collective-permute-start | bytes 24584 | tf_op jit(solution)/shard_map/ppermute | solution.py:234
  31.1 3.8 %copy-start.2 = (f32[2048]{0:T(1024)S(1)}, f32[2048]{0:T(1024)}, u32[]{:S(2)}) copy-start(f32[2048]{0:T(1024)} %param.5) | copy-start | bytes 24580
  31.1 3.7 %collective-permute-start.9 = (f32[16,128]{1,0:T(8,128)S(1)}, f32[16,128]{1,0:T(8,128)S(1)}, u32[]{:S(2)}, u32[]{:S(2)}) collective-permute-start(f32[16,128]{1,0:T(8,128)S(1)} %get-tuple-element.58), channel_id=1, source_target_pairs={{2,0},{3,1},{18,2},{19,3},{6,4},{7,5},{22,6},{23,7},{10,8},{11,9},... | collective-permute-start | bytes 24584 | tf_op jit(solution)/shard_map/ppermute | solution.py:244

commit v5 on v4

--- a/solution.py
+++ b/solution.py
@@ -112,7 +112,8 @@
     block = lax.axis_index("corpus")
     block = jnp.where(lax.axis_index("slab") % 2 == 1, count - 1 - block, block)
     has_pair = (block % ROUNDS >= 2).astype(jnp.int32).reshape(1)
-    far = jnp.where(block % ROUNDS == 0, block == count - ROUNDS, block < ROUNDS).astype(jnp.int32).reshape(1)
+    far = jnp.where(block % ROUNDS == 0, block == count - ROUNDS, block < ROUNDS)
+    far = (far & (lax.axis_index("corpus") < ROUNDS)).astype(jnp.int32).reshape(1)
     marks = struct(tokens, LANES, dtype=BF16)
     marks1, marks2 = struct(head, LANES, dtype=BF16), struct(tokens - head, LANES, dtype=BF16)
     smem = pl.BlockSpec(memory_space=pltpu.SMEM)
@@ -179,8 +180,12 @@
 
     own_max, z_max = call("layer2", layer2, [own, own_m, z2, z_m2, own_max, z_max], [whole, whole])
 
-    def pairs(has, z1, z2, q, r, z_max, z_out, out, q_m, other_m):
-        mark(q[tokens:], q_m, MARK)
+    def q_marks(q, after, out):
+        mark(q[tokens:], out, MARK)
+
+    (q_m,) = call("q_marks", q_marks, [q, own_max], [marks])
+
+    def pairs(has, z1, z2, q, q_m, r, z_max, z_out, out, other_m):
         z_out[lines:] = jnp.full((3 * lines, LANES), NEG, F32)
 
         @pl.when(has[0] > 0)
@@ -200,10 +205,10 @@
     z_max, mine = call(
         "pairs",
         pairs,
-        [has_pair, z1, z2, q, r, z_max],
+        [has_pair, z1, z2, q, q_m, r, z_max],
         [struct(4 * lines, LANES), struct(2 * lines, LANES)],
-        specs=[smem] + [vmem] * 5,
-        scratch=[pltpu.VMEM((tokens, LANES), BF16)] * 2,
+        specs=[smem] + [vmem] * 6,
+        scratch=[pltpu.VMEM((tokens, LANES), BF16)],
     )
     theirs = lax.ppermute(mine, axes, beside)
 

time: 35.7 us -> 35.4 us (level)
    pallas_call x10 -> x11, Pallas kernels: 11.5 us -> 11.4 us  [call(): pl.pallas_call(kernel, out_shape=outs, in_specs=specs or [pl.BlockSpec(me...]
  transfers between devices with their start and end apart: 10 -> 10, of which waited for: 5 -> 5; matrix products, arithmetic and copies ran while one was open for 0% -> 0% of each run, Pallas kernels for 24% -> 25%
where the time goes in v5:
time: 35.4 us; the launch traced here: 35.2 us
  starting transfers between devices  13.2 us (37%)
  Pallas kernels  11.4 us (32%)
  waiting for transfers between devices  8.16 us (23%)
  local copies, waits for them, and re-layouts  1.74 us (5%)
  other arithmetic  0.61 us (2%)
    pallas_call x11, Pallas kernels, call(): pl.pallas_call(kernel, out_shape=outs, in_specs=specs or [pl.BlockSpec(me...  11.4 us
    ppermute x1, waiting for transfers between devices, per_device(): p1 = lax.ppermute(own1, axes, ring)  5.06 us
    ppermute x1, starting transfers between devices, per_device(): z1 = lax.ppermute(own1, axes, layer)  3.6 us
    ppermute x1, starting transfers between devices, per_device(): q = lax.ppermute(own, axes, pair)  2.98 us
    ppermute x1, starting transfers between devices, per_device(): q_back = lax.ppermute(q_max, axes, backwards(pair))  1.9 us
    unnamed x6, local copies, waits for them, and re-layouts  1.74 us
    ppermute x1, starting transfers between devices, per_device(): p1 = lax.ppermute(own1, axes, ring)  1.49 us
    ppermute x1, starting transfers between devices, per_device(): p_back = lax.ppermute(p_max, axes, backwards(ring))  1.49 us
  transfers between devices with their start and end apart: 10, of which 5 were waited for; matrix products, arithmetic and copies ran while one was open for 0% of the time, Pallas kernels for 25%

profile of v5, /device:TPU:0, one launch (start us, length us, event | category | flops | bytes accessed | tf_op | source)
XLA Modules:
  0.0 35.2 jit_solution(12984083687414387052)
XLA Ops:
  0.0 0.0 copy-start
  0.0 1.0 %copy-done = bf16[2048,128]{1,0:T(8,128)(2,1)S(1)} copy-done((bf16[2048,128]{1,0:T(8,128)(2,1)S(1)}, bf16[2048,128]{1,0:T(8,128)(2,1)}, u32[]{:S(2)}) %copy-start) | copy-done | bytes 524312
  1.0 0.0 copy-start.1
  1.0 0.7 %copy-done.1 = s32[2048]{0:T(1024)S(1)} copy-done((s32[2048]{0:T(1024)S(1)}, s32[2048]{0:T(1024)}, u32[]{:S(2)}) %copy-start.1) | copy-done | bytes 8216
  1.7 0.1 pack.1
  1.8 3.0 %collective-permute-start.2 = (bf16[2064,128]{1,0:T(8,128)(2,1)S(1)}, bf16[2064,128]{1,0:T(8,128)(2,1)S(1)}, u32[]{:S(2)}, u32[]{:S(2)}) collective-permute-start(bf16[2064,128]{1,0:T(8,128)(2,1)S(1)} %get-tuple-element.34.own), channel_id=1, source_target_pairs={{0,2},{1,3},{2,18},{3,19},{4,6},{5,7},{6,22},{7,23},{8,10},{9,11},... | collective-permute-start | bytes 1585160 | tf_op jit(solution)/shard_map/ppermute | solution.py:131
  4.8 1.5 %collective-permute-start.3 = (bf16[1296,128]{1,0:T(8,128)(2,1)S(1)}, bf16[1296,128]{1,0:T(8,128)(2,1)S(1)}, u32[]{:S(2)}, u32[]{:S(2)}) collective-permute-start(bf16[1296,128]{1,0:T(8,128)(2,1)S(1)} %get-tuple-element.32), channel_id=1, source_target_pairs={{0,1},{1,2},{2,3},{3,0},{4,5},{5,6},{6,7},{7,4},{8,9},{9,10},{10,1... | collective-permute-start | bytes 995336 | tf_op jit(solution)/shard_map/ppermute | solution.py:129
  6.3 3.6 %collective-permute-start = (bf16[1296,128]{1,0:T(8,128)(2,1)S(1)}, bf16[1296,128]{1,0:T(8,128)(2,1)S(1)}, u32[]{:S(2)}, u32[]{:S(2)}) collective-permute-start(bf16[1296,128]{1,0:T(8,128)(2,1)S(1)} %get-tuple-element.32), channel_id=1, source_target_pairs={{0,12},{1,5},{2,6},{3,7},{4,0},{5,9},{6,10},{7,11},{8,4},{9,13},{1... | collective-permute-start | bytes 995336 | tf_op jit(solution)/shard_map/ppermute | solution.py:130
  9.9 0.4 %collective-permute-start.1 = (bf16[768,128]{1,0:T(8,128)(2,1)S(1)}, bf16[768,128]{1,0:T(8,128)(2,1)S(1)}, u32[]{:S(2)}, u32[]{:S(2)}) collective-permute-start(bf16[768,128]{1,0:T(8,128)(2,1)S(1)} %get-tuple-element.33), channel_id=1, source_target_pairs={{0,12},{1,5},{2,6},{3,7},{4,0},{5,9},{6,10},{7,11},{8,4},{9,13},{1... | collective-permute-start | bytes 589832 | tf_op jit(solution)/shard_map/ppermute | solution.py:133
  10.3 0.0 collective-permute-start.4
  10.3 0.2 own_marks.1.own_m
  10.6 5.1 %collective-permute-done.3.p1 = bf16[1296,128]{1,0:T(8,128)(2,1)S(1)} collective-permute-done((bf16[1296,128]{1,0:T(8,128)(2,1)S(1)}, bf16[1296,128]{1,0:T(8,128)(2,1)S(1)}, u32[]{:S(2)}, u32[]{:S(2)}) %collective-permute-start.3) | collective-permute-done | bytes 331808 | tf_op jit(solution)/shard_map/ppermute | solution.py:129
  15.6 1.7 %ring1.1 = (bf16[1280,128]{1,0:T(8,128)(2,1)S(1)}, bf16[768,128]{1,0:T(8,128)(2,1)S(1)}, f32[16,128]{1,0:T(8,128)S(1)}, f32[10,128]{1,0:T(8,128)S(1)}) custom-call(bf16[2064,128]{1,0:T(8,128)(2,1)S(1)} %get-tuple-element.34.own, bf16[2048,128]{1,0:T(8,128)(2,1)S(1)} %own_marks.1.own_m, bf16[1296,128]{1,0:T(8,128)(2,1)S(1)} %collective-permute-done.3.p1), custom_call_target="tpu_custom_call" | custom-call | bytes 1922048 | tf_op jit(solution)/shard_map/ring1/pallas_call | solution.py:49
  17.4 0.8 %collective-permute-done.z1 = bf16[1296,128]{1,0:T(8,128)(2,1)S(1)} collective-permute-done((bf16[1296,128]{1,0:T(8,128)(2,1)S(1)}, bf16[1296,128]{1,0:T(8,128)(2,1)S(1)}, u32[]{:S(2)}, u32[]{:S(2)}) %collective-permute-start) | collective-permute-done | bytes 331808 | tf_op jit(solution)/shard_map/ppermute | solution.py:130
  18.1 2.6 %layer1.1 = (bf16[1280,128]{1,0:T(8,128)(2,1)S(1)}, bf16[768,128]{1,0:T(8,128)(2,1)S(1)}, f32[16,128]{1,0:T(8,128)S(1)}, f32[10,128]{1,0:T(8,128)S(1)}, f32[10,128]{1,0:T(8,128)S(1)}) custom-call(bf16[2064,128]{1,0:T(8,128)(2,1)S(1)} %get-tuple-element.34.own, bf16[2048,128]{1,0:T(8,128)(2,1)S(1)} %own_marks.1.own_m, ...), custom_call_target="tpu_custom_call" | custom-call | bytes 2599936 | tf_op jit(solution)/shard_map/layer1/pallas_call | solution.py:49
  20.7 0.0 collective-permute-done.1.z2
  20.8 0.0 collective-permute-done.4.p2
  20.8 1.7 %second.1 = (f32[16,128]{1,0:T(8,128)S(1)}, f32[16,128]{1,0:T(8,128)S(1)}) custom-call(bf16[1296,128]{1,0:T(8,128)(2,1)S(1)} %collective-permute-done.3.p1, bf16[1280,128]{1,0:T(8,128)(2,1)S(1)} %get-tuple-element.35.p_m1, bf16[768,128]{1,0:T(8,128)(2,1)S(1)} %collective-permute-done.4.p2, bf16[768,128]{1,0:T(8,128)(2,1)S(1)} %get-tuple-element.40.p_m2, ...), custom_call_target="tpu_custom_call" | custom-call | bytes 2131968 | tf_op jit(solution)/shard_map/second/pallas_call | solution.py:49
  22.5 0.0 collective-permute-done.2.q
  22.5 0.1 collective-permute-start.5
  22.6 1.1 %layer2.1 = (f32[16,128]{1,0:T(8,128)S(1)}, f32[16,128]{1,0:T(8,128)S(1)}) custom-call(bf16[2064,128]{1,0:T(8,128)(2,1)S(1)} %get-tuple-element.34.own, bf16[2048,128]{1,0:T(8,128)(2,1)S(1)} %own_marks.1.own_m, bf16[768,128]{1,0:T(8,128)(2,1)S(1)} %collective-permute-done.1.z2, bf16[768,128]{1,0:T(8,128)(2,1)S(1)} %get-tuple-element.38.z_m2, ...), custom_call_target="tpu_custom_call" | custom-call | bytes 1478656 | tf_op jit(solution)/shard_map/layer2/pallas_call | solution.py:49
  23.7 0.2 q_marks.1.q_m
  23.9 0.5 %collective-permute-done.5.r = bf16[2064,128]{1,0:T(8,128)(2,1)S(1)} collective-permute-done((bf16[2064,128]{1,0:T(8,128)(2,1)S(1)}, bf16[2064,128]{1,0:T(8,128)(2,1)S(1)}, u32[]{:S(2)}, u32[]{:S(2)}) %collective-permute-start.5) | collective-permute-done | bytes 528416 | tf_op jit(solution)/shard_map/ppermute | solution.py:173
  24.5 2.6 %pairs.1 = (f32[64,128]{1,0:T(8,128)S(1)}, f32[32,128]{1,0:T(8,128)S(1)}) custom-call(s32[1]{0:T(128)} %bitcast.has, bf16[1296,128]{1,0:T(8,128)(2,1)S(1)} %collective-permute-done.z1, bf16[768,128]{1,0:T(8,128)(2,1)S(1)} %collective-permute-done.1.z2, bf16[2064,128]{1,0:T(8,128)(2,1)S(1)} %collective-permute-done.2.q, bf16[2048,128]{1,0:T(8,128)(2,1)S(1)} %q_marks.1.q_m, ...), custom_call_target="tpu_custom_call" | custom-call | bytes 2166788 | tf_op jit(solution)/shard_map/pairs/pallas_call | solution.py:49
  27.1 1.2 %collective-permute-start.7 = (f32[64,128]{1,0:T(8,128)S(1)}, f32[64,128]{1,0:T(8,128)S(1)}, u32[]{:S(2)}, u32[]{:S(2)}) collective-permute-start(f32[64,128]{1,0:T(8,128)S(1)} %get-tuple-element.56), channel_id=1, source_target_pairs={{12,0},{5,1},{6,2},{7,3},{0,4},{9,5},{10,6},{11,7},{4,8},{13,9},{1... | collective-permute-start | bytes 98312 | tf_op jit(solution)/shard_map/ppermute | solution.py:238
  28.3 0.0 collective-permute-start.6
  28.3 1.1 %ring2.3 = (f32[16,128]{1,0:T(8,128)S(1)}, f32[16,128]{1,0:T(8,128)S(1)}) custom-call(s32[1]{0:T(128)} %bitcast.2.far, bf16[2064,128]{1,0:T(8,128)(2,1)S(1)} %get-tuple-element.34.own, bf16[2048,128]{1,0:T(8,128)(2,1)S(1)} %own_marks.1.own_m, bf16[768,128]{1,0:T(8,128)(2,1)S(1)} %collective-permute-done.4.p2, bf16[768,128]{1,0:T(8,128)(2,1)S(1)} %get-tuple-element.40.p_m2, ...), custom_call_target="tpu_custom_call" | custom-call | bytes 1478660 | tf_op jit(solution)/shard_map/ring2/pallas_call | solution.py:49
  29.5 1.5 %collective-permute-start.8 = (f32[16,128]{1,0:T(8,128)S(1)}, f32[16,128]{1,0:T(8,128)S(1)}, u32[]{:S(2)}, u32[]{:S(2)}) collective-permute-start(f32[16,128]{1,0:T(8,128)S(1)} %get-tuple-element.57), channel_id=1, source_target_pairs={{1,0},{2,1},{3,2},{0,3},{5,4},{6,5},{7,6},{4,7},{9,8},{10,9},{11,1... | collective-permute-start | bytes 24584 | tf_op jit(solution)/shard_map/ppermute | solution.py:239
  30.9 0.0 collective-permute-done.6.theirs
  30.9 0.0 copy-start.2
  31.0 1.9 %collective-permute-start.9 = (f32[16,128]{1,0:T(8,128)S(1)}, f32[16,128]{1,0:T(8,128)S(1)}, u32[]{:S(2)}, u32[]{:S(2)}) collective-permute-start(f32[16,128]{1,0:T(8,128)S(1)} %get-tuple-element.58), channel_id=1, source_target_pairs={{2,0},{3,1},{18,2},{19,3},{6,4},{7,5},{22,6},{23,7},{10,8},{11,9},... | collective-permute-start | bytes 24584 | tf_op jit(solution)/shard_map/ppermute | solution.py:249
  32.9 0.3 collective-permute-done.8
  33.2 1.5 %collective-permute-done.9 = f32[16,128]{1,0:T(8,128)S(1)} collective-permute-done((f32[16,128]{1,0:T(8,128)S(1)}, f32[16,128]{1,0:T(8,128)S(1)}, u32[]{:S(2)}, u32[]{:S(2)}) %collective-permute-start.9) | collective-permute-done | bytes 8224 | tf_op jit(solution)/shard_map/ppermute | solution.py:249
  34.6 0.0 collective-permute-done.7
  34.6 0.0 copy-done.2
  34.6 0.6 %fusion.2 = f32[2048]{0:T(1024)} fusion(f32[2048]{0:T(1024)S(1)} %copy-done.2, f32[16,128]{1,0:T(8,128)S(1)} %get-tuple-element.54, f32[64,128]{1,0:T(8,128)S(1)} %collective-permute-done.7, f32[16,128]{1,0:T(8,128)S(1)} %collective-permute-done.8, f32[16,128]{1,0:T(8,128)S(1)} %collective-permute-done.9, pred[]{:T(512)} %bitcast.3), kind=kLoop, calls=%fused_computation.3 | loop fusion | flops 10240 | bytes 49153 | tf_op jit(solution)/shard_map/max | solution.py:252
  (2 shorter events, 0.0 us)
Async XLA Ops:
  0.0 1.0 %copy-start = (bf16[2048,128]{1,0:T(8,128)(2,1)S(1)}, bf16[2048,128]{1,0:T(8,128)(2,1)}, u32[]{:S(2)}) copy-start(bf16[2048,128]{1,0:T(8,128)(2,1)} %vec.1) | copy-start | bytes 1572868
  1.0 0.7 %copy-start.1 = (s32[2048]{0:T(1024)S(1)}, s32[2048]{0:T(1024)}, u32[]{:S(2)}) copy-start(s32[2048]{0:T(1024)} %param.4) | copy-start | bytes 24580
  1.8 20.7 %collective-permute-start.2 = (bf16[2064,128]{1,0:T(8,128)(2,1)S(1)}, bf16[2064,128]{1,0:T(8,128)(2,1)S(1)}, u32[]{:S(2)}, u32[]{:S(2)}) collective-permute-start(bf16[2064,128]{1,0:T(8,128)(2,1)S(1)} %get-tuple-element.34.own), channel_id=1, source_target_pairs={{0,2},{1,3},{2,18},{3,19},{4,6},{5,7},{6,22},{7,23},{8,10},{9,11},... | collective-permute-start | bytes 1585160 | tf_op jit(solution)/shard_map/ppermute | solution.py:131
  4.8 10.8 %collective-permute-start.3 = (bf16[1296,128]{1,0:T(8,128)(2,1)S(1)}, bf16[1296,128]{1,0:T(8,128)(2,1)S(1)}, u32[]{:S(2)}, u32[]{:S(2)}) collective-permute-start(bf16[1296,128]{1,0:T(8,128)(2,1)S(1)} %get-tuple-element.32), channel_id=1, source_target_pairs={{0,1},{1,2},{2,3},{3,0},{4,5},{5,6},{6,7},{7,4},{8,9},{9,10},{10,1... | collective-permute-start | bytes 995336 | tf_op jit(solution)/shard_map/ppermute | solution.py:129
  6.3 11.9 %collective-permute-start = (bf16[1296,128]{1,0:T(8,128)(2,1)S(1)}, bf16[1296,128]{1,0:T(8,128)(2,1)S(1)}, u32[]{:S(2)}, u32[]{:S(2)}) collective-permute-start(bf16[1296,128]{1,0:T(8,128)(2,1)S(1)} %get-tuple-element.32), channel_id=1, source_target_pairs={{0,12},{1,5},{2,6},{3,7},{4,0},{5,9},{6,10},{7,11},{8,4},{9,13},{1... | collective-permute-start | bytes 995336 | tf_op jit(solution)/shard_map/ppermute | solution.py:130
  9.9 10.9 %collective-permute-start.1 = (bf16[768,128]{1,0:T(8,128)(2,1)S(1)}, bf16[768,128]{1,0:T(8,128)(2,1)S(1)}, u32[]{:S(2)}, u32[]{:S(2)}) collective-permute-start(bf16[768,128]{1,0:T(8,128)(2,1)S(1)} %get-tuple-element.33), channel_id=1, source_target_pairs={{0,12},{1,5},{2,6},{3,7},{4,0},{5,9},{6,10},{7,11},{8,4},{9,13},{1... | collective-permute-start | bytes 589832 | tf_op jit(solution)/shard_map/ppermute | solution.py:133
  10.3 10.4 %collective-permute-start.4 = (bf16[768,128]{1,0:T(8,128)(2,1)S(1)}, bf16[768,128]{1,0:T(8,128)(2,1)S(1)}, u32[]{:S(2)}, u32[]{:S(2)}) collective-permute-start(bf16[768,128]{1,0:T(8,128)(2,1)S(1)} %get-tuple-element.33), channel_id=1, source_target_pairs={{0,1},{1,2},{2,3},{3,0},{4,5},{5,6},{6,7},{7,4},{8,9},{9,10},{10,1... | collective-permute-start | bytes 589832 | tf_op jit(solution)/shard_map/ppermute | solution.py:132
  22.5 2.0 %collective-permute-start.5 = (bf16[2064,128]{1,0:T(8,128)(2,1)S(1)}, bf16[2064,128]{1,0:T(8,128)(2,1)S(1)}, u32[]{:S(2)}, u32[]{:S(2)}) collective-permute-start(bf16[2064,128]{1,0:T(8,128)(2,1)S(1)} %collective-permute-done.2.q), channel_id=1, source_target_pairs={{0,16},{1,17},{2,18},{3,19},{4,20},{5,21},{6,22},{7,23},{8,24},{9,... | collective-permute-start | bytes 1585160 | tf_op jit(solution)/shard_map/ppermute | solution.py:173
  27.1 7.5 %collective-permute-start.7 = (f32[64,128]{1,0:T(8,128)S(1)}, f32[64,128]{1,0:T(8,128)S(1)}, u32[]{:S(2)}, u32[]{:S(2)}) collective-permute-start(f32[64,128]{1,0:T(8,128)S(1)} %get-tuple-element.56), channel_id=1, source_target_pairs={{12,0},{5,1},{6,2},{7,3},{0,4},{9,5},{10,6},{11,7},{4,8},{13,9},{1... | collective-permute-start | bytes 98312 | tf_op jit(solution)/shard_map/ppermute | solution.py:238
  28.3 2.6 %collective-permute-start.6 = (f32[32,128]{1,0:T(8,128)S(1)}, f32[32,128]{1,0:T(8,128)S(1)}, u32[]{:S(2)}, u32[]{:S(2)}) collective-permute-start(f32[32,128]{1,0:T(8,128)S(1)} %get-tuple-element.48.mine), channel_id=1, source_target_pairs={{0,16},{1,17},{2,18},{3,19},{4,20},{5,21},{6,22},{7,23},{8,24},{9,... | collective-permute-start | bytes 49160 | tf_op jit(solution)/shard_map/ppermute | solution.py:213
  29.5 3.7 %collective-permute-start.8 = (f32[16,128]{1,0:T(8,128)S(1)}, f32[16,128]{1,0:T(8,128)S(1)}, u32[]{:S(2)}, u32[]{:S(2)}) collective-permute-start(f32[16,128]{1,0:T(8,128)S(1)} %get-tuple-element.57), channel_id=1, source_target_pairs={{1,0},{2,1},{3,2},{0,3},{5,4},{6,5},{7,6},{4,7},{9,8},{10,9},{11,1... | collective-permute-start | bytes 24584 | tf_op jit(solution)/shard_map/ppermute | solution.py:239
  30.9 3.7 %copy-start.2 = (f32[2048]{0:T(1024)S(1)}, f32[2048]{0:T(1024)}, u32[]{:S(2)}) copy-start(f32[2048]{0:T(1024)} %param.5) | copy-start | bytes 24580
  31.0 3.7 %collective-permute-start.9 = (f32[16,128]{1,0:T(8,128)S(1)}, f32[16,128]{1,0:T(8,128)S(1)}, u32[]{:S(2)}, u32[]{:S(2)}) collective-permute-start(f32[16,128]{1,0:T(8,128)S(1)} %get-tuple-element.58), channel_id=1, source_target_pairs={{2,0},{3,1},{18,2},{19,3},{6,4},{7,5},{22,6},{23,7},{10,8},{11,9},... | collective-permute-start | bytes 24584 | tf_op jit(solution)/shard_map/ppermute | solution.py:249

commit v6 on v5

--- a/solution.py
+++ b/solution.py
@@ -87,13 +87,13 @@
 
 
 def pack(vec, docs, own1, own2, own):
-    tokens = vec.shape[0]
+    tokens = vec.shape[0] - docs.shape[0]
     head = own1.shape[0] - docs.shape[0]
     tags = docs[...].astype(F32).astype(BF16)
     own1[:head] = vec[:head]
     own1[head:] = tags
-    own2[...] = vec[head:]
-    own[:tokens] = vec[...]
+    own2[...] = vec[head:tokens]
+    own[:tokens] = vec[:tokens]
     own[tokens:] = tags
 
 
@@ -123,7 +123,7 @@
     own1, own2, own = call(
         "pack",
         pack,
-        [vectors, docs.reshape(lines, LANES)],
+        [jnp.pad(vectors, ((0, lines), (0, 0))), docs.reshape(lines, LANES)],
         [struct(rows, dim, dtype=BF16) for rows in (head + lines, tokens - head, tokens + lines)],
     )
     p1 = lax.ppermute(own1, axes, ring)

time: 35.4 us -> 34.8 us (0.983)
  local copies, waits for them, and re-layouts: 1.74 us -> 1.1 us
    unnamed x6 -> x4, local copies, waits for them, and re-layouts: 1.74 us -> 0.01 us
    pad x0 -> x1, local copies, waits for them, and re-layouts: none -> 1.09 us  [per_device(): jnp.pad(vectors, ((0, lines), (0, 0)))]
where the time goes in v6:
time: 34.8 us; the launch traced here: 34.6 us
  starting transfers between devices  13.2 us (38%)
  Pallas kernels  11.4 us (33%)
  waiting for transfers between devices  8.17 us (23%)
  local copies, waits for them, and re-layouts  1.1 us (3%)
  other arithmetic  0.61 us (2%)
    pallas_call x11, Pallas kernels, call(): pl.pallas_call(kernel, out_shape=outs, in_specs=specs or [pl.BlockSpec(me...  11.4 us
    ppermute x1, waiting for transfers between devices, per_device(): p1 = lax.ppermute(own1, axes, ring)  5.06 us
    ppermute x1, starting transfers between devices, per_device(): z1 = lax.ppermute(own1, axes, layer)  3.6 us
    ppermute x1, starting transfers between devices, per_device(): q = lax.ppermute(own, axes, pair)  2.98 us
    ppermute x1, starting transfers between devices, per_device(): q_back = lax.ppermute(q_max, axes, backwards(pair))  1.89 us
    ppermute x1, starting transfers between devices, per_device(): p_back = lax.ppermute(p_max, axes, backwards(ring))  1.5 us
    ppermute x1, starting transfers between devices, per_device(): p1 = lax.ppermute(own1, axes, ring)  1.49 us
    ppermute x1, waiting for transfers between devices, per_device(): q_back = lax.ppermute(q_max, axes, backwards(pair))  1.48 us
  transfers between devices with their start and end apart: 10, of which 5 were waited for; matrix products, arithmetic and copies ran while one was open for 0% of the time, Pallas kernels for 25%

profile of v6, /device:TPU:0, one launch (start us, length us, event | category | flops | bytes accessed | tf_op | source)
XLA Modules:
  0.0 34.6 jit_solution(157313971500341787)
XLA Ops:
  0.0 0.0 copy-start
  0.0 1.1 %pad.4.vec = bf16[2064,128]{1,0:T(8,128)(2,1)S(1)} pad(bf16[2048,128]{1,0:T(8,128)(2,1)} %param.3, bf16[]{:T(256)} %constant.42.clone.1), padding=0_16x0_0 | pad | bytes 1052674 | tf_op jit(solution)/shard_map/jit(_pad)/pad | solution.py:126
  1.1 0.0 copy-done
  1.1 0.1 pack.1
  1.2 3.0 %collective-permute-start.2 = (bf16[2064,128]{1,0:T(8,128)(2,1)S(1)}, bf16[2064,128]{1,0:T(8,128)(2,1)S(1)}, u32[]{:S(2)}, u32[]{:S(2)}) collective-permute-start(bf16[2064,128]{1,0:T(8,128)(2,1)S(1)} %get-tuple-element.34.own), channel_id=1, source_target_pairs={{0,2},{1,3},{2,18},{3,19},{4,6},{5,7},{6,22},{7,23},{8,10},{9,11},... | collective-permute-start | bytes 1585160 | tf_op jit(solution)/shard_map/ppermute | solution.py:131
  4.2 1.5 %collective-permute-start.3 = (bf16[1296,128]{1,0:T(8,128)(2,1)S(1)}, bf16[1296,128]{1,0:T(8,128)(2,1)S(1)}, u32[]{:S(2)}, u32[]{:S(2)}) collective-permute-start(bf16[1296,128]{1,0:T(8,128)(2,1)S(1)} %get-tuple-element.32), channel_id=1, source_target_pairs={{0,1},{1,2},{2,3},{3,0},{4,5},{5,6},{6,7},{7,4},{8,9},{9,10},{10,1... | collective-permute-start | bytes 995336 | tf_op jit(solution)/shard_map/ppermute | solution.py:129
  5.7 3.6 %collective-permute-start = (bf16[1296,128]{1,0:T(8,128)(2,1)S(1)}, bf16[1296,128]{1,0:T(8,128)(2,1)S(1)}, u32[]{:S(2)}, u32[]{:S(2)}) collective-permute-start(bf16[1296,128]{1,0:T(8,128)(2,1)S(1)} %get-tuple-element.32), channel_id=1, source_target_pairs={{0,12},{1,5},{2,6},{3,7},{4,0},{5,9},{6,10},{7,11},{8,4},{9,13},{1... | collective-permute-start | bytes 995336 | tf_op jit(solution)/shard_map/ppermute | solution.py:130
  9.3 0.4 %collective-permute-start.1 = (bf16[768,128]{1,0:T(8,128)(2,1)S(1)}, bf16[768,128]{1,0:T(8,128)(2,1)S(1)}, u32[]{:S(2)}, u32[]{:S(2)}) collective-permute-start(bf16[768,128]{1,0:T(8,128)(2,1)S(1)} %get-tuple-element.33), channel_id=1, source_target_pairs={{0,12},{1,5},{2,6},{3,7},{4,0},{5,9},{6,10},{7,11},{8,4},{9,13},{1... | collective-permute-start | bytes 589832 | tf_op jit(solution)/shard_map/ppermute | solution.py:133
  9.7 0.0 collective-permute-start.4
  9.7 0.2 own_marks.1.own_m
  9.9 5.1 %collective-permute-done.3.p1 = bf16[1296,128]{1,0:T(8,128)(2,1)S(1)} collective-permute-done((bf16[1296,128]{1,0:T(8,128)(2,1)S(1)}, bf16[1296,128]{1,0:T(8,128)(2,1)S(1)}, u32[]{:S(2)}, u32[]{:S(2)}) %collective-permute-start.3) | collective-permute-done | bytes 331808 | tf_op jit(solution)/shard_map/ppermute | solution.py:129
  15.0 1.7 %ring1.1 = (bf16[1280,128]{1,0:T(8,128)(2,1)S(1)}, bf16[768,128]{1,0:T(8,128)(2,1)S(1)}, f32[16,128]{1,0:T(8,128)S(1)}, f32[10,128]{1,0:T(8,128)S(1)}) custom-call(bf16[2064,128]{1,0:T(8,128)(2,1)S(1)} %get-tuple-element.34.own, bf16[2048,128]{1,0:T(8,128)(2,1)S(1)} %own_marks.1.own_m, bf16[1296,128]{1,0:T(8,128)(2,1)S(1)} %collective-permute-done.3.p1), custom_call_target="tpu_custom_call" | custom-call | bytes 1922048 | tf_op jit(solution)/shard_map/ring1/pallas_call | solution.py:49
  16.7 0.8 %collective-permute-done.z1 = bf16[1296,128]{1,0:T(8,128)(2,1)S(1)} collective-permute-done((bf16[1296,128]{1,0:T(8,128)(2,1)S(1)}, bf16[1296,128]{1,0:T(8,128)(2,1)S(1)}, u32[]{:S(2)}, u32[]{:S(2)}) %collective-permute-start) | collective-permute-done | bytes 331808 | tf_op jit(solution)/shard_map/ppermute | solution.py:130
  17.5 2.6 %layer1.1 = (bf16[1280,128]{1,0:T(8,128)(2,1)S(1)}, bf16[768,128]{1,0:T(8,128)(2,1)S(1)}, f32[16,128]{1,0:T(8,128)S(1)}, f32[10,128]{1,0:T(8,128)S(1)}, f32[10,128]{1,0:T(8,128)S(1)}) custom-call(bf16[2064,128]{1,0:T(8,128)(2,1)S(1)} %get-tuple-element.34.own, bf16[2048,128]{1,0:T(8,128)(2,1)S(1)} %own_marks.1.own_m, ...), custom_call_target="tpu_custom_call" | custom-call | bytes 2599936 | tf_op jit(solution)/shard_map/layer1/pallas_call | solution.py:49
  20.1 0.0 collective-permute-done.1.z2
  20.1 0.0 collective-permute-done.4.p2
  20.1 1.7 %second.1 = (f32[16,128]{1,0:T(8,128)S(1)}, f32[16,128]{1,0:T(8,128)S(1)}) custom-call(bf16[1296,128]{1,0:T(8,128)(2,1)S(1)} %collective-permute-done.3.p1, bf16[1280,128]{1,0:T(8,128)(2,1)S(1)} %get-tuple-element.35.p_m1, bf16[768,128]{1,0:T(8,128)(2,1)S(1)} %collective-permute-done.4.p2, bf16[768,128]{1,0:T(8,128)(2,1)S(1)} %get-tuple-element.40.p_m2, ...), custom_call_target="tpu_custom_call" | custom-call | bytes 2131968 | tf_op jit(solution)/shard_map/second/pallas_call | solution.py:49
  21.8 0.0 collective-permute-done.2.q
  21.9 0.1 collective-permute-start.5
  22.0 1.1 %layer2.1 = (f32[16,128]{1,0:T(8,128)S(1)}, f32[16,128]{1,0:T(8,128)S(1)}) custom-call(bf16[2064,128]{1,0:T(8,128)(2,1)S(1)} %get-tuple-element.34.own, bf16[2048,128]{1,0:T(8,128)(2,1)S(1)} %own_marks.1.own_m, bf16[768,128]{1,0:T(8,128)(2,1)S(1)} %collective-permute-done.1.z2, bf16[768,128]{1,0:T(8,128)(2,1)S(1)} %get-tuple-element.38.z_m2, ...), custom_call_target="tpu_custom_call" | custom-call | bytes 1478656 | tf_op jit(solution)/shard_map/layer2/pallas_call | solution.py:49
  23.1 0.2 q_marks.1.q_m
  23.3 0.5 %collective-permute-done.5.r = bf16[2064,128]{1,0:T(8,128)(2,1)S(1)} collective-permute-done((bf16[2064,128]{1,0:T(8,128)(2,1)S(1)}, bf16[2064,128]{1,0:T(8,128)(2,1)S(1)}, u32[]{:S(2)}, u32[]{:S(2)}) %collective-permute-start.5) | collective-permute-done | bytes 528416 | tf_op jit(solution)/shard_map/ppermute | solution.py:173
  23.8 2.6 %pairs.1 = (f32[64,128]{1,0:T(8,128)S(1)}, f32[32,128]{1,0:T(8,128)S(1)}) custom-call(s32[1]{0:T(128)} %bitcast.has, bf16[1296,128]{1,0:T(8,128)(2,1)S(1)} %collective-permute-done.z1, bf16[768,128]{1,0:T(8,128)(2,1)S(1)} %collective-permute-done.1.z2, bf16[2064,128]{1,0:T(8,128)(2,1)S(1)} %collective-permute-done.2.q, bf16[2048,128]{1,0:T(8,128)(2,1)S(1)} %q_marks.1.q_m, ...), custom_call_target="tpu_custom_call" | custom-call | bytes 2166788 | tf_op jit(solution)/shard_map/pairs/pallas_call | solution.py:49
  26.5 1.2 %collective-permute-start.7 = (f32[64,128]{1,0:T(8,128)S(1)}, f32[64,128]{1,0:T(8,128)S(1)}, u32[]{:S(2)}, u32[]{:S(2)}) collective-permute-start(f32[64,128]{1,0:T(8,128)S(1)} %get-tuple-element.56), channel_id=1, source_target_pairs={{12,0},{5,1},{6,2},{7,3},{0,4},{9,5},{10,6},{11,7},{4,8},{13,9},{1... | collective-permute-start | bytes 98312 | tf_op jit(solution)/shard_map/ppermute | solution.py:238
  27.7 0.0 collective-permute-start.6
  27.7 1.1 %ring2.3 = (f32[16,128]{1,0:T(8,128)S(1)}, f32[16,128]{1,0:T(8,128)S(1)}) custom-call(s32[1]{0:T(128)} %bitcast.2.far, bf16[2064,128]{1,0:T(8,128)(2,1)S(1)} %get-tuple-element.34.own, bf16[2048,128]{1,0:T(8,128)(2,1)S(1)} %own_marks.1.own_m, bf16[768,128]{1,0:T(8,128)(2,1)S(1)} %collective-permute-done.4.p2, bf16[768,128]{1,0:T(8,128)(2,1)S(1)} %get-tuple-element.40.p_m2, ...), custom_call_target="tpu_custom_call" | custom-call | bytes 1478660 | tf_op jit(solution)/shard_map/ring2/pallas_call | solution.py:49
  28.8 1.5 %collective-permute-start.8 = (f32[16,128]{1,0:T(8,128)S(1)}, f32[16,128]{1,0:T(8,128)S(1)}, u32[]{:S(2)}, u32[]{:S(2)}) collective-permute-start(f32[16,128]{1,0:T(8,128)S(1)} %get-tuple-element.57), channel_id=1, source_target_pairs={{1,0},{2,1},{3,2},{0,3},{5,4},{6,5},{7,6},{4,7},{9,8},{10,9},{11,1... | collective-permute-start | bytes 24584 | tf_op jit(solution)/shard_map/ppermute | solution.py:239
  30.3 0.0 collective-permute-done.6.theirs
  30.3 0.0 copy-start.1
  30.3 1.9 %collective-permute-start.9 = (f32[16,128]{1,0:T(8,128)S(1)}, f32[16,128]{1,0:T(8,128)S(1)}, u32[]{:S(2)}, u32[]{:S(2)}) collective-permute-start(f32[16,128]{1,0:T(8,128)S(1)} %get-tuple-element.58), channel_id=1, source_target_pairs={{2,0},{3,1},{18,2},{19,3},{6,4},{7,5},{22,6},{23,7},{10,8},{11,9},... | collective-permute-start | bytes 24584 | tf_op jit(solution)/shard_map/ppermute | solution.py:249
  32.2 0.3 collective-permute-done.8
  32.5 1.5 %collective-permute-done.9 = f32[16,128]{1,0:T(8,128)S(1)} collective-permute-done((f32[16,128]{1,0:T(8,128)S(1)}, f32[16,128]{1,0:T(8,128)S(1)}, u32[]{:S(2)}, u32[]{:S(2)}) %collective-permute-start.9) | collective-permute-done | bytes 8224 | tf_op jit(solution)/shard_map/ppermute | solution.py:249
  34.0 0.0 collective-permute-done.7
  34.0 0.0 copy-done.1
  34.0 0.6 %fusion.2 = f32[2048]{0:T(1024)} fusion(f32[2048]{0:T(1024)S(1)} %copy-done.1, f32[16,128]{1,0:T(8,128)S(1)} %get-tuple-element.54, f32[64,128]{1,0:T(8,128)S(1)} %collective-permute-done.7, f32[16,128]{1,0:T(8,128)S(1)} %collective-permute-done.8, f32[16,128]{1,0:T(8,128)S(1)} %collective-permute-done.9, pred[]{:T(512)} %bitcast.3), kind=kLoop, calls=%fused_computation.3 | loop fusion | flops 10240 | bytes 49153 | tf_op jit(solution)/shard_map/max | solution.py:252
  (2 shorter events, 0.0 us)
Async XLA Ops:
  0.0 1.1 %copy-start = (s32[2048]{0:T(1024)S(1)}, s32[2048]{0:T(1024)}, u32[]{:S(2)}) copy-start(s32[2048]{0:T(1024)} %param.4) | copy-start | bytes 24580
  1.2 20.7 %collective-permute-start.2 = (bf16[2064,128]{1,0:T(8,128)(2,1)S(1)}, bf16[2064,128]{1,0:T(8,128)(2,1)S(1)}, u32[]{:S(2)}, u32[]{:S(2)}) collective-permute-start(bf16[2064,128]{1,0:T(8,128)(2,1)S(1)} %get-tuple-element.34.own), channel_id=1, source_target_pairs={{0,2},{1,3},{2,18},{3,19},{4,6},{5,7},{6,22},{7,23},{8,10},{9,11},... | collective-permute-start | bytes 1585160 | tf_op jit(solution)/shard_map/ppermute | solution.py:131
  4.2 10.8 %collective-permute-start.3 = (bf16[1296,128]{1,0:T(8,128)(2,1)S(1)}, bf16[1296,128]{1,0:T(8,128)(2,1)S(1)}, u32[]{:S(2)}, u32[]{:S(2)}) collective-permute-start(bf16[1296,128]{1,0:T(8,128)(2,1)S(1)} %get-tuple-element.32), channel_id=1, source_target_pairs={{0,1},{1,2},{2,3},{3,0},{4,5},{5,6},{6,7},{7,4},{8,9},{9,10},{10,1... | collective-permute-start | bytes 995336 | tf_op jit(solution)/shard_map/ppermute | solution.py:129
  5.7 11.9 %collective-permute-start = (bf16[1296,128]{1,0:T(8,128)(2,1)S(1)}, bf16[1296,128]{1,0:T(8,128)(2,1)S(1)}, u32[]{:S(2)}, u32[]{:S(2)}) collective-permute-start(bf16[1296,128]{1,0:T(8,128)(2,1)S(1)} %get-tuple-element.32), channel_id=1, source_target_pairs={{0,12},{1,5},{2,6},{3,7},{4,0},{5,9},{6,10},{7,11},{8,4},{9,13},{1... | collective-permute-start | bytes 995336 | tf_op jit(solution)/shard_map/ppermute | solution.py:130
  9.3 10.9 %collective-permute-start.1 = (bf16[768,128]{1,0:T(8,128)(2,1)S(1)}, bf16[768,128]{1,0:T(8,128)(2,1)S(1)}, u32[]{:S(2)}, u32[]{:S(2)}) collective-permute-start(bf16[768,128]{1,0:T(8,128)(2,1)S(1)} %get-tuple-element.33), channel_id=1, source_target_pairs={{0,12},{1,5},{2,6},{3,7},{4,0},{5,9},{6,10},{7,11},{8,4},{9,13},{1... | collective-permute-start | bytes 589832 | tf_op jit(solution)/shard_map/ppermute | solution.py:133
  9.7 10.4 %collective-permute-start.4 = (bf16[768,128]{1,0:T(8,128)(2,1)S(1)}, bf16[768,128]{1,0:T(8,128)(2,1)S(1)}, u32[]{:S(2)}, u32[]{:S(2)}) collective-permute-start(bf16[768,128]{1,0:T(8,128)(2,1)S(1)} %get-tuple-element.33), channel_id=1, source_target_pairs={{0,1},{1,2},{2,3},{3,0},{4,5},{5,6},{6,7},{7,4},{8,9},{9,10},{10,1... | collective-permute-start | bytes 589832 | tf_op jit(solution)/shard_map/ppermute | solution.py:132
  21.9 2.0 %collective-permute-start.5 = (bf16[2064,128]{1,0:T(8,128)(2,1)S(1)}, bf16[2064,128]{1,0:T(8,128)(2,1)S(1)}, u32[]{:S(2)}, u32[]{:S(2)}) collective-permute-start(bf16[2064,128]{1,0:T(8,128)(2,1)S(1)} %collective-permute-done.2.q), channel_id=1, source_target_pairs={{0,16},{1,17},{2,18},{3,19},{4,20},{5,21},{6,22},{7,23},{8,24},{9,... | collective-permute-start | bytes 1585160 | tf_op jit(solution)/shard_map/ppermute | solution.py:173
  26.5 7.5 %collective-permute-start.7 = (f32[64,128]{1,0:T(8,128)S(1)}, f32[64,128]{1,0:T(8,128)S(1)}, u32[]{:S(2)}, u32[]{:S(2)}) collective-permute-start(f32[64,128]{1,0:T(8,128)S(1)} %get-tuple-element.56), channel_id=1, source_target_pairs={{12,0},{5,1},{6,2},{7,3},{0,4},{9,5},{10,6},{11,7},{4,8},{13,9},{1... | collective-permute-start | bytes 98312 | tf_op jit(solution)/shard_map/ppermute | solution.py:238
  27.7 2.7 %collective-permute-start.6 = (f32[32,128]{1,0:T(8,128)S(1)}, f32[32,128]{1,0:T(8,128)S(1)}, u32[]{:S(2)}, u32[]{:S(2)}) collective-permute-start(f32[32,128]{1,0:T(8,128)S(1)} %get-tuple-element.48.mine), channel_id=1, source_target_pairs={{0,16},{1,17},{2,18},{3,19},{4,20},{5,21},{6,22},{7,23},{8,24},{9,... | collective-permute-start | bytes 49160 | tf_op jit(solution)/shard_map/ppermute | solution.py:213
  28.8 3.7 %collective-permute-start.8 = (f32[16,128]{1,0:T(8,128)S(1)}, f32[16,128]{1,0:T(8,128)S(1)}, u32[]{:S(2)}, u32[]{:S(2)}) collective-permute-start(f32[16,128]{1,0:T(8,128)S(1)} %get-tuple-element.57), channel_id=1, source_target_pairs={{1,0},{2,1},{3,2},{0,3},{5,4},{6,5},{7,6},{4,7},{9,8},{10,9},{11,1... | collective-permute-start | bytes 24584 | tf_op jit(solution)/shard_map/ppermute | solution.py:239
  30.3 3.7 %copy-start.1 = (f32[2048]{0:T(1024)S(1)}, f32[2048]{0:T(1024)}, u32[]{:S(2)}) copy-start(f32[2048]{0:T(1024)} %param.5) | copy-start | bytes 24580
  30.3 3.7 %collective-permute-start.9 = (f32[16,128]{1,0:T(8,128)S(1)}, f32[16,128]{1,0:T(8,128)S(1)}, u32[]{:S(2)}, u32[]{:S(2)}) collective-permute-start(f32[16,128]{1,0:T(8,128)S(1)} %get-tuple-element.58), channel_id=1, source_target_pairs={{2,0},{3,1},{18,2},{19,3},{6,4},{7,5},{22,6},{23,7},{10,8},{11,9},... | collective-permute-start | bytes 24584 | tf_op jit(solution)/shard_map/ppermute | solution.py:249

commit v7 on v6

--- a/solution.py
+++ b/solution.py
@@ -58,10 +58,11 @@
     )(*operands)
 
 
-def mark(tags, out, value):
+def mark(tags, out, value, first=0):
     lane = lax.broadcasted_iota(jnp.int32, (LANES, LANES), 0).astype(F32)
-    for row in range(tags.shape[0]):
-        hit = jnp.where(tags[row : row + 1].astype(F32) == lane, F32(value), F32(0.0))
+    tags = tags.astype(F32)
+    for row in range(out.shape[0] // LANES):
+        hit = jnp.where(tags[first + row : first + row + 1] == lane, F32(value), F32(0.0))
         out[row * LANES : (row + 1) * LANES] = hit.T.astype(BF16)
 
 
@@ -138,15 +139,15 @@
     (own_m,) = call("own_marks", own_marks, [own], [marks])
 
     def ring1(own, own_m, p1, p_m1, p_m2, own_out, p_out):
-        mark(p1[head : head + part], p_m1, MARK)
-        mark(p1[head + part :], p_m2, MARK)
+        mark(p1[head:], p_m1, MARK)
+        mark(p1[head:], p_m2, MARK, part)
         p_out[...], own_out[...] = tile([(p1[:head], p_m1[...])], [(own[:tokens], own_m[...])])
 
     p_m1, p_m2, own_max, p1_max = call("ring1", ring1, [own, own_m, p1], [marks1, marks2, whole, piece1])
 
     def layer1(own, own_m, p1, p_m1, z1, own_max, p_max, z_m1, z_m2, own_out, p_out, z_out):
-        mark(z1[head : head + part], z_m1, MARK)
-        mark(z1[head + part :], z_m2, MARK)
+        mark(z1[head:], z_m1, MARK)
+        mark(z1[head:], z_m2, MARK, part)
         row, col = tile([(z1[:head], z_m1[...])], [(own[:tokens], own_m[...]), (p1[:head], -p_m1[...])])
         own_out[...] = jnp.maximum(own_max[...], col[:lines])
         p_out[...] = jnp.maximum(p_max[...], col[lines:])

time: 34.8 us -> 34.8 us (level)
  no operation moved by 1% of the time
where the time goes in v7:
time: 34.8 us; the launch traced here: 34.6 us
  starting transfers between devices  13.2 us (38%)
  Pallas kernels  11.4 us (33%)
  waiting for transfers between devices  8.16 us (23%)
  local copies, waits for them, and re-layouts  1.1 us (3%)
  other arithmetic  0.61 us (2%)
    pallas_call x11, Pallas kernels, call(): pl.pallas_call(kernel, out_shape=outs, in_specs=specs or [pl.BlockSpec(me...  11.4 us
    ppermute x1, waiting for transfers between devices, per_device(): p1 = lax.ppermute(own1, axes, ring)  5.06 us
    ppermute x1, starting transfers between devices, per_device(): z1 = lax.ppermute(own1, axes, layer)  3.6 us
    ppermute x1, starting transfers between devices, per_device(): q = lax.ppermute(own, axes, pair)  2.98 us
    ppermute x1, starting transfers between devices, per_device(): q_back = lax.ppermute(q_max, axes, backwards(pair))  1.89 us
    ppermute x1, starting transfers between devices, per_device(): p_back = lax.ppermute(p_max, axes, backwards(ring))  1.5 us
    ppermute x1, starting transfers between devices, per_device(): p1 = lax.ppermute(own1, axes, ring)  1.49 us
    ppermute x1, waiting for transfers between devices, per_device(): q_back = lax.ppermute(q_max, axes, backwards(pair))  1.48 us
  transfers between devices with their start and end apart: 10, of which 5 were waited for; matrix products, arithmetic and copies ran while one was open for 0% of the time, Pallas kernels for 25%

profile of v7, /device:TPU:0, one launch (start us, length us, event | category | flops | bytes accessed | tf_op | source)
XLA Modules:
  0.0 34.6 jit_solution(10895599899178352984)
XLA Ops:
  0.0 0.0 copy-start
  0.0 1.1 %pad.4.vec = bf16[2064,128]{1,0:T(8,128)(2,1)S(1)} pad(bf16[2048,128]{1,0:T(8,128)(2,1)} %param.3, bf16[]{:T(256)} %constant.42.clone.1), padding=0_16x0_0 | pad | bytes 1052674 | tf_op jit(solution)/shard_map/jit(_pad)/pad | solution.py:127
  1.1 0.0 copy-done
  1.1 0.1 pack.1
  1.2 3.0 %collective-permute-start.2 = (bf16[2064,128]{1,0:T(8,128)(2,1)S(1)}, bf16[2064,128]{1,0:T(8,128)(2,1)S(1)}, u32[]{:S(2)}, u32[]{:S(2)}) collective-permute-start(bf16[2064,128]{1,0:T(8,128)(2,1)S(1)} %get-tuple-element.34.own), channel_id=1, source_target_pairs={{0,2},{1,3},{2,18},{3,19},{4,6},{5,7},{6,22},{7,23},{8,10},{9,11},... | collective-permute-start | bytes 1585160 | tf_op jit(solution)/shard_map/ppermute | solution.py:132
  4.2 1.5 %collective-permute-start.3 = (bf16[1296,128]{1,0:T(8,128)(2,1)S(1)}, bf16[1296,128]{1,0:T(8,128)(2,1)S(1)}, u32[]{:S(2)}, u32[]{:S(2)}) collective-permute-start(bf16[1296,128]{1,0:T(8,128)(2,1)S(1)} %get-tuple-element.32), channel_id=1, source_target_pairs={{0,1},{1,2},{2,3},{3,0},{4,5},{5,6},{6,7},{7,4},{8,9},{9,10},{10,1... | collective-permute-start | bytes 995336 | tf_op jit(solution)/shard_map/ppermute | solution.py:130
  5.7 3.6 %collective-permute-start = (bf16[1296,128]{1,0:T(8,128)(2,1)S(1)}, bf16[1296,128]{1,0:T(8,128)(2,1)S(1)}, u32[]{:S(2)}, u32[]{:S(2)}) collective-permute-start(bf16[1296,128]{1,0:T(8,128)(2,1)S(1)} %get-tuple-element.32), channel_id=1, source_target_pairs={{0,12},{1,5},{2,6},{3,7},{4,0},{5,9},{6,10},{7,11},{8,4},{9,13},{1... | collective-permute-start | bytes 995336 | tf_op jit(solution)/shard_map/ppermute | solution.py:131
  9.3 0.4 %collective-permute-start.1 = (bf16[768,128]{1,0:T(8,128)(2,1)S(1)}, bf16[768,128]{1,0:T(8,128)(2,1)S(1)}, u32[]{:S(2)}, u32[]{:S(2)}) collective-permute-start(bf16[768,128]{1,0:T(8,128)(2,1)S(1)} %get-tuple-element.33), channel_id=1, source_target_pairs={{0,12},{1,5},{2,6},{3,7},{4,0},{5,9},{6,10},{7,11},{8,4},{9,13},{1... | collective-permute-start | bytes 589832 | tf_op jit(solution)/shard_map/ppermute | solution.py:134
  9.7 0.0 collective-permute-start.4
  9.7 0.2 own_marks.1.own_m
  9.9 5.1 %collective-permute-done.3.p1 = bf16[1296,128]{1,0:T(8,128)(2,1)S(1)} collective-permute-done((bf16[1296,128]{1,0:T(8,128)(2,1)S(1)}, bf16[1296,128]{1,0:T(8,128)(2,1)S(1)}, u32[]{:S(2)}, u32[]{:S(2)}) %collective-permute-start.3) | collective-permute-done | bytes 331808 | tf_op jit(solution)/shard_map/ppermute | solution.py:130
  15.0 1.7 %ring1.1 = (bf16[1280,128]{1,0:T(8,128)(2,1)S(1)}, bf16[768,128]{1,0:T(8,128)(2,1)S(1)}, f32[16,128]{1,0:T(8,128)S(1)}, f32[10,128]{1,0:T(8,128)S(1)}) custom-call(bf16[2064,128]{1,0:T(8,128)(2,1)S(1)} %get-tuple-element.34.own, bf16[2048,128]{1,0:T(8,128)(2,1)S(1)} %own_marks.1.own_m, bf16[1296,128]{1,0:T(8,128)(2,1)S(1)} %collective-permute-done.3.p1), custom_call_target="tpu_custom_call" | custom-call | bytes 1922048 | tf_op jit(solution)/shard_map/ring1/pallas_call | solution.py:49
  16.7 0.8 %collective-permute-done.z1 = bf16[1296,128]{1,0:T(8,128)(2,1)S(1)} collective-permute-done((bf16[1296,128]{1,0:T(8,128)(2,1)S(1)}, bf16[1296,128]{1,0:T(8,128)(2,1)S(1)}, u32[]{:S(2)}, u32[]{:S(2)}) %collective-permute-start) | collective-permute-done | bytes 331808 | tf_op jit(solution)/shard_map/ppermute | solution.py:131
  17.5 2.6 %layer1.1 = (bf16[1280,128]{1,0:T(8,128)(2,1)S(1)}, bf16[768,128]{1,0:T(8,128)(2,1)S(1)}, f32[16,128]{1,0:T(8,128)S(1)}, f32[10,128]{1,0:T(8,128)S(1)}, f32[10,128]{1,0:T(8,128)S(1)}) custom-call(bf16[2064,128]{1,0:T(8,128)(2,1)S(1)} %get-tuple-element.34.own, bf16[2048,128]{1,0:T(8,128)(2,1)S(1)} %own_marks.1.own_m, ...), custom_call_target="tpu_custom_call" | custom-call | bytes 2599936 | tf_op jit(solution)/shard_map/layer1/pallas_call | solution.py:49
  20.1 0.0 collective-permute-done.1.z2
  20.1 0.0 collective-permute-done.4.p2
  20.1 1.7 %second.1 = (f32[16,128]{1,0:T(8,128)S(1)}, f32[16,128]{1,0:T(8,128)S(1)}) custom-call(bf16[1296,128]{1,0:T(8,128)(2,1)S(1)} %collective-permute-done.3.p1, bf16[1280,128]{1,0:T(8,128)(2,1)S(1)} %get-tuple-element.35.p_m1, bf16[768,128]{1,0:T(8,128)(2,1)S(1)} %collective-permute-done.4.p2, bf16[768,128]{1,0:T(8,128)(2,1)S(1)} %get-tuple-element.40.p_m2, ...), custom_call_target="tpu_custom_call" | custom-call | bytes 2131968 | tf_op jit(solution)/shard_map/second/pallas_call | solution.py:49
  21.8 0.0 collective-permute-done.2.q
  21.9 0.1 collective-permute-start.5
  22.0 1.1 %layer2.1 = (f32[16,128]{1,0:T(8,128)S(1)}, f32[16,128]{1,0:T(8,128)S(1)}) custom-call(bf16[2064,128]{1,0:T(8,128)(2,1)S(1)} %get-tuple-element.34.own, bf16[2048,128]{1,0:T(8,128)(2,1)S(1)} %own_marks.1.own_m, bf16[768,128]{1,0:T(8,128)(2,1)S(1)} %collective-permute-done.1.z2, bf16[768,128]{1,0:T(8,128)(2,1)S(1)} %get-tuple-element.38.z_m2, ...), custom_call_target="tpu_custom_call" | custom-call | bytes 1478656 | tf_op jit(solution)/shard_map/layer2/pallas_call | solution.py:49
  23.1 0.2 q_marks.1.q_m
  23.3 0.5 %collective-permute-done.5.r = bf16[2064,128]{1,0:T(8,128)(2,1)S(1)} collective-permute-done((bf16[2064,128]{1,0:T(8,128)(2,1)S(1)}, bf16[2064,128]{1,0:T(8,128)(2,1)S(1)}, u32[]{:S(2)}, u32[]{:S(2)}) %collective-permute-start.5) | collective-permute-done | bytes 528416 | tf_op jit(solution)/shard_map/ppermute | solution.py:174
  23.8 2.6 %pairs.1 = (f32[64,128]{1,0:T(8,128)S(1)}, f32[32,128]{1,0:T(8,128)S(1)}) custom-call(s32[1]{0:T(128)} %bitcast.has, bf16[1296,128]{1,0:T(8,128)(2,1)S(1)} %collective-permute-done.z1, bf16[768,128]{1,0:T(8,128)(2,1)S(1)} %collective-permute-done.1.z2, bf16[2064,128]{1,0:T(8,128)(2,1)S(1)} %collective-permute-done.2.q, bf16[2048,128]{1,0:T(8,128)(2,1)S(1)} %q_marks.1.q_m, ...), custom_call_target="tpu_custom_call" | custom-call | bytes 2166788 | tf_op jit(solution)/shard_map/pairs/pallas_call | solution.py:49
  26.5 1.2 %collective-permute-start.7 = (f32[64,128]{1,0:T(8,128)S(1)}, f32[64,128]{1,0:T(8,128)S(1)}, u32[]{:S(2)}, u32[]{:S(2)}) collective-permute-start(f32[64,128]{1,0:T(8,128)S(1)} %get-tuple-element.56), channel_id=1, source_target_pairs={{12,0},{5,1},{6,2},{7,3},{0,4},{9,5},{10,6},{11,7},{4,8},{13,9},{1... | collective-permute-start | bytes 98312 | tf_op jit(solution)/shard_map/ppermute | solution.py:239
  27.7 0.0 collective-permute-start.6
  27.7 1.1 %ring2.3 = (f32[16,128]{1,0:T(8,128)S(1)}, f32[16,128]{1,0:T(8,128)S(1)}) custom-call(s32[1]{0:T(128)} %bitcast.2.far, bf16[2064,128]{1,0:T(8,128)(2,1)S(1)} %get-tuple-element.34.own, bf16[2048,128]{1,0:T(8,128)(2,1)S(1)} %own_marks.1.own_m, bf16[768,128]{1,0:T(8,128)(2,1)S(1)} %collective-permute-done.4.p2, bf16[768,128]{1,0:T(8,128)(2,1)S(1)} %get-tuple-element.40.p_m2, ...), custom_call_target="tpu_custom_call" | custom-call | bytes 1478660 | tf_op jit(solution)/shard_map/ring2/pallas_call | solution.py:49
  28.8 1.5 %collective-permute-start.8 = (f32[16,128]{1,0:T(8,128)S(1)}, f32[16,128]{1,0:T(8,128)S(1)}, u32[]{:S(2)}, u32[]{:S(2)}) collective-permute-start(f32[16,128]{1,0:T(8,128)S(1)} %get-tuple-element.57), channel_id=1, source_target_pairs={{1,0},{2,1},{3,2},{0,3},{5,4},{6,5},{7,6},{4,7},{9,8},{10,9},{11,1... | collective-permute-start | bytes 24584 | tf_op jit(solution)/shard_map/ppermute | solution.py:240
  30.3 0.0 collective-permute-done.6.theirs
  30.3 0.0 copy-start.1
  30.3 1.9 %collective-permute-start.9 = (f32[16,128]{1,0:T(8,128)S(1)}, f32[16,128]{1,0:T(8,128)S(1)}, u32[]{:S(2)}, u32[]{:S(2)}) collective-permute-start(f32[16,128]{1,0:T(8,128)S(1)} %get-tuple-element.58), channel_id=1, source_target_pairs={{2,0},{3,1},{18,2},{19,3},{6,4},{7,5},{22,6},{23,7},{10,8},{11,9},... | collective-permute-start | bytes 24584 | tf_op jit(solution)/shard_map/ppermute | solution.py:250
  32.2 0.3 collective-permute-done.8
  32.5 1.5 %collective-permute-done.9 = f32[16,128]{1,0:T(8,128)S(1)} collective-permute-done((f32[16,128]{1,0:T(8,128)S(1)}, f32[16,128]{1,0:T(8,128)S(1)}, u32[]{:S(2)}, u32[]{:S(2)}) %collective-permute-start.9) | collective-permute-done | bytes 8224 | tf_op jit(solution)/shard_map/ppermute | solution.py:250
  34.0 0.0 collective-permute-done.7
  34.0 0.0 copy-done.1
  34.0 0.6 %fusion.2 = f32[2048]{0:T(1024)} fusion(f32[2048]{0:T(1024)S(1)} %copy-done.1, f32[16,128]{1,0:T(8,128)S(1)} %get-tuple-element.54, f32[64,128]{1,0:T(8,128)S(1)} %collective-permute-done.7, f32[16,128]{1,0:T(8,128)S(1)} %collective-permute-done.8, f32[16,128]{1,0:T(8,128)S(1)} %collective-permute-done.9, pred[]{:T(512)} %bitcast.3), kind=kLoop, calls=%fused_computation.3 | loop fusion | flops 10240 | bytes 49153 | tf_op jit(solution)/shard_map/max | solution.py:253
  (2 shorter events, 0.0 us)
Async XLA Ops:
  0.0 1.1 %copy-start = (s32[2048]{0:T(1024)S(1)}, s32[2048]{0:T(1024)}, u32[]{:S(2)}) copy-start(s32[2048]{0:T(1024)} %param.4) | copy-start | bytes 24580
  1.2 20.7 %collective-permute-start.2 = (bf16[2064,128]{1,0:T(8,128)(2,1)S(1)}, bf16[2064,128]{1,0:T(8,128)(2,1)S(1)}, u32[]{:S(2)}, u32[]{:S(2)}) collective-permute-start(bf16[2064,128]{1,0:T(8,128)(2,1)S(1)} %get-tuple-element.34.own), channel_id=1, source_target_pairs={{0,2},{1,3},{2,18},{3,19},{4,6},{5,7},{6,22},{7,23},{8,10},{9,11},... | collective-permute-start | bytes 1585160 | tf_op jit(solution)/shard_map/ppermute | solution.py:132
  4.2 10.8 %collective-permute-start.3 = (bf16[1296,128]{1,0:T(8,128)(2,1)S(1)}, bf16[1296,128]{1,0:T(8,128)(2,1)S(1)}, u32[]{:S(2)}, u32[]{:S(2)}) collective-permute-start(bf16[1296,128]{1,0:T(8,128)(2,1)S(1)} %get-tuple-element.32), channel_id=1, source_target_pairs={{0,1},{1,2},{2,3},{3,0},{4,5},{5,6},{6,7},{7,4},{8,9},{9,10},{10,1... | collective-permute-start | bytes 995336 | tf_op jit(solution)/shard_map/ppermute | solution.py:130
  5.7 11.9 %collective-permute-start = (bf16[1296,128]{1,0:T(8,128)(2,1)S(1)}, bf16[1296,128]{1,0:T(8,128)(2,1)S(1)}, u32[]{:S(2)}, u32[]{:S(2)}) collective-permute-start(bf16[1296,128]{1,0:T(8,128)(2,1)S(1)} %get-tuple-element.32), channel_id=1, source_target_pairs={{0,12},{1,5},{2,6},{3,7},{4,0},{5,9},{6,10},{7,11},{8,4},{9,13},{1... | collective-permute-start | bytes 995336 | tf_op jit(solution)/shard_map/ppermute | solution.py:131
  9.3 10.9 %collective-permute-start.1 = (bf16[768,128]{1,0:T(8,128)(2,1)S(1)}, bf16[768,128]{1,0:T(8,128)(2,1)S(1)}, u32[]{:S(2)}, u32[]{:S(2)}) collective-permute-start(bf16[768,128]{1,0:T(8,128)(2,1)S(1)} %get-tuple-element.33), channel_id=1, source_target_pairs={{0,12},{1,5},{2,6},{3,7},{4,0},{5,9},{6,10},{7,11},{8,4},{9,13},{1... | collective-permute-start | bytes 589832 | tf_op jit(solution)/shard_map/ppermute | solution.py:134
  9.7 10.4 %collective-permute-start.4 = (bf16[768,128]{1,0:T(8,128)(2,1)S(1)}, bf16[768,128]{1,0:T(8,128)(2,1)S(1)}, u32[]{:S(2)}, u32[]{:S(2)}) collective-permute-start(bf16[768,128]{1,0:T(8,128)(2,1)S(1)} %get-tuple-element.33), channel_id=1, source_target_pairs={{0,1},{1,2},{2,3},{3,0},{4,5},{5,6},{6,7},{7,4},{8,9},{9,10},{10,1... | collective-permute-start | bytes 589832 | tf_op jit(solution)/shard_map/ppermute | solution.py:133
  21.9 2.0 %collective-permute-start.5 = (bf16[2064,128]{1,0:T(8,128)(2,1)S(1)}, bf16[2064,128]{1,0:T(8,128)(2,1)S(1)}, u32[]{:S(2)}, u32[]{:S(2)}) collective-permute-start(bf16[2064,128]{1,0:T(8,128)(2,1)S(1)} %collective-permute-done.2.q), channel_id=1, source_target_pairs={{0,16},{1,17},{2,18},{3,19},{4,20},{5,21},{6,22},{7,23},{8,24},{9,... | collective-permute-start | bytes 1585160 | tf_op jit(solution)/shard_map/ppermute | solution.py:174
  26.5 7.5 %collective-permute-start.7 = (f32[64,128]{1,0:T(8,128)S(1)}, f32[64,128]{1,0:T(8,128)S(1)}, u32[]{:S(2)}, u32[]{:S(2)}) collective-permute-start(f32[64,128]{1,0:T(8,128)S(1)} %get-tuple-element.56), channel_id=1, source_target_pairs={{12,0},{5,1},{6,2},{7,3},{0,4},{9,5},{10,6},{11,7},{4,8},{13,9},{1... | collective-permute-start | bytes 98312 | tf_op jit(solution)/shard_map/ppermute | solution.py:239
  27.7 2.6 %collective-permute-start.6 = (f32[32,128]{1,0:T(8,128)S(1)}, f32[32,128]{1,0:T(8,128)S(1)}, u32[]{:S(2)}, u32[]{:S(2)}) collective-permute-start(f32[32,128]{1,0:T(8,128)S(1)} %get-tuple-element.48.mine), channel_id=1, source_target_pairs={{0,16},{1,17},{2,18},{3,19},{4,20},{5,21},{6,22},{7,23},{8,24},{9,... | collective-permute-start | bytes 49160 | tf_op jit(solution)/shard_map/ppermute | solution.py:214
  28.8 3.7 %collective-permute-start.8 = (f32[16,128]{1,0:T(8,128)S(1)}, f32[16,128]{1,0:T(8,128)S(1)}, u32[]{:S(2)}, u32[]{:S(2)}) collective-permute-start(f32[16,128]{1,0:T(8,128)S(1)} %get-tuple-element.57), channel_id=1, source_target_pairs={{1,0},{2,1},{3,2},{0,3},{5,4},{6,5},{7,6},{4,7},{9,8},{10,9},{11,1... | collective-permute-start | bytes 24584 | tf_op jit(solution)/shard_map/ppermute | solution.py:240
  30.3 3.7 %copy-start.1 = (f32[2048]{0:T(1024)S(1)}, f32[2048]{0:T(1024)}, u32[]{:S(2)}) copy-start(f32[2048]{0:T(1024)} %param.5) | copy-start | bytes 24580
  30.3 3.7 %collective-permute-start.9 = (f32[16,128]{1,0:T(8,128)S(1)}, f32[16,128]{1,0:T(8,128)S(1)}, u32[]{:S(2)}, u32[]{:S(2)}) collective-permute-start(f32[16,128]{1,0:T(8,128)S(1)} %get-tuple-element.58), channel_id=1, source_target_pairs={{2,0},{3,1},{18,2},{19,3},{6,4},{7,5},{22,6},{23,7},{10,8},{11,9},... | collective-permute-start | bytes 24584 | tf_op jit(solution)/shard_map/ppermute | solution.py:250

commit v8 on v7

--- a/solution.py
+++ b/solution.py
@@ -15,11 +15,11 @@
 VMEM = 24 * 2**20
 F32 = jnp.float32
 BF16 = jnp.bfloat16
-HEAD = 10
+HEAD = 9
 
 
 def routes(slabs, count):
-    layer, ring, pair, beside = [], [], [], []
+    layer, ring, pair, beside, across = [], [], [], [], []
     for slab in range(slabs):
         for block in range(count):
             place = block % ROUNDS
@@ -33,7 +33,9 @@
             ring.append((here, device(block - place + (place + 1) % ROUNDS)))
             pair.append((here, device(block + 2) if place < 2 else other))
             beside.append((here, other))
-    return layer, ring, pair, beside
+            aim = count - 1 - block + (-2 if place < 2 else 2)
+            across.append((here, device(aim, slab ^ 1)))
+    return layer, ring, pair, beside, across
 
 
 def backwards(pairs):
@@ -109,7 +111,7 @@
     head = tokens * HEAD // 16
     part = head // LANES
     rest = lines - part
-    layer, ring, pair, beside = routes(slabs, count)
+    layer, ring, pair, beside, across = routes(slabs, count)
     block = lax.axis_index("corpus")
     block = jnp.where(lax.axis_index("slab") % 2 == 1, count - 1 - block, block)
     has_pair = (block % ROUNDS >= 2).astype(jnp.int32).reshape(1)
@@ -173,83 +175,76 @@
     )
     r = lax.ppermute(after(q, z_max), axes, beside)
 
-    def layer2(own, own_m, z2, z_m2, own_max, z_max, own_out, z_out):
+    def inner(has, own, own_m, z1, z2, z_m2, p2, p_m2, q, own_max, z_max, p_max, own_out, z_out, p_out, out,
+              q_m, z_m):
+        z_out[lines:] = jnp.full((7 * lines, LANES), NEG, F32)
         row, col = tile([(z2[...], z_m2[...])], [(own[:tokens], own_m[...])])
-        own_out[...] = jnp.maximum(own_max[...], col)
-        z_out[:part] = z_max[:part]
-        z_out[part:] = jnp.maximum(z_max[part:], row)
-
-    own_max, z_max = call("layer2", layer2, [own, own_m, z2, z_m2, own_max, z_max], [whole, whole])
-
-    def q_marks(q, after, out):
-        mark(q[tokens:], out, MARK)
-
-    (q_m,) = call("q_marks", q_marks, [q, own_max], [marks])
-
-    def pairs(has, z1, z2, q, q_m, r, z_max, z_out, out, other_m):
-        z_out[lines:] = jnp.full((3 * lines, LANES), NEG, F32)
+        p_out[:part] = p_max[:part]
+        p_out[lines:] = jnp.full((3 * lines, LANES), NEG, F32)
 
         @pl.when(has[0] > 0)
         def _():
-            mark(z1[head:], other_m, -MARK)
-            row, col = tile([(z1[:head], other_m[:head]), (z2[...], other_m[head:])], [(q[:tokens], q_m[...])])
-            z_out[:lines] = jnp.maximum(z_max[...], row)
+            mark(q[tokens:], q_m, MARK)
+            mark(z1[head:], z_m, -MARK)
+            z_row, q_col = tile([(z1[:head], z_m[:head]), (z2[...], z_m[head:])], [(q[:tokens], q_m[...])])
+            z_out[:part] = jnp.maximum(z_max[:part], z_row[:part])
+            z_out[part:lines] = jnp.maximum(jnp.maximum(z_max[part:], row), z_row[part:])
+            own_out[...] = jnp.maximum(own_max[...], col)
+            p_out[part:lines] = p_max[part:]
             out[:lines] = jnp.full((lines, LANES), NEG, F32)
-            out[lines:] = col
+            out[lines:] = q_col
 
         @pl.when(has[0] == 0)
         def _():
-            mark(r[tokens:], other_m, -MARK)
-            z_out[:lines] = z_max[...]
-            out[:lines], out[lines:] = tile([(q[:tokens], q_m[...])], [(r[:tokens], other_m[...])])
-
-    z_max, mine = call(
-        "pairs",
-        pairs,
-        [has_pair, z1, z2, q, q_m, r, z_max],
-        [struct(4 * lines, LANES), struct(2 * lines, LANES)],
-        specs=[smem] + [vmem] * 6,
-        scratch=[pltpu.VMEM((tokens, LANES), BF16)],
-    )
-    theirs = lax.ppermute(mine, axes, beside)
-
-    def ring2(wanted, far, own, own_m, p2, p_m2, own_max, p_max, own_out, p_out):
-        @pl.when(far[0] == wanted)
+            p_row, p_col = tile([(p2[...], p_m2[...])], [(own[:tokens], own_m[...])])
+            z_out[:part] = z_max[:part]
+            z_out[part:lines] = jnp.maximum(z_max[part:], row)
+            own_out[...] = jnp.maximum(jnp.maximum(own_max[...], col), p_col)
+            p_out[part:lines] = jnp.maximum(p_max[part:], p_row)
+            out[...] = jnp.full((2 * lines, LANES), NEG, F32)
+
+    own_max, z_max, p_max, mine = call(
+        "inner",
+        inner,
+        [has_pair, own, own_m, z1, z2, z_m2, p2, p_m2, q, own_max, z_max, p_max],
+        [whole, struct(8 * lines, LANES), struct(4 * lines, LANES), struct(2 * lines, LANES)],
+        specs=[smem] + [vmem] * 11,
+        scratch=[pltpu.VMEM((tokens, LANES), BF16)] * 2,
+    )
+
+    def outer(wanted, far, has, own, own_m, p2, p_m2, q, r, own_max, p_max, mine, own_out, p_out, out, q_m, r_m):
+        own_out[...] = own_max[...]
+        p_out[...] = p_max[...]
+        out[...] = mine[...]
+
+        @pl.when((far[0] == wanted) & (has[0] > 0))
         def _():
             row, col = tile([(p2[...], p_m2[...])], [(own[:tokens], own_m[...])])
             own_out[...] = jnp.maximum(own_max[...], col)
-            p_out[:part] = p_max[:part]
-            p_out[part:] = jnp.maximum(p_max[part:], row)
-
-        @pl.when(far[0] != wanted)
-        def _():
-            own_out[...] = own_max[...]
-            p_out[...] = p_max[...]
-
-    p_max = after(p_max, mine)
+            p_out[part:lines] = jnp.maximum(p_max[part:lines], row)
+
+        @pl.when((far[0] == wanted) & (has[0] == 0))
+        def _():
+            mark(q[tokens:], q_m, MARK)
+            mark(r[tokens:], r_m, -MARK)
+            out[:lines], out[lines:] = tile([(q[:tokens], q_m[...])], [(r[:tokens], r_m[...])])
+
     for wanted in (1, 0):
-        own_max, p_max = call(
-            "ring2",
-            functools.partial(ring2, wanted),
-            [far, own, own_m, p2, p_m2, own_max, p_max],
-            [whole, whole],
-            specs=[smem] + [vmem] * 6,
+        own_max, p_max, mine = call(
+            "outer",
+            functools.partial(outer, wanted),
+            [far, has_pair, own, own_m, p2, p_m2, q, r, own_max, p_max, mine],
+            [whole, struct(4 * lines, LANES), struct(2 * lines, LANES)],
+            specs=[smem] * 2 + [vmem] * 9,
+            scratch=[pltpu.VMEM((tokens, LANES), BF16)] * 2,
         )
         if wanted:
-            z_back = lax.ppermute(after(z_max, p_max), axes, backwards(layer))
+            z_back = lax.ppermute(after(z_max, own_max), axes, backwards(layer))
+    q_back = lax.ppermute(mine, axes, backwards(pair))
+    r_back = lax.ppermute(mine, axes, across)
     p_back = lax.ppermute(p_max, axes, backwards(ring))
-
-    def merge(has, mine, theirs, own_max, own_out, q_out):
-        got = jnp.where(has[0] > 0, theirs[...], F32(NEG))
-        own_out[...] = jnp.maximum(own_max[...], got[:lines])
-        q_out[...] = jnp.maximum(mine[lines:], got[lines:])
-
-    own_max, q_max = call(
-        "merge", merge, [has_pair, mine, theirs, own_max], [whole, whole], specs=[smem] + [vmem] * 3
-    )
-    q_back = lax.ppermute(q_max, axes, backwards(pair))
-    q_back = jnp.where(has_pair > 0, NEG, q_back)
-    best = jnp.maximum(jnp.maximum(own_max, z_back[:lines]), jnp.maximum(p_back, q_back))
+    pair_back = jnp.where(has_pair > 0, q_back[:lines], jnp.maximum(q_back[lines:], r_back[lines:]))
+    best = jnp.maximum(jnp.maximum(own_max, z_back[:lines]), jnp.maximum(p_back[:lines], pair_back))
     return jnp.maximum(prior, best.reshape(tokens))
 
 

time: 34.8 us -> 34.7 us (level)
  the two profiles are of different devices: /device:TPU:0 before, /device:TPU:9 now
where the time goes in v8:
time: 34.7 us; the launch traced here: 34.6 us
  starting transfers between devices  14.6 us (42%)
  Pallas kernels  11.6 us (33%)
  waiting for transfers between devices  6.62 us (19%)
  local copies, waits for them, and re-layouts  1.1 us (3%)
  other arithmetic  0.61 us (2%)
    pallas_call x8, Pallas kernels, call(): pl.pallas_call(kernel, out_shape=outs, in_specs=specs or [pl.BlockSpec(me...  11.6 us
    ppermute x1, starting transfers between devices, per_device(): r = lax.ppermute(after(q, z_max), axes, beside)  2.62 us
    ppermute x1, starting transfers between devices, per_device(): q_back = lax.ppermute(mine, axes, backwards(pair))  2.43 us
    ppermute x1, waiting for transfers between devices, per_device(): p1 = lax.ppermute(own1, axes, ring)  2.14 us
    ppermute x1, waiting for transfers between devices, per_device(): r_back = lax.ppermute(mine, axes, across)  2.1 us
    ppermute x1, starting transfers between devices, per_device(): z2 = lax.ppermute(own2, axes, layer)  1.94 us
    ppermute x1, starting transfers between devices, per_device(): p1 = lax.ppermute(own1, axes, ring)  1.72 us
    ppermute x1, waiting for transfers between devices, per_device(): z2 = lax.ppermute(own2, axes, layer)  1.45 us
  transfers between devices with their start and end apart: 10, of which 4 were waited for; matrix products, arithmetic and copies ran while one was open for 0% of the time, Pallas kernels for 33%

profile of v8, /device:TPU:9, one launch (start us, length us, event | category | flops | bytes accessed | tf_op | source)
XLA Modules:
  0.0 34.6 jit_solution(11281908059966285723)
XLA Ops:
  0.0 0.0 copy-start
  0.0 1.1 %pad.4.vec = bf16[2064,128]{1,0:T(8,128)(2,1)S(1)} pad(bf16[2048,128]{1,0:T(8,128)(2,1)} %param.3, bf16[]{:T(256)} %constant.42.clone.1), padding=0_16x0_0 | pad | bytes 1052674 | tf_op jit(solution)/shard_map/jit(_pad)/pad | solution.py:129
  1.1 0.0 copy-done
  1.1 0.1 pack.1
  1.2 0.7 %collective-permute-start.2 = (bf16[2064,128]{1,0:T(8,128)(2,1)S(1)}, bf16[2064,128]{1,0:T(8,128)(2,1)S(1)}, u32[]{:S(2)}, u32[]{:S(2)}) collective-permute-start(bf16[2064,128]{1,0:T(8,128)(2,1)S(1)} %get-tuple-element.31.own), channel_id=1, source_target_pairs={{0,2},{1,3},{2,18},{3,19},{4,6},{5,7},{6,22},{7,23},{8,10},{9,11},... | collective-permute-start | bytes 1585160 | tf_op jit(solution)/shard_map/ppermute | solution.py:134
  1.9 1.7 %collective-permute-start.1 = (bf16[1168,128]{1,0:T(8,128)(2,1)S(1)}, bf16[1168,128]{1,0:T(8,128)(2,1)S(1)}, u32[]{:S(2)}, u32[]{:S(2)}) collective-permute-start(bf16[1168,128]{1,0:T(8,128)(2,1)S(1)} %get-tuple-element.33), channel_id=1, source_target_pairs={{0,1},{1,2},{2,3},{3,0},{4,5},{5,6},{6,7},{7,4},{8,9},{9,10},{10,1... | collective-permute-start | bytes 897032 | tf_op jit(solution)/shard_map/ppermute | solution.py:132
  3.6 0.2 collective-permute-start.3
  3.8 1.4 %collective-permute-start = (bf16[896,128]{1,0:T(8,128)(2,1)S(1)}, bf16[896,128]{1,0:T(8,128)(2,1)S(1)}, u32[]{:S(2)}, u32[]{:S(2)}) collective-permute-start(bf16[896,128]{1,0:T(8,128)(2,1)S(1)} %get-tuple-element.32), channel_id=1, source_target_pairs={{0,1},{1,2},{2,3},{3,0},{4,5},{5,6},{6,7},{7,4},{8,9},{9,10},{10,1... | collective-permute-start | bytes 688136 | tf_op jit(solution)/shard_map/ppermute | solution.py:135
  5.1 1.9 %collective-permute-start.4 = (bf16[896,128]{1,0:T(8,128)(2,1)S(1)}, bf16[896,128]{1,0:T(8,128)(2,1)S(1)}, u32[]{:S(2)}, u32[]{:S(2)}) collective-permute-start(bf16[896,128]{1,0:T(8,128)(2,1)S(1)} %get-tuple-element.32), channel_id=1, source_target_pairs={{0,12},{1,5},{2,6},{3,7},{4,0},{5,9},{6,10},{7,11},{8,4},{9,13},{1... | collective-permute-start | bytes 688136 | tf_op jit(solution)/shard_map/ppermute | solution.py:136
  7.1 0.2 own_marks.1.own_m
  7.3 2.1 %collective-permute-done.1.p1 = bf16[1168,128]{1,0:T(8,128)(2,1)S(1)} collective-permute-done((bf16[1168,128]{1,0:T(8,128)(2,1)S(1)}, bf16[1168,128]{1,0:T(8,128)(2,1)S(1)}, u32[]{:S(2)}, u32[]{:S(2)}) %collective-permute-start.1) | collective-permute-done | bytes 299040 | tf_op jit(solution)/shard_map/ppermute | solution.py:132
  9.4 1.6 %ring1.1 = (bf16[1152,128]{1,0:T(8,128)(2,1)S(1)}, bf16[896,128]{1,0:T(8,128)(2,1)S(1)}, f32[16,128]{1,0:T(8,128)S(1)}, f32[9,128]{1,0:T(8,128)S(1)}) custom-call(bf16[2064,128]{1,0:T(8,128)(2,1)S(1)} %get-tuple-element.31.own, bf16[2048,128]{1,0:T(8,128)(2,1)S(1)} %own_marks.1.own_m, bf16[1168,128]{1,0:T(8,128)(2,1)S(1)} %collective-permute-done.1.p1), custom_call_target="tpu_custom_call" | custom-call | bytes 1888768 | tf_op jit(solution)/shard_map/ring1/pallas_call | solution.py:51
  11.0 0.0 collective-permute-done.3.z1
  11.0 2.4 %layer1.1 = (bf16[1152,128]{1,0:T(8,128)(2,1)S(1)}, bf16[896,128]{1,0:T(8,128)(2,1)S(1)}, f32[16,128]{1,0:T(8,128)S(1)}, f32[9,128]{1,0:T(8,128)S(1)}, f32[9,128]{1,0:T(8,128)S(1)}) custom-call(bf16[2064,128]{1,0:T(8,128)(2,1)S(1)} %get-tuple-element.31.own, bf16[2048,128]{1,0:T(8,128)(2,1)S(1)} %own_marks.1.own_m, ...), custom_call_target="tpu_custom_call" | custom-call | bytes 2500096 | tf_op jit(solution)/shard_map/layer1/pallas_call | solution.py:51
  13.4 0.9 %collective-permute-done.p2 = bf16[896,128]{1,0:T(8,128)(2,1)S(1)} collective-permute-done((bf16[896,128]{1,0:T(8,128)(2,1)S(1)}, bf16[896,128]{1,0:T(8,128)(2,1)S(1)}, u32[]{:S(2)}, u32[]{:S(2)}) %collective-permute-start) | collective-permute-done | bytes 229408 | tf_op jit(solution)/shard_map/ppermute | solution.py:135
  14.4 1.4 %collective-permute-done.4.z2 = bf16[896,128]{1,0:T(8,128)(2,1)S(1)} collective-permute-done((bf16[896,128]{1,0:T(8,128)(2,1)S(1)}, bf16[896,128]{1,0:T(8,128)(2,1)S(1)}, u32[]{:S(2)}, u32[]{:S(2)}) %collective-permute-start.4) | collective-permute-done | bytes 229408 | tf_op jit(solution)/shard_map/ppermute | solution.py:136
  15.8 1.9 %second.1 = (f32[16,128]{1,0:T(8,128)S(1)}, f32[16,128]{1,0:T(8,128)S(1)}) custom-call(bf16[1168,128]{1,0:T(8,128)(2,1)S(1)} %collective-permute-done.1.p1, bf16[1152,128]{1,0:T(8,128)(2,1)S(1)} %get-tuple-element.35.p_m1, bf16[896,128]{1,0:T(8,128)(2,1)S(1)} %collective-permute-done.p2, bf16[896,128]{1,0:T(8,128)(2,1)S(1)} %get-tuple-element.34.p_m2, ...), custom_call_target="tpu_custom_call" | custom-call | bytes 2130944 | tf_op jit(solution)/shard_map/second/pallas_call | solution.py:51
  17.7 0.0 collective-permute-done.2.q
  17.7 2.6 %collective-permute-start.5 = (bf16[2064,128]{1,0:T(8,128)(2,1)S(1)}, bf16[2064,128]{1,0:T(8,128)(2,1)S(1)}, u32[]{:S(2)}, u32[]{:S(2)}) collective-permute-start(bf16[2064,128]{1,0:T(8,128)(2,1)S(1)} %collective-permute-done.2.q), channel_id=1, source_target_pairs={{0,16},{1,17},{2,18},{3,19},{4,20},{5,21},{6,22},{7,23},{8,24},{9,... | collective-permute-start | bytes 1585160 | tf_op jit(solution)/shard_map/ppermute | solution.py:176
  20.3 4.0 %inner.1 = (f32[16,128]{1,0:T(8,128)S(1)}, f32[128,128]{1,0:T(8,128)S(1)}, f32[64,128]{1,0:T(8,128)S(1)}, f32[32,128]{1,0:T(8,128)S(1)}) custom-call(s32[1]{0:T(128)} %bitcast.1.has, bf16[2064,128]{1,0:T(8,128)(2,1)S(1)} %get-tuple-element.31.own, bf16[2048,128]{1,0:T(8,128)(2,1)S(1)} %own_marks.1.own_m, bf16[1168,128]{1,0:T(8,128)(2,1)S(1)} %collective-permute-done.3.z1, ...), custom_call_target="tpu_custom_call" | custom-call | bytes 2945028 | tf_op jit(solution)/shard_map/inner/pallas_call | solution.py:51
  24.3 0.0 collective-permute-done.5.r
  24.3 0.2 outer.2
  24.5 1.4 %collective-permute-start.6 = (f32[128,128]{1,0:T(8,128)S(1)}, f32[128,128]{1,0:T(8,128)S(1)}, u32[]{:S(2)}, u32[]{:S(2)}) collective-permute-start(f32[128,128]{1,0:T(8,128)S(1)} %get-tuple-element.54), channel_id=1, source_target_pairs={{12,0},{5,1},{6,2},{7,3},{0,4},{9,5},{10,6},{11,7},{4,8},{13,9},{1... | collective-permute-start | bytes 196616 | tf_op jit(solution)/shard_map/ppermute | solution.py:242
  25.9 1.3 %outer.3 = (f32[16,128]{1,0:T(8,128)S(1)}, f32[64,128]{1,0:T(8,128)S(1)}, f32[32,128]{1,0:T(8,128)S(1)}) custom-call(s32[1]{0:T(128)} %bitcast.far, s32[1]{0:T(128)} %bitcast.1.has, bf16[2064,128]{1,0:T(8,128)(2,1)S(1)} %get-tuple-element.31.own, bf16[2048,128]{1,0:T(8,128)(2,1)S(1)} %own_marks.1.own_m, bf16[896,128]{1,0:T(8,128)(2,1)S(1)} %collective-permute-done.p2, ...), custom_call_target="tpu_custom_call" | custom-call | bytes 2682888 | tf_op jit(solution)/shard_map/outer/pallas_call | solution.py:51
  27.1 0.0 copy-start.1
  27.1 1.2 %collective-permute-start.7 = (f32[64,128]{1,0:T(8,128)S(1)}, f32[64,128]{1,0:T(8,128)S(1)}, u32[]{:S(2)}, u32[]{:S(2)}) collective-permute-start(f32[64,128]{1,0:T(8,128)S(1)} %get-tuple-element.55), channel_id=1, source_target_pairs={{1,0},{2,1},{3,2},{0,3},{5,4},{6,5},{7,6},{4,7},{9,8},{10,9},{11,1... | collective-permute-start | bytes 98312 | tf_op jit(solution)/shard_map/ppermute | solution.py:245
  28.4 2.4 %collective-permute-start.8 = (f32[32,128]{1,0:T(8,128)S(1)}, f32[32,128]{1,0:T(8,128)S(1)}, u32[]{:S(2)}, u32[]{:S(2)}) collective-permute-start(f32[32,128]{1,0:T(8,128)S(1)} %get-tuple-element.56), channel_id=1, source_target_pairs={{2,0},{3,1},{18,2},{19,3},{6,4},{7,5},{22,6},{23,7},{10,8},{11,9},... | collective-permute-start | bytes 49160 | tf_op jit(solution)/shard_map/ppermute | solution.py:243
  30.8 1.1 %collective-permute-start.9 = (f32[32,128]{1,0:T(8,128)S(1)}, f32[32,128]{1,0:T(8,128)S(1)}, u32[]{:S(2)}, u32[]{:S(2)}) collective-permute-start(f32[32,128]{1,0:T(8,128)S(1)} %get-tuple-element.56), channel_id=1, source_target_pairs={{0,18},{1,19},{2,16},{3,17},{4,22},{5,23},{6,20},{7,21},{8,26},{9,... | collective-permute-start | bytes 49160 | tf_op jit(solution)/shard_map/ppermute | solution.py:244
  31.9 0.0 collective-permute-done.8
  31.9 2.1 %collective-permute-done.9 = f32[32,128]{1,0:T(8,128)S(1)} collective-permute-done((f32[32,128]{1,0:T(8,128)S(1)}, f32[32,128]{1,0:T(8,128)S(1)}, u32[]{:S(2)}, u32[]{:S(2)}) %collective-permute-start.9) | collective-permute-done | bytes 16416 | tf_op jit(solution)/shard_map/ppermute | solution.py:244
  34.0 0.0 collective-permute-done.7
  34.0 0.0 collective-permute-done.6
  34.0 0.0 copy-done.1
  34.0 0.6 %fusion.4 = f32[2048]{0:T(1024)} fusion(f32[2048]{0:T(1024)S(1)} %copy-done.1, f32[32,128]{1,0:T(8,128)S(1)} %collective-permute-done.9, f32[32,128]{1,0:T(8,128)S(1)} %collective-permute-done.8, f32[64,128]{1,0:T(8,128)S(1)} %collective-permute-done.7, f32[16,128]{1,0:T(8,128)S(1)} %get-tuple-element.52, f32[128,128]{1,0:T(8,128)S(1)} %collective-permute-done.6, ...), kind=kLoop, calls=%fused_computation.5 | loop fusion | flops 12288 | bytes 65537 | tf_op jit(solution)/shard_map/max | solution.py:248
Async XLA Ops:
  0.0 1.1 %copy-start = (s32[2048]{0:T(1024)S(1)}, s32[2048]{0:T(1024)}, u32[]{:S(2)}) copy-start(s32[2048]{0:T(1024)} %param.4) | copy-start | bytes 24580
  1.2 16.5 %collective-permute-start.2 = (bf16[2064,128]{1,0:T(8,128)(2,1)S(1)}, bf16[2064,128]{1,0:T(8,128)(2,1)S(1)}, u32[]{:S(2)}, u32[]{:S(2)}) collective-permute-start(bf16[2064,128]{1,0:T(8,128)(2,1)S(1)} %get-tuple-element.31.own), channel_id=1, source_target_pairs={{0,2},{1,3},{2,18},{3,19},{4,6},{5,7},{6,22},{7,23},{8,10},{9,11},... | collective-permute-start | bytes 1585160 | tf_op jit(solution)/shard_map/ppermute | solution.py:134
  1.9 7.6 %collective-permute-start.1 = (bf16[1168,128]{1,0:T(8,128)(2,1)S(1)}, bf16[1168,128]{1,0:T(8,128)(2,1)S(1)}, u32[]{:S(2)}, u32[]{:S(2)}) collective-permute-start(bf16[1168,128]{1,0:T(8,128)(2,1)S(1)} %get-tuple-element.33), channel_id=1, source_target_pairs={{0,1},{1,2},{2,3},{3,0},{4,5},{5,6},{6,7},{7,4},{8,9},{9,10},{10,1... | collective-permute-start | bytes 897032 | tf_op jit(solution)/shard_map/ppermute | solution.py:132
  3.6 7.4 %collective-permute-start.3 = (bf16[1168,128]{1,0:T(8,128)(2,1)S(1)}, bf16[1168,128]{1,0:T(8,128)(2,1)S(1)}, u32[]{:S(2)}, u32[]{:S(2)}) collective-permute-start(bf16[1168,128]{1,0:T(8,128)(2,1)S(1)} %get-tuple-element.33), channel_id=1, source_target_pairs={{0,12},{1,5},{2,6},{3,7},{4,0},{5,9},{6,10},{7,11},{8,4},{9,13},{1... | collective-permute-start | bytes 897032 | tf_op jit(solution)/shard_map/ppermute | solution.py:133
  3.8 10.6 %collective-permute-start = (bf16[896,128]{1,0:T(8,128)(2,1)S(1)}, bf16[896,128]{1,0:T(8,128)(2,1)S(1)}, u32[]{:S(2)}, u32[]{:S(2)}) collective-permute-start(bf16[896,128]{1,0:T(8,128)(2,1)S(1)} %get-tuple-element.32), channel_id=1, source_target_pairs={{0,1},{1,2},{2,3},{3,0},{4,5},{5,6},{6,7},{7,4},{8,9},{9,10},{10,1... | collective-permute-start | bytes 688136 | tf_op jit(solution)/shard_map/ppermute | solution.py:135
  5.1 10.7 %collective-permute-start.4 = (bf16[896,128]{1,0:T(8,128)(2,1)S(1)}, bf16[896,128]{1,0:T(8,128)(2,1)S(1)}, u32[]{:S(2)}, u32[]{:S(2)}) collective-permute-start(bf16[896,128]{1,0:T(8,128)(2,1)S(1)} %get-tuple-element.32), channel_id=1, source_target_pairs={{0,12},{1,5},{2,6},{3,7},{4,0},{5,9},{6,10},{7,11},{8,4},{9,13},{1... | collective-permute-start | bytes 688136 | tf_op jit(solution)/shard_map/ppermute | solution.py:136
  17.7 6.6 %collective-permute-start.5 = (bf16[2064,128]{1,0:T(8,128)(2,1)S(1)}, bf16[2064,128]{1,0:T(8,128)(2,1)S(1)}, u32[]{:S(2)}, u32[]{:S(2)}) collective-permute-start(bf16[2064,128]{1,0:T(8,128)(2,1)S(1)} %collective-permute-done.2.q), channel_id=1, source_target_pairs={{0,16},{1,17},{2,18},{3,19},{4,20},{5,21},{6,22},{7,23},{8,24},{9,... | collective-permute-start | bytes 1585160 | tf_op jit(solution)/shard_map/ppermute | solution.py:176
  24.5 9.5 %collective-permute-start.6 = (f32[128,128]{1,0:T(8,128)S(1)}, f32[128,128]{1,0:T(8,128)S(1)}, u32[]{:S(2)}, u32[]{:S(2)}) collective-permute-start(f32[128,128]{1,0:T(8,128)S(1)} %get-tuple-element.54), channel_id=1, source_target_pairs={{12,0},{5,1},{6,2},{7,3},{0,4},{9,5},{10,6},{11,7},{4,8},{13,9},{1... | collective-permute-start | bytes 196616 | tf_op jit(solution)/shard_map/ppermute | solution.py:242
  27.1 6.8 %copy-start.1 = (f32[2048]{0:T(1024)S(1)}, f32[2048]{0:T(1024)}, u32[]{:S(2)}) copy-start(f32[2048]{0:T(1024)} %param.5) | copy-start | bytes 24580
  27.1 6.8 %collective-permute-start.7 = (f32[64,128]{1,0:T(8,128)S(1)}, f32[64,128]{1,0:T(8,128)S(1)}, u32[]{:S(2)}, u32[]{:S(2)}) collective-permute-start(f32[64,128]{1,0:T(8,128)S(1)} %get-tuple-element.55), channel_id=1, source_target_pairs={{1,0},{2,1},{3,2},{0,3},{5,4},{6,5},{7,6},{4,7},{9,8},{10,9},{11,1... | collective-permute-start | bytes 98312 | tf_op jit(solution)/shard_map/ppermute | solution.py:245
  28.4 3.5 %collective-permute-start.8 = (f32[32,128]{1,0:T(8,128)S(1)}, f32[32,128]{1,0:T(8,128)S(1)}, u32[]{:S(2)}, u32[]{:S(2)}) collective-permute-start(f32[32,128]{1,0:T(8,128)S(1)} %get-tuple-element.56), channel_id=1, source_target_pairs={{2,0},{3,1},{18,2},{19,3},{6,4},{7,5},{22,6},{23,7},{10,8},{11,9},... | collective-permute-start | bytes 49160 | tf_op jit(solution)/shard_map/ppermute | solution.py:243
  30.8 3.2 %collective-permute-start.9 = (f32[32,128]{1,0:T(8,128)S(1)}, f32[32,128]{1,0:T(8,128)S(1)}, u32[]{:S(2)}, u32[]{:S(2)}) collective-permute-start(f32[32,128]{1,0:T(8,128)S(1)} %get-tuple-element.56), channel_id=1, source_target_pairs={{0,18},{1,19},{2,16},{3,17},{4,22},{5,23},{6,20},{7,21},{8,26},{9,... | collective-permute-start | bytes 49160 | tf_op jit(solution)/shard_map/ppermute | solution.py:244
